TPU v7x, 32 devices: a whole 2x2x4 slice. The times are simulated.
32 devices in a mesh: gz: 8 (over y, x, core), gy: 4 (over z).
Axes of the slice: x: 2, y: 2, z: 4, core: 2. Of those that a mesh axis runs over, the one named last changes fastest.
Arguments:
- orbitals: bfloat16 [256, 256, 512], P(('gz', 'gy')), may hold values from -2 to 2
- points: int32 [1024], replicated, may hold values from 0 to 131071, as said below
- coulomb: float32 [256, 512], P(None, 'gy'), may hold values from 10 to 1000
Outputs:
- potentials: bfloat16 [256, 512, 1024], P('gz', 'gy')
Inputs may be any that keep to these rules, and one draw needn't show every extreme that they name: `points`: 1024 distinct grid cells.
All inputs are finite; a program needn't handle non-finite values.
Results may differ from a plain program's by a relative error of at most 0.0025.
Values may be sent and summed in bfloat16 or wider, within the bound.
No kernel may reach another device: no remote copies, remote signals or barrier semaphores. Data moves between devices by JAX's collectives and lax.ppermute only.
A program may use at most 192 MiB of HBM per device.

v0:
```python
import functools
import math

import jax
import jax.numpy as jnp
import numpy as np
from jax import lax
from jax.experimental import pallas as pl
from jax.experimental.pallas import tpu as pltpu
from jax.sharding import PartitionSpec as P

F32 = jnp.float32
BF16 = jnp.bfloat16
HIGH = lax.Precision.HIGHEST
MIB = 1024 * 1024


def split(value):
    high = value.astype(BF16)
    return high, (value - high.astype(F32)).astype(BF16)


def points_kernel(where_ref, field_ref, out_ref):
    bands = field_ref.shape[1]
    lane = lax.broadcasted_iota(jnp.int32, (bands, 128), 1)

    def tile(t, _):
        base = pl.multiple_of(t * 128, 128)

        def some(s, accs):
            accs = list(accs)
            for u in range(16):
                m = s * 16 + u
                column = where_ref[0, base + m]
                at = pl.multiple_of(where_ref[1, base + m], 128)
                row = field_ref[column, :, pl.ds(at, 128)]
                row = pltpu.roll(row, where_ref[2, base + m], 1)
                accs[u % 4] = jnp.where(lane == m, row, accs[u % 4])
            return tuple(accs)

        accs = lax.fori_loop(0, 8, some, (jnp.zeros((bands, 128), F32),) * 4)
        out_ref[:, pl.ds(base, 128)] = (accs[0] + accs[1]) + (accs[2] + accs[3])
        return 0

    lax.fori_loop(0, out_ref.shape[1] // 128, tile, 0)


def take_points(points, field, columns):
    plane = points // columns
    at = plane // 128 * 128
    shift = (jnp.arange(points.shape[0], dtype=jnp.int32) - plane) % 128
    where = jnp.stack([points - plane * columns, at, shift])
    return pl.pallas_call(
        points_kernel,
        out_shape=jax.ShapeDtypeStruct((field.shape[1], points.shape[0]), F32),
        in_specs=[
            pl.BlockSpec(memory_space=pltpu.SMEM),
            pl.BlockSpec(memory_space=pltpu.VMEM),
        ],
        out_specs=pl.BlockSpec(memory_space=pltpu.VMEM),
        compiler_params=pltpu.CompilerParams(vmem_limit_bytes=32 * MIB),
        name="take_points",
    )(where, field)


def sweep_small(a):
    n = a.shape[0]
    lane = lax.broadcasted_iota(jnp.int32, (8, n), 1)
    wide = lax.broadcasted_iota(jnp.int32, (n, n), 1)
    sub = lax.broadcasted_iota(jnp.int32, (8, n), 0)
    for g in range(n // 8):
        lo = 8 * g
        rows = a[lo : lo + 8, :]
        cols = [jnp.broadcast_to(a[:, lo + j : lo + j + 1], (n, n)) for j in range(8)]
        t = [c[lo : lo + 8, :] for c in cols]
        for k in range(8):
            pivot = jnp.broadcast_to(t[k][k : k + 1, :], (8, n))
            scale = pl.reciprocal(pivot, approx=True)
            scale = scale * (2.0 - pivot * scale)
            scale = scale * (2.0 - pivot * scale)
            here = sub == k
            new = []
            for j in range(8):
                if j == k:
                    new.append(jnp.where(here, -1.0, t[k]) * scale)
                else:
                    factor = jnp.broadcast_to(t[j][k : k + 1, :], (8, n))
                    kept = jnp.where(here, 0.0, t[j])
                    new.append(kept - (jnp.where(here, -1.0, t[k]) * factor) * scale)
            t = new
        terms = [t[j] * jnp.broadcast_to(rows[j : j + 1, :], (8, n)) for j in range(8)]
        while len(terms) > 1:
            terms = [x + y for x, y in zip(terms[::2], terms[1::2])]
        q = -terms[0]
        for j in range(8):
            q = jnp.where(lane == lo + j, t[j], q)
        inside = (wide >= lo) & (wide < lo + 8)
        terms = [cols[j] * jnp.broadcast_to(q[j : j + 1, :], (n, n)) for j in range(8)]
        while len(terms) > 1:
            terms = [x + y for x, y in zip(terms[::2], terms[1::2])]
        upd = jnp.where(inside, 0.0, a) - terms[0]
        a = jnp.concatenate(
            ([upd[:lo]] if lo else []) + [q] + ([upd[lo + 8 :]] if lo + 8 < n else []), axis=0
        )
    return a


def mm(a, b):
    return jnp.dot(a, b, precision=HIGH, preferred_element_type=F32)


def sweep_step(gram, block, panel, k, *, big, small):
    n = gram.shape[0]
    inner = lax.broadcasted_iota(jnp.int32, (small, big), 1)
    inner_full = lax.broadcasted_iota(jnp.int32, (big, big), 1)
    at = k * big
    kr = slice(at, at + big)
    block[...] = gram[kr, kr]
    for s in range(big // small):
        lo = s * small
        sr = slice(lo, lo + small)
        negative = sweep_small(block[sr, sr])
        q = -mm(negative, block[sr, :])
        inside = (inner >= lo) & (inner < lo + small)
        q = jnp.where(inside, jnp.concatenate([negative] * (big // small), axis=1), q)
        inside_full = (inner_full >= lo) & (inner_full < lo + small)
        upd = jnp.where(inside_full, 0.0, block[...]) - mm(block[:, sr], q)
        block[...] = upd
        block[sr, :] = q
    panel[...] = -mm(block[...], gram[kr, :])
    panel[:, kr] = block[...]
    wide = lax.broadcasted_iota(jnp.int32, (big, n), 1)
    inside = (wide >= at) & (wide < at + big)

    @pl.loop(0, n // big)
    def _(t):
        r = pl.ds(pl.multiple_of(t * big, big), big)
        col = gram[r, kr]
        gram[r, :] = jnp.where(inside, 0.0, gram[r, :]) - mm(col, panel[...])

    gram[kr, :] = panel[...]


def first_kernel(values_ref, gram, block, panel, *, big, small):
    @pl.loop(0, gram.shape[0] // big)
    def _(t):
        r = pl.ds(pl.multiple_of(t * big, big), big)
        base = lax.dot_general(
            values_ref[:, r], values_ref[...], (((0,), (0,)), ((), ())), preferred_element_type=F32
        )
        gram[r, :] = base * base

    sweep_step(gram, block, panel, 0, big=big, small=small)


def middle_kernel(*refs, step, big, small):
    gram, block, panel = refs[-3:]
    sweep_step(gram, block, panel, step, big=big, small=small)


def last_kernel(gram_ref, *refs, step, big, small):
    out_ref, gram, block, panel = refs[-4:]
    n = gram.shape[0]
    gram[...] = gram_ref[...]
    sweep_step(gram, block, panel, step, big=big, small=small)

    @pl.loop(0, n // big)
    def _(t):
        at = pl.multiple_of(t * big, big)
        high, low = split(-gram[pl.ds(at, big), :])
        out_ref[pl.ds(at, big), :] = high
        out_ref[pl.ds(at + n, big), :] = low


def sweep_gram(values, gram, step, after):
    big, small = 256, 128
    n = values.shape[1]
    last = step == n // big - 1
    vmem = pl.BlockSpec(memory_space=pltpu.VMEM)
    anywhere = pl.BlockSpec(memory_space=pl.ANY)
    state = jax.ShapeDtypeStruct((n, n), F32)
    scratch = [pltpu.VMEM((big, big), F32), pltpu.VMEM((big, n), F32)]
    options = dict(big=big, small=small)
    params = pltpu.CompilerParams(vmem_limit_bytes=24 * MIB)
    cost = pl.CostEstimate(flops=n * n, bytes_accessed=n * n, transcendentals=0)
    if step == 0:
        return pl.pallas_call(
            functools.partial(first_kernel, **options),
            out_shape=state,
            in_specs=[vmem],
            out_specs=vmem,
            scratch_shapes=scratch,
            compiler_params=params,
            cost_estimate=cost,
            name="sweep_first",
        )(values)
    specs = [vmem] + [anywhere] * len(after)
    if not last:
        return pl.pallas_call(
            functools.partial(middle_kernel, step=step, **options),
            out_shape=state,
            in_specs=specs,
            out_specs=vmem,
            scratch_shapes=scratch,
            input_output_aliases={0: 0},
            compiler_params=params,
            cost_estimate=cost,
            name="sweep_middle",
        )(gram, *after)
    return pl.pallas_call(
        functools.partial(last_kernel, step=step, **options),
        out_shape=jax.ShapeDtypeStruct((2 * n, n), BF16),
        in_specs=specs,
        out_specs=vmem,
        scratch_shapes=[pltpu.VMEM((n, n), F32)] + scratch,
        compiler_params=params,
        cost_estimate=cost,
        name="sweep_last",
    )(gram, *after)


def column_kernel(*refs, pieces):
    fields = refs[:pieces]
    values_ref, lags_ref, out_ref = refs[pieces], refs[pieces + 1], refs[-1]
    step, planes_out, _ = out_ref.shape
    n = values_ref.shape[1]
    planes = lags_ref.shape[1]
    first = pl.program_id(0) * step
    turned = [jnp.concatenate([f[i] for f in fields], axis=0).T for i in range(step)]
    sums = jnp.dot(
        jnp.concatenate(turned, axis=0), values_ref[...], preferred_element_type=F32
    )
    for i in range(step):
        mine = sums[i * planes : (i + 1) * planes]
        high, low = split(mine * mine)
        row = jnp.broadcast_to(lags_ref[pl.ds(first + i, 1), :], (planes_out, planes))
        circ_high, circ_low = split(pltpu.roll(row, 0, 1, stride=1, stride_axis=0))
        circ = jnp.concatenate([circ_high, circ_low], axis=0)
        both = jnp.dot(
            jnp.concatenate([circ, circ], axis=1),
            jnp.concatenate([high, low], axis=0),
            preferred_element_type=F32,
        )
        w_high, w_low = split(both[:planes_out] + both[planes_out:])
        out_ref[i, :, :n] = w_high
        out_ref[i, :, n:] = w_low


def convolve(pieces, values, lags, planes_out, start, state, after):
    cols, _, planes = pieces[0].shape
    all_cols = lags.shape[0]
    bands, n = values.shape
    step = 4
    extra = ([] if state is None else [state]) + list(after)
    return pl.pallas_call(
        functools.partial(column_kernel, pieces=len(pieces)),
        grid=(cols // step,),
        out_shape=jax.ShapeDtypeStruct((all_cols, planes_out, 2 * n), BF16),
        in_specs=[pl.BlockSpec((step, p.shape[1], planes), lambda j: (j, 0, 0)) for p in pieces]
        + [
            pl.BlockSpec((bands, n), lambda j: (0, 0)),
            pl.BlockSpec((cols, planes), lambda j: (start // cols, 0)),
        ]
        + [pl.BlockSpec(memory_space=pl.ANY)] * len(extra),
        out_specs=pl.BlockSpec((step, planes_out, 2 * n), lambda j: (j + start // step, 0, 0)),
        input_output_aliases={} if state is None else {len(pieces) + 2: 0},
        compiler_params=pltpu.CompilerParams(vmem_limit_bytes=40 * MIB),
        cost_estimate=pl.CostEstimate(
            flops=2 * cols * n * planes * (bands + 4 * planes_out),
            bytes_accessed=2 * cols * (bands * planes + 2 * planes_out * n),
            transcendentals=0,
        ),
        name="convolve",
    )(*pieces, values, lags, *extra)


def fit_kernel(at_ref, w_ref, inverse_ref, out_ref, turn):
    slab, cols, n = out_ref.shape
    w = w_ref[...].reshape(cols * slab, 2 * n)
    out = jnp.dot(w[:, :n], inverse_ref[:n], preferred_element_type=F32)
    out = out + jnp.dot(w[:, :n], inverse_ref[n:], preferred_element_type=F32)
    out = out + jnp.dot(w[:, n:], inverse_ref[:n], preferred_element_type=F32)
    for t in range(n // 128):
        lanes = slice(t * 128, (t + 1) * 128)
        for c in range(cols):
            turn[t, pl.ds(c, slab, stride=cols), :] = out[c * slab : (c + 1) * slab, lanes]
        out_ref[:, :, lanes] = turn[t].reshape(slab, cols, 128).astype(out_ref.dtype)


def fit(at, w, inverse, width):
    cols, planes_out, n2 = w.shape
    n = n2 // 2
    slab = planes_out // 2
    step = 16
    return pl.pallas_call(
        fit_kernel,
        grid_spec=pltpu.PrefetchScalarGridSpec(
            num_scalar_prefetch=1,
            grid=(cols // step,),
            in_specs=[
                pl.BlockSpec((step, slab, n2), lambda j, at: (j, at[0], 0)),
                pl.BlockSpec((2 * n, n), lambda j, at: (0, 0)),
            ],
            out_specs=pl.BlockSpec((slab, step, n), lambda j, at: (0, j + at[1], 0)),
            scratch_shapes=[pltpu.VMEM((n // 128, slab * step, 128), F32)],
        ),
        out_shape=jax.ShapeDtypeStruct((slab, width, n), BF16),
        compiler_params=pltpu.CompilerParams(vmem_limit_bytes=48 * MIB),
        cost_estimate=pl.CostEstimate(
            flops=6 * cols * slab * n * n,
            bytes_accessed=6 * cols * slab * n + 4 * n * n,
            transcendentals=0,
        ),
        name="fit",
    )(at, w, inverse)


def zero_after(array):
    return jnp.isnan(array[(0,) * array.ndim]).astype(jnp.int32)


def per_device(orbitals, points, coulomb):
    gz_count = lax.axis_size("gz")
    gy_count = lax.axis_size("gy")
    gz = lax.axis_index("gz")
    gy = lax.axis_index("gy")
    bands_local, planes, columns = orbitals.shape
    n = points.shape[0]
    col_block = columns // gy_count
    half = col_block // 2
    slab = planes // gz_count
    pairs = gz_count // 2
    me = gz % 2
    pair = gz // 2
    total_bands = bands_local * gz_count * gy_count
    chunks = 2
    chunk = half // chunks

    def hop(array, bit):
        return lax.ppermute(array, "gz", [(z, z ^ bit) for z in range(gz_count)])

    def wait_for(array, other):
        return jnp.where(zero_after(other) == 0, array, jnp.zeros_like(array))

    def relay(both, other):
        first, second = both
        first = wait_for(first[:, rows // 2 :], other)
        second = wait_for(second[:, : rows // 2], other)
        return hop(second, 2), hop(first, 4)

    def gy_shift(array, by):
        return lax.ppermute(array, "gy", [(y, (y + by) % gy_count) for y in range(gy_count)])

    turned = jnp.transpose(orbitals, (2, 0, 1))
    blocks = turned.reshape(gy_count, 2, half, bands_local, planes)
    own = lax.dynamic_index_in_dim(blocks, me, 1, keepdims=False)
    partner = hop(lax.dynamic_index_in_dim(blocks, 1 - me, 1, keepdims=False), 1)

    values = take_points(points, turned.astype(F32), columns).astype(BF16)
    values = jnp.concatenate([values, hop(values, 1)], axis=0)
    values = jnp.concatenate(
        [values] + [gy_shift(values, dg) for dg in range(1, gy_count)], axis=0
    )
    column_values = values
    values = jnp.concatenate(
        [values] + [hop(values, 2 * p) for p in range(1, pairs)], axis=0
    )
    zero = zero_after(column_values[-1:])

    merged = jnp.concatenate([own, partner], axis=2)
    arriving = []
    for c in range(chunks):
        arriving.append([])
        for dg in range(gy_count):
            part = lax.dynamic_slice(
                merged,
                ((gy + dg + zero) % gy_count, c * chunk, 0, 0),
                (1, chunk, 2 * bands_local, planes),
            )[0]
            arriving[c].append(gy_shift(part, dg) if dg else part)

    steps = n // 256
    gram = sweep_gram(values, None, 0, ())

    fields = [None] * chunks
    rows = total_bands // pairs
    pending = None
    for step in range(1, steps):
        after = ()
        if step <= chunks:
            c = step - 1
            mine = wait_for(jnp.concatenate(arriving[c], axis=1), gram)
            after = (mine,)
            if pairs == 4:
                if pending is not None:
                    after = after + pending
                    fields[c - 1] = fields[c - 1] + relay(pending, gram)
                pending = (hop(mine, 2), hop(mine, 4))
                fields[c] = (mine,) + pending
            else:
                fields[c] = (mine,) + tuple(hop(mine, 2 * p) for p in range(1, pairs))
        elif pending is not None:
            after = pending
            fields[chunks - 1] = fields[chunks - 1] + relay(pending, gram)
            pending = None
        gram = sweep_gram(values, gram, step, after)
    inverse = gram

    grid = np.arange(planes, dtype=np.int64)
    table = np.cos((2.0 * np.pi / planes) * ((grid[:, None] * grid[None, :]) % planes))
    kernel = lax.dynamic_slice_in_dim(coulomb, me * half, half, 1).T
    lags = jnp.dot(
        kernel, jnp.asarray(table / planes, F32), precision=HIGH, preferred_element_type=F32
    )
    lags = jnp.roll(lags, pair * (2 * slab), axis=1)

    weights = None
    for c in range(chunks):
        weights = convolve(fields[c], values, lags, 2 * slab, c * chunk, weights, ())
    there = fit(jnp.stack([1 - me, jnp.zeros((), jnp.int32)]), weights, inverse, half)
    there = hop(there, 1)
    result = fit(jnp.stack([me, me * half // 16]), weights, inverse, col_block)
    return lax.dynamic_update_slice(result, there, (0, (1 - me) * half, 0))


def solution(mesh):
    return jax.shard_map(
        per_device,
        mesh=mesh,
        in_specs=(P(("gz", "gy"), None, None), P(), P(None, "gy")),
        out_specs=P("gz", "gy", None),
        check_vma=False,
    )
```

profile of v0, /device:TPU:1, one launch (start us, length us, event | category | flops | bytes accessed | tf_op | source)
XLA Modules:
  0.0 220.5 jit_solution(16798709295232656159)
XLA Ops:
  0.0 3.4 %copy.8 = bf16[8,256,512]{1,0,2:T(8,128)(2,1)S(1)} copy(bf16[8,256,512]{2,1,0:T(8,128)(2,1)} %param.4) | data formatting | bytes 4194304 | tf_op args[0]
  3.4 1.1 dynamic-slice_bitcast_fusion.1
  4.6 0.3 bitcast_convert_fusion.field_ref
  4.9 0.3 copy-done.9
  5.2 10.1 %take_points.1 = f32[8,1024]{1,0:T(8,128)S(1)} custom-call(s32[3,1024]{1,0:T(4,128)S(1)} %pad_add_fusion.where_ref, f32[512,8,256]{2,1,0:T(8,128)S(1)} %bitcast_convert_fusion.field_ref), custom_call_target="tpu_custom_call" | custom-call | tf_op jit(solution)/shard_map/take_points/pallas_call | solution.py:53
  15.5 1.0 collective-permute-done
  16.6 4.5 %collective-permute-start.3 = (bf16[16,1024]{1,0:T(8,128)(2,1)S(1)}, bf16[16,1024]{1,0:T(8,128)(2,1)S(1)}, u32[]{:S(2)}, u32[]{:S(2)}) collective-permute-start(bf16[16,1024]{1,0:T(8,128)(2,1)S(1)} %pad_maximum_fusion), channel_id=1, source_target_pairs={{0,3},{1,0},{2,1},{3,2},{4,7},{5,4},{6,5},{7,6},{8,11},{9,8},{10,9... | collective-permute-start | bytes 98312 | tf_op jit(solution)/shard_map/ppermute | solution.py:352
  21.0 0.5 collective-permute-start.2
  21.5 4.1 %collective-permute-done.1 = bf16[16,1024]{1,0:T(8,128)(2,1)S(1)} collective-permute-done((bf16[16,1024]{1,0:T(8,128)(2,1)S(1)}, bf16[16,1024]{1,0:T(8,128)(2,1)S(1)}, u32[]{:S(2)}, u32[]{:S(2)}) %collective-permute-start.1) | collective-permute-done | bytes 32800 | tf_op jit(solution)/shard_map/ppermute | solution.py:352
  25.6 0.6 slice.38
  27.7 1.3 collective-permute-start.4
  29.0 1.2 collective-permute-start.5
  30.4 1.4 fusion.14
  31.8 0.4 collective-permute-start.10
  32.2 1.7 collective-permute-start.8
  33.9 2.4 %collective-permute-done.6 = bf16[64,1024]{1,0:T(8,128)(2,1)S(1)} collective-permute-done((bf16[64,1024]{1,0:T(8,128)(2,1)S(1)}, bf16[64,1024]{1,0:T(8,128)(2,1)S(1)}, u32[]{:S(2)}, u32[]{:S(2)}) %collective-permute-start.6) | collective-permute-done | bytes 131104 | tf_op jit(solution)/shard_map/ppermute | solution.py:340
  36.3 19.4 %sweep_first.1.refs_0_ = f32[1024,1024]{1,0:T(8,128)S(1)} custom-call(bf16[256,1024]{1,0:T(8,128)(2,1)S(1)} %constant_dynamic-update-slice_fusion.5.values_ref.refs_5_), custom_call_target="tpu_custom_call" | custom-call | flops 1048576 | bytes 1048576 | tf_op jit(solution)/shard_map/sweep_first/pallas_call | solution.py:187
  55.7 0.5 slice.37
  57.6 1.2 maximum_select_fusion.refs_1_.refs_0_
  59.0 0.8 collective-permute-start.13
  59.8 0.8 collective-permute-start.12
  60.6 1.6 collective-permute-start.11
  62.2 1.2 collective-permute-start.16
  63.4 0.9 fusion.10
  64.3 18.3 %sweep_middle.2.refs_0_ = f32[1024,1024]{1,0:T(8,128)S(1)} custom-call(f32[1024,1024]{1,0:T(8,128)S(1)} %sweep_first.1.refs_0_, bf16[32,64,256]{2,1,0:T(8,128)(2,1)} %maximum_select_fusion.refs_1_.refs_0_), custom_call_target="tpu_custom_call", output_to_operand_aliasing={{}: (0, {})} | custom-call | flops 1048576 | bytes 1048576 | tf_op jit(solution)/shard_map/sweep_middle/pallas_call | solution.py:199
  82.6 0.6 slice.39
  83.2 2.0 copy-done.2
  86.7 0.3 collective-permute-start.15
  87.0 0.3 collective-permute-start.14
  87.3 1.1 fusion.16
  88.3 0.9 fusion.18.refs_6_
  89.3 1.1 slice_select_fusion.1
  90.4 1.4 collective-permute-start.20
  91.7 1.1 slice_select_fusion
  92.8 1.2 collective-permute-start.21
  94.1 2.2 copy-done.3
  96.3 18.4 %sweep_middle.3.gram_ref = f32[1024,1024]{1,0:T(8,128)S(1)} custom-call(f32[1024,1024]{1,0:T(8,128)S(1)} %copy-done.3, bf16[32,64,256]{2,1,0:T(8,128)(2,1)S(1)} %maximum_select_fusion.1.refs_1_.refs_0_, bf16[32,64,256]{2,1,0:T(8,128)(2,1)} %collective-permute-done.16.refs_2_.refs_1_, ...), custom_call_target="tpu_custom_call", output_to_operand_aliasing={{}: (0, {})} | custom-call | flops 1048576 | bytes 1048576 | tf_op jit(solution)/shard_map/sweep_middle/pallas_call | solution.py:199
  114.7 0.5 slice.40
  116.6 0.4 collective-permute-start.18
  117.3 19.0 %sweep_last.1.inverse_ref = bf16[2048,1024]{1,0:T(8,128)(2,1)S(1)} custom-call(f32[1024,1024]{1,0:T(8,128)S(1)} %sweep_middle.3.gram_ref, bf16[32,64,256]{2,1,0:T(8,128)(2,1)S(1)} %collective-permute-done.14.refs_1_.refs_0_, bf16[32,64,256]{2,1,0:T(8,128)(2,1)S(1)} %collective-permute-done.15.refs_2_.refs_1_), custom_call_target="tpu_custom_call" | custom-call | flops 1048576 | bytes 1048576 | tf_op jit(solution)/shard_map/sweep_last/pallas_call | solution.py:210
  136.3 2.0 copy-done.4
  138.4 13.5 %convolve.2.refs_7_ = bf16[64,64,2048]{2,1,0:T(8,128)(2,1)} custom-call(bf16[32,64,256]{2,1,0:T(8,128)(2,1)} %maximum_select_fusion.refs_1_.refs_0_, bf16[32,64,256]{2,1,0:T(8,128)(2,1)} %collective-permute-done.16.refs_2_.refs_1_, bf16[32,64,256]{2,1,0:T(8,128)(2,1)} %collective-permute-done.17.refs_3_.refs_2_, ...), custom_call_target="tpu_custom_call" | custom-call | flops 8589934592 | bytes 12582912 | tf_op jit(solution)/shard_map/convolve/pallas_call | solution.py:255
  151.8 12.2 %convolve.3.w_ref = bf16[64,64,2048]{2,1,0:T(8,128)(2,1)} custom-call(bf16[32,64,256]{2,1,0:T(8,128)(2,1)S(1)} %maximum_select_fusion.1.refs_1_.refs_0_, bf16[32,64,256]{2,1,0:T(8,128)(2,1)S(1)} %collective-permute-done.14.refs_1_.refs_0_, bf16[32,64,256]{2,1,0:T(8,128)(2,1)S(1)} %collective-permute-done.15.refs_2_.refs_1_, ...), custom_call_target="tpu_custom_call", output_to_operand_aliasing={{}: (7, {})} | custom-call | flops 8589934592 | bytes 12582912 | tf_op jit(solution)/shard_map/convolve/pallas_call | solution.py:255
  164.1 22.2 %fit.3 = bf16[32,64,1024]{2,1,0:T(8,128)(2,1)} custom-call(s32[2]{0:T(128)S(1)} %pad_add_fusion.2.at_ref, bf16[64,64,2048]{2,1,0:T(8,128)(2,1)} %convolve.3.w_ref, bf16[2048,1024]{1,0:T(8,128)(2,1)} %copy-done.4), custom_call_target="tpu_custom_call" | custom-call | flops 12884901888 | bytes 16777216 | tf_op jit(solution)/shard_map/fit/pallas_call | solution.py:295
  186.3 5.9 %collective-permute-start.22 = (bf16[32,64,1024]{2,1,0:T(8,128)(2,1)}, bf16[32,64,1024]{2,1,0:T(8,128)(2,1)}, u32[]{:S(2)}, u32[]{:S(2)}) collective-permute-start(bf16[32,64,1024]{2,1,0:T(8,128)(2,1)} %fit.3), channel_id=1, source_target_pairs={{0,4},{4,0},{8,12},{12,8},{16,20},{20,16},{24,28},{28,24},{1,5},{5... | collective-permute-start | bytes 12582920 | tf_op jit(solution)/shard_map/ppermute | solution.py:340
  192.3 2.2 copy-done.5
  194.5 20.9 %fit.2 = bf16[32,128,1024]{2,1,0:T(8,128)(2,1)} custom-call(s32[2]{0:T(128)S(1)} %pad_add_fusion.1.at_ref, bf16[64,64,2048]{2,1,0:T(8,128)(2,1)} %convolve.3.w_ref, bf16[2048,1024]{1,0:T(8,128)(2,1)S(1)} %copy-done.5), custom_call_target="tpu_custom_call" | custom-call | flops 12884901888 | bytes 16777216 | tf_op jit(solution)/shard_map/fit/pallas_call | solution.py:295
  215.3 5.0 %constant_dynamic-update-slice_fusion.13 = bf16[32,128,1024]{2,1,0:T(8,128)(2,1)} fusion(bf16[32,128,1024]{2,1,0:T(8,128)(2,1)} %fit.2, bf16[32,64,1024]{2,1,0:T(8,128)(2,1)} %collective-permute-done.22, s32[]{:T(128)S(6)} %select_n.158), kind=kLoop, calls=%fused_computation.72 | loop fusion | bytes 8388612 | tf_op jit(solution)/shard_map/dynamic_update_slice | solution.py:423
  (59 shorter events, 1.6 us)
Async XLA Ops:
  0.0 87.3 %copy-start = (f32[256,128]{1,0:T(8,128)S(1)}, f32[256,128]{1,0:T(8,128)}, u32[]{:S(2)}) copy-start(f32[256,128]{1,0:T(8,128)} %param.6) | copy-start | bytes 393220
  4.5 0.7 copy-start.9
  4.5 25.9 %collective-permute-start.7 = (bf16[4,64,8,256]{3,2,1,0:T(8,128)(2,1)}, bf16[4,64,8,256]{3,2,1,0:T(8,128)(2,1)}, u32[]{:S(2)}, u32[]{:S(2)}) collective-permute-start(bf16[4,64,8,256]{3,2,1,0:T(8,128)(2,1)} %get-tuple-element.15), channel_id=1, source_target_pairs={{0,4},{4,0},{8,12},{12,8},{16,20},{20,16},{24,28},{28,24},{1,5},{5... | collective-permute-start | bytes 3145736 | tf_op jit(solution)/shard_map/ppermute | solution.py:340
  15.3 1.2 collective-permute-start
  16.6 9.1 %collective-permute-start.3 = (bf16[16,1024]{1,0:T(8,128)(2,1)S(1)}, bf16[16,1024]{1,0:T(8,128)(2,1)S(1)}, u32[]{:S(2)}, u32[]{:S(2)}) collective-permute-start(bf16[16,1024]{1,0:T(8,128)(2,1)S(1)} %pad_maximum_fusion), channel_id=1, source_target_pairs={{0,3},{1,0},{2,1},{3,2},{4,7},{5,4},{6,5},{7,6},{8,11},{9,8},{10,9... | collective-permute-start | bytes 98312 | tf_op jit(solution)/shard_map/ppermute | solution.py:352
  21.0 4.6 %collective-permute-start.1 = (bf16[16,1024]{1,0:T(8,128)(2,1)S(1)}, bf16[16,1024]{1,0:T(8,128)(2,1)S(1)}, u32[]{:S(2)}, u32[]{:S(2)}) collective-permute-start(bf16[16,1024]{1,0:T(8,128)(2,1)S(1)} %pad_maximum_fusion), channel_id=1, source_target_pairs={{0,1},{1,2},{2,3},{3,0},{4,5},{5,6},{6,7},{7,4},{8,9},{9,10},{10,1... | collective-permute-start | bytes 98312 | tf_op jit(solution)/shard_map/ppermute | solution.py:352
  21.0 6.6 %collective-permute-start.2 = (bf16[16,1024]{1,0:T(8,128)(2,1)S(1)}, bf16[16,1024]{1,0:T(8,128)(2,1)S(1)}, u32[]{:S(2)}, u32[]{:S(2)}) collective-permute-start(bf16[16,1024]{1,0:T(8,128)(2,1)S(1)} %pad_maximum_fusion), channel_id=1, source_target_pairs={{0,2},{1,3},{2,0},{3,1},{4,6},{5,7},{6,4},{7,5},{8,10},{9,11},{10,... | collective-permute-start | bytes 98312 | tf_op jit(solution)/shard_map/ppermute | solution.py:352
  27.7 4.5 %collective-permute-start.4 = (bf16[64,1024]{1,0:T(8,128)(2,1)S(1)}, bf16[64,1024]{1,0:T(8,128)(2,1)S(1)}, u32[]{:S(2)}, u32[]{:S(2)}) collective-permute-start(bf16[64,1024]{1,0:T(8,128)(2,1)S(1)} %get-tuple-element.16), channel_id=1, source_target_pairs={{0,8},{4,12},{8,0},{12,4},{16,24},{20,28},{24,16},{28,20},{1,9},{5... | collective-permute-start | bytes 393224 | tf_op jit(solution)/shard_map/ppermute | solution.py:340
  29.0 4.9 %collective-permute-start.5 = (bf16[64,1024]{1,0:T(8,128)(2,1)S(1)}, bf16[64,1024]{1,0:T(8,128)(2,1)S(1)}, u32[]{:S(2)}, u32[]{:S(2)}) collective-permute-start(bf16[64,1024]{1,0:T(8,128)(2,1)S(1)} %get-tuple-element.16), channel_id=1, source_target_pairs={{0,16},{4,20},{8,24},{12,28},{16,0},{20,4},{24,8},{28,12},{1,17},{... | collective-permute-start | bytes 393224 | tf_op jit(solution)/shard_map/ppermute | solution.py:340
  30.2 6.0 %collective-permute-start.6 = (bf16[64,1024]{1,0:T(8,128)(2,1)S(1)}, bf16[64,1024]{1,0:T(8,128)(2,1)S(1)}, u32[]{:S(2)}, u32[]{:S(2)}) collective-permute-start(bf16[64,1024]{1,0:T(8,128)(2,1)S(1)} %get-tuple-element.16), channel_id=1, source_target_pairs={{0,24},{4,28},{8,16},{12,20},{16,8},{20,12},{24,0},{28,4},{1,25},{... | collective-permute-start | bytes 393224 | tf_op jit(solution)/shard_map/ppermute | solution.py:340
  31.8 25.7 %collective-permute-start.10 = (bf16[32,16,256]{2,1,0:T(8,128)(2,1)S(1)}, bf16[32,16,256]{2,1,0:T(8,128)(2,1)S(1)}, u32[]{:S(2)}, u32[]{:S(2)}) collective-permute-start(bf16[32,16,256]{2,1,0:T(8,128)(2,1)S(1)} %get-tuple-element.10), channel_id=1, source_target_pairs={{0,3},{1,0},{2,1},{3,2},{4,7},{5,4},{6,5},{7,6},{8,11},{9,8},{10,9... | collective-permute-start | bytes 786440 | tf_op jit(solution)/shard_map/ppermute | solution.py:352
  32.2 25.4 %collective-permute-start.9 = (bf16[32,16,256]{2,1,0:T(8,128)(2,1)S(1)}, bf16[32,16,256]{2,1,0:T(8,128)(2,1)S(1)}, u32[]{:S(2)}, u32[]{:S(2)}) collective-permute-start(bf16[32,16,256]{2,1,0:T(8,128)(2,1)S(1)} %get-tuple-element.9), channel_id=1, source_target_pairs={{0,2},{1,3},{2,0},{3,1},{4,6},{5,7},{6,4},{7,5},{8,10},{9,11},{10,... | collective-permute-start | bytes 786440 | tf_op jit(solution)/shard_map/ppermute | solution.py:352
  32.2 25.4 %collective-permute-start.8 = (bf16[32,16,256]{2,1,0:T(8,128)(2,1)S(1)}, bf16[32,16,256]{2,1,0:T(8,128)(2,1)S(1)}, u32[]{:S(2)}, u32[]{:S(2)}) collective-permute-start(bf16[32,16,256]{2,1,0:T(8,128)(2,1)S(1)} %get-tuple-element.8), channel_id=1, source_target_pairs={{0,1},{1,2},{2,3},{3,0},{4,5},{5,6},{6,7},{7,4},{8,9},{9,10},{10,1... | collective-permute-start | bytes 786440 | tf_op jit(solution)/shard_map/ppermute | solution.py:352
  36.3 19.4 %copy-start.6 = (bf16[256,1024]{1,0:T(8,128)(2,1)}, bf16[256,1024]{1,0:T(8,128)(2,1)S(1)}, u32[]{:S(2)}) copy-start(bf16[256,1024]{1,0:T(8,128)(2,1)S(1)} %constant_dynamic-update-slice_fusion.5.values_ref.refs_5_) | copy-start | bytes 1572868
  58.8 30.5 %collective-permute-start.17 = (bf16[32,64,256]{2,1,0:T(8,128)(2,1)}, bf16[32,64,256]{2,1,0:T(8,128)(2,1)}, u32[]{:S(2)}, u32[]{:S(2)}) collective-permute-start(bf16[32,64,256]{2,1,0:T(8,128)(2,1)} %maximum_select_fusion.refs_1_.refs_0_), channel_id=1, source_target_pairs={{0,16},{4,20},{8,24},{12,28},{16,0},{20,4},{24,8},{28,12},{1,17},{... | collective-permute-start | bytes 3145736 | tf_op jit(solution)/shard_map/ppermute | solution.py:340
  59.0 27.5 %collective-permute-start.13 = (bf16[32,16,256]{2,1,0:T(8,128)(2,1)S(1)}, bf16[32,16,256]{2,1,0:T(8,128)(2,1)S(1)}, u32[]{:S(2)}, u32[]{:S(2)}) collective-permute-start(bf16[32,16,256]{2,1,0:T(8,128)(2,1)S(1)} %get-tuple-element.13), channel_id=1, source_target_pairs={{0,3},{1,0},{2,1},{3,2},{4,7},{5,4},{6,5},{7,6},{8,11},{9,8},{10,9... | collective-permute-start | bytes 786440 | tf_op jit(solution)/shard_map/ppermute | solution.py:352
  59.8 26.7 %collective-permute-start.12 = (bf16[32,16,256]{2,1,0:T(8,128)(2,1)S(1)}, bf16[32,16,256]{2,1,0:T(8,128)(2,1)S(1)}, u32[]{:S(2)}, u32[]{:S(2)}) collective-permute-start(bf16[32,16,256]{2,1,0:T(8,128)(2,1)S(1)} %get-tuple-element.12), channel_id=1, source_target_pairs={{0,2},{1,3},{2,0},{3,1},{4,6},{5,7},{6,4},{7,5},{8,10},{9,11},{10,... | collective-permute-start | bytes 786440 | tf_op jit(solution)/shard_map/ppermute | solution.py:352
  60.6 25.9 %collective-permute-start.11 = (bf16[32,16,256]{2,1,0:T(8,128)(2,1)S(1)}, bf16[32,16,256]{2,1,0:T(8,128)(2,1)S(1)}, u32[]{:S(2)}, u32[]{:S(2)}) collective-permute-start(bf16[32,16,256]{2,1,0:T(8,128)(2,1)S(1)} %get-tuple-element.11), channel_id=1, source_target_pairs={{0,1},{1,2},{2,3},{3,0},{4,5},{5,6},{6,7},{7,4},{8,9},{9,10},{10,1... | collective-permute-start | bytes 786440 | tf_op jit(solution)/shard_map/ppermute | solution.py:352
  62.2 29.6 %collective-permute-start.16 = (bf16[32,64,256]{2,1,0:T(8,128)(2,1)}, bf16[32,64,256]{2,1,0:T(8,128)(2,1)}, u32[]{:S(2)}, u32[]{:S(2)}) collective-permute-start(bf16[32,64,256]{2,1,0:T(8,128)(2,1)} %maximum_select_fusion.refs_1_.refs_0_), channel_id=1, source_target_pairs={{0,8},{4,12},{8,0},{12,4},{16,24},{20,28},{24,16},{28,20},{1,9},{5... | collective-permute-start | bytes 3145736 | tf_op jit(solution)/shard_map/ppermute | solution.py:340
  82.6 4.7 %copy-start.8 = (f32[256,256]{1,0:T(8,128)S(1)}, f32[256,256]{1,0:T(8,128)}, u32[]{:S(2)}) copy-start(f32[256,256]{1,0:T(8,128)} %constant.158.clone) | copy-start | bytes 786436
  83.2 2.0 copy-start.2
  86.7 29.8 %collective-permute-start.15 = (bf16[32,64,256]{2,1,0:T(8,128)(2,1)S(1)}, bf16[32,64,256]{2,1,0:T(8,128)(2,1)S(1)}, u32[]{:S(2)}, u32[]{:S(2)}) collective-permute-start(bf16[32,64,256]{2,1,0:T(8,128)(2,1)S(1)} %maximum_select_fusion.1.refs_1_.refs_0_), channel_id=1, source_target_pairs={{0,16},{4,20},{8,24},{12,28},{16,0},{20,4},{24,8},{28,12},{1,17},{... | collective-permute-start | bytes 3145736 | tf_op jit(solution)/shard_map/ppermute | solution.py:340
  87.0 30.0 %collective-permute-start.14 = (bf16[32,64,256]{2,1,0:T(8,128)(2,1)S(1)}, bf16[32,64,256]{2,1,0:T(8,128)(2,1)S(1)}, u32[]{:S(2)}, u32[]{:S(2)}) collective-permute-start(bf16[32,64,256]{2,1,0:T(8,128)(2,1)S(1)} %maximum_select_fusion.1.refs_1_.refs_0_), channel_id=1, source_target_pairs={{0,8},{4,12},{8,0},{12,4},{16,24},{20,28},{24,16},{28,20},{1,9},{5... | collective-permute-start | bytes 3145736 | tf_op jit(solution)/shard_map/ppermute | solution.py:340
  90.4 48.0 %collective-permute-start.20 = (bf16[32,32,256]{2,1,0:T(8,128)(2,1)S(1)}, bf16[32,32,256]{2,1,0:T(8,128)(2,1)S(1)}, u32[]{:S(2)}, u32[]{:S(2)}) collective-permute-start(bf16[32,32,256]{2,1,0:T(8,128)(2,1)S(1)} %slice_select_fusion.1), channel_id=1, source_target_pairs={{0,8},{4,12},{8,0},{12,4},{16,24},{20,28},{24,16},{28,20},{1,9},{5... | collective-permute-start | bytes 1572872 | tf_op jit(solution)/shard_map/ppermute | solution.py:340
  92.8 45.5 %collective-permute-start.21 = (bf16[32,32,256]{2,1,0:T(8,128)(2,1)S(1)}, bf16[32,32,256]{2,1,0:T(8,128)(2,1)S(1)}, u32[]{:S(2)}, u32[]{:S(2)}) collective-permute-start(bf16[32,32,256]{2,1,0:T(8,128)(2,1)S(1)} %slice_select_fusion), channel_id=1, source_target_pairs={{0,16},{4,20},{8,24},{12,28},{16,0},{20,4},{24,8},{28,12},{1,17},{... | collective-permute-start | bytes 1572872 | tf_op jit(solution)/shard_map/ppermute | solution.py:340
  94.1 2.2 copy-start.3
  116.6 35.2 %collective-permute-start.18 = (bf16[32,32,256]{2,1,0:T(8,128)(2,1)S(1)}, bf16[32,32,256]{2,1,0:T(8,128)(2,1)S(1)}, u32[]{:S(2)}, u32[]{:S(2)}) collective-permute-start(bf16[32,32,256]{2,1,0:T(8,128)(2,1)S(1)} %slice_select_fusion.3), channel_id=1, source_target_pairs={{0,8},{4,12},{8,0},{12,4},{16,24},{20,28},{24,16},{28,20},{1,9},{5... | collective-permute-start | bytes 1572872 | tf_op jit(solution)/shard_map/ppermute | solution.py:340
  117.1 21.3 %copy-start.7 = (bf16[256,1024]{1,0:T(8,128)(2,1)S(1)}, bf16[256,1024]{1,0:T(8,128)(2,1)}, u32[]{:S(2)}) copy-start(bf16[256,1024]{1,0:T(8,128)(2,1)} %copy-done.6) | copy-start | bytes 1572868
  117.1 34.7 %collective-permute-start.19 = (bf16[32,32,256]{2,1,0:T(8,128)(2,1)S(1)}, bf16[32,32,256]{2,1,0:T(8,128)(2,1)S(1)}, u32[]{:S(2)}, u32[]{:S(2)}) collective-permute-start(bf16[32,32,256]{2,1,0:T(8,128)(2,1)S(1)} %slice_select_fusion.2), channel_id=1, source_target_pairs={{0,16},{4,20},{8,24},{12,28},{16,0},{20,4},{24,8},{28,12},{1,17},{... | collective-permute-start | bytes 1572872 | tf_op jit(solution)/shard_map/ppermute | solution.py:340
  136.3 2.0 copy-start.4
  186.3 29.1 %collective-permute-start.22 = (bf16[32,64,1024]{2,1,0:T(8,128)(2,1)}, bf16[32,64,1024]{2,1,0:T(8,128)(2,1)}, u32[]{:S(2)}, u32[]{:S(2)}) collective-permute-start(bf16[32,64,1024]{2,1,0:T(8,128)(2,1)} %fit.3), channel_id=1, source_target_pairs={{0,4},{4,0},{8,12},{12,8},{16,20},{20,16},{24,28},{28,24},{1,5},{5... | collective-permute-start | bytes 12582920 | tf_op jit(solution)/shard_map/ppermute | solution.py:340
  192.3 2.2 copy-start.5
  215.3 5.0 %copy-start.1 = (f32[256,128]{1,0:T(8,128)S(1)}, f32[256,128]{1,0:T(8,128)}, u32[]{:S(2)}) copy-start(f32[256,128]{1,0:T(8,128)} %param.6) | copy-start | bytes 393220
where the time goes:
time: 223 us; the launch traced here: 220 us
  Pallas kernels  154 us (69%)
  starting transfers between devices  24.3 us (11%)
  local copies, waits for them, and re-layouts  20.4 us (9%)
  waiting for transfers between devices  7.55 us (3%)
  other arithmetic  7.46 us (3%)
  between operations  5.76 us (3%)
    pallas_call x2, Pallas kernels, fit(): pl.pallas_call(fit_kernel, grid_spec=pltpu.PrefetchScalarGridSpec(num_sca...  43 us
    pallas_call x2, Pallas kernels, sweep_gram(): pl.pallas_call(functools.partial(middle_kernel, step=step, **options), ou...  36.7 us
    pallas_call x2, Pallas kernels, convolve(): pl.pallas_call(functools.partial(column_kernel, pieces=len(pieces)), grid...  25.7 us
    pallas_call x1, Pallas kernels, sweep_gram(): pl.pallas_call(functools.partial(first_kernel, **options), out_shape=stat...  19.4 us
    pallas_call x1, Pallas kernels, sweep_gram(): pl.pallas_call(functools.partial(last_kernel, step=step, **options), out_...  19 us
    ppermute x14, starting transfers between devices, hop(): return lax.ppermute(array, 'gz', [(z, z ^ bit) for z in range(gz_count)])  14.1 us
    unnamed x27, local copies, waits for them, and re-layouts  12.1 us
    ppermute x9, starting transfers between devices, gy_shift(): lax.ppermute(array, 'gy', [(y, (y + by) % gy_count) for y in range(gy_cou...  10.2 us
  transfers between devices with their start and end apart: 23, of which 3 were waited for; matrix products, arithmetic and copies ran while one was open for 4% of the time, Pallas kernels for 54%

commit v1 on v0

--- a/solution.py
+++ b/solution.py
@@ -29,16 +29,18 @@
 
         def some(s, accs):
             accs = list(accs)
-            for u in range(16):
-                m = s * 16 + u
+            first = s * 32
+            late = lane - first
+            for u in range(32):
+                m = first + u
                 column = where_ref[0, base + m]
                 at = pl.multiple_of(where_ref[1, base + m], 128)
                 row = field_ref[column, :, pl.ds(at, 128)]
                 row = pltpu.roll(row, where_ref[2, base + m], 1)
-                accs[u % 4] = jnp.where(lane == m, row, accs[u % 4])
+                accs[u % 4] = jnp.where(late == u, row, accs[u % 4])
             return tuple(accs)
 
-        accs = lax.fori_loop(0, 8, some, (jnp.zeros((bands, 128), F32),) * 4)
+        accs = lax.fori_loop(0, 4, some, (jnp.zeros((bands, 128), F32),) * 4)
         out_ref[:, pl.ds(base, 128)] = (accs[0] + accs[1]) + (accs[2] + accs[3])
         return 0
 
@@ -75,9 +77,7 @@
         t = [c[lo : lo + 8, :] for c in cols]
         for k in range(8):
             pivot = jnp.broadcast_to(t[k][k : k + 1, :], (8, n))
-            scale = pl.reciprocal(pivot, approx=True)
-            scale = scale * (2.0 - pivot * scale)
-            scale = scale * (2.0 - pivot * scale)
+            scale = 1.0 / pivot
             here = sub == k
             new = []
             for j in range(8):
@@ -181,7 +181,7 @@
     state = jax.ShapeDtypeStruct((n, n), F32)
     scratch = [pltpu.VMEM((big, big), F32), pltpu.VMEM((big, n), F32)]
     options = dict(big=big, small=small)
-    params = pltpu.CompilerParams(vmem_limit_bytes=24 * MIB)
+    params = pltpu.CompilerParams(vmem_limit_bytes=16 * MIB)
     cost = pl.CostEstimate(flops=n * n, bytes_accessed=n * n, transcendentals=0)
     if step == 0:
         return pl.pallas_call(
@@ -221,10 +221,10 @@
 
 def column_kernel(*refs, pieces):
     fields = refs[:pieces]
-    values_ref, lags_ref, out_ref = refs[pieces], refs[pieces + 1], refs[-1]
-    step, planes_out, _ = out_ref.shape
+    values_ref, lags_ref, own_ref, other_ref = refs[pieces], refs[pieces + 1], refs[-2], refs[-1]
+    step, slab, _ = own_ref.shape
     n = values_ref.shape[1]
-    planes = lags_ref.shape[1]
+    planes = lags_ref.shape[2]
     first = pl.program_id(0) * step
     turned = [jnp.concatenate([f[i] for f in fields], axis=0).T for i in range(step)]
     sums = jnp.dot(
@@ -233,64 +233,77 @@
     for i in range(step):
         mine = sums[i * planes : (i + 1) * planes]
         high, low = split(mine * mine)
-        row = jnp.broadcast_to(lags_ref[pl.ds(first + i, 1), :], (planes_out, planes))
-        circ_high, circ_low = split(pltpu.roll(row, 0, 1, stride=1, stride_axis=0))
-        circ = jnp.concatenate([circ_high, circ_low], axis=0)
+        circ = []
+        for whose in range(2):
+            row = jnp.broadcast_to(lags_ref[whose, pl.ds(first + i, 1), :], (slab, planes))
+            circ.append(pltpu.roll(row, 0, 1, stride=1, stride_axis=0))
+        circ = jnp.concatenate(split(jnp.concatenate(circ, axis=0)), axis=0)
         both = jnp.dot(
             jnp.concatenate([circ, circ], axis=1),
             jnp.concatenate([high, low], axis=0),
             preferred_element_type=F32,
         )
-        w_high, w_low = split(both[:planes_out] + both[planes_out:])
-        out_ref[i, :, :n] = w_high
-        out_ref[i, :, n:] = w_low
-
-
-def convolve(pieces, values, lags, planes_out, start, state, after):
+        w_high, w_low = split(both[: 2 * slab] + both[2 * slab :])
+        own_ref[i, :, :n] = w_high[:slab]
+        own_ref[i, :, n:] = w_low[:slab]
+        other_ref[i, :, :n] = w_high[slab:]
+        other_ref[i, :, n:] = w_low[slab:]
+
+
+def convolve(pieces, values, lags, slab, start, state, after):
     cols, _, planes = pieces[0].shape
-    all_cols = lags.shape[0]
+    all_cols = lags.shape[1]
     bands, n = values.shape
     step = 4
-    extra = ([] if state is None else [state]) + list(after)
+    shape = jax.ShapeDtypeStruct((all_cols, slab, 2 * n), BF16)
+    out_spec = pl.BlockSpec((step, slab, 2 * n), lambda j: (j + start // step, 0, 0))
     return pl.pallas_call(
         functools.partial(column_kernel, pieces=len(pieces)),
         grid=(cols // step,),
-        out_shape=jax.ShapeDtypeStruct((all_cols, planes_out, 2 * n), BF16),
+        out_shape=(shape, shape),
         in_specs=[pl.BlockSpec((step, p.shape[1], planes), lambda j: (j, 0, 0)) for p in pieces]
         + [
             pl.BlockSpec((bands, n), lambda j: (0, 0)),
-            pl.BlockSpec((cols, planes), lambda j: (start // cols, 0)),
+            pl.BlockSpec((2, cols, planes), lambda j: (0, start // cols, 0)),
         ]
-        + [pl.BlockSpec(memory_space=pl.ANY)] * len(extra),
-        out_specs=pl.BlockSpec((step, planes_out, 2 * n), lambda j: (j + start // step, 0, 0)),
-        input_output_aliases={} if state is None else {len(pieces) + 2: 0},
-        compiler_params=pltpu.CompilerParams(vmem_limit_bytes=40 * MIB),
+        + [pl.BlockSpec(memory_space=pl.ANY)] * (len(state) + len(after)),
+        out_specs=(out_spec, out_spec),
+        input_output_aliases={len(pieces) + 2 + i: i for i in range(len(state))},
+        compiler_params=pltpu.CompilerParams(vmem_limit_bytes=28 * MIB),
         cost_estimate=pl.CostEstimate(
-            flops=2 * cols * n * planes * (bands + 4 * planes_out),
-            bytes_accessed=2 * cols * (bands * planes + 2 * planes_out * n),
+            flops=2 * cols * n * planes * (bands + 8 * slab),
+            bytes_accessed=2 * cols * (bands * planes + 4 * slab * n),
             transcendentals=0,
         ),
         name="convolve",
-    )(*pieces, values, lags, *extra)
-
-
-def fit_kernel(at_ref, w_ref, inverse_ref, out_ref, turn):
+    )(*pieces, values, lags, *state, *after)
+
+
+def fit_kernel(at_ref, w_ref, inverse_ref, *refs):
+    out_ref, turn = refs[-2:]
     slab, cols, n = out_ref.shape
     w = w_ref[...].reshape(cols * slab, 2 * n)
-    out = jnp.dot(w[:, :n], inverse_ref[:n], preferred_element_type=F32)
-    out = out + jnp.dot(w[:, :n], inverse_ref[n:], preferred_element_type=F32)
-    out = out + jnp.dot(w[:, n:], inverse_ref[:n], preferred_element_type=F32)
-    for t in range(n // 128):
-        lanes = slice(t * 128, (t + 1) * 128)
-        for c in range(cols):
-            turn[t, pl.ds(c, slab, stride=cols), :] = out[c * slab : (c + 1) * slab, lanes]
-        out_ref[:, :, lanes] = turn[t].reshape(slab, cols, 128).astype(out_ref.dtype)
-
-
-def fit(at, w, inverse, width):
-    cols, planes_out, n2 = w.shape
+    w_high, w_low = w[:, :n], w[:, n:]
+    tile = 256
+    for first in range(0, n, tile):
+        lanes = slice(first, first + tile)
+        high = inverse_ref[:n, lanes]
+        out = jnp.dot(w_high, high, preferred_element_type=F32)
+        out = out + jnp.dot(w_high, inverse_ref[n:, lanes], preferred_element_type=F32)
+        out = out + jnp.dot(w_low, high, preferred_element_type=F32)
+        for t in range(tile // 128):
+            at = first // 128 + t
+            part = slice(t * 128, (t + 1) * 128)
+            for c in range(cols):
+                turn[at, pl.ds(c, slab, stride=cols), :] = out[c * slab : (c + 1) * slab, part]
+            out_ref[:, :, at * 128 : (at + 1) * 128] = (
+                turn[at].reshape(slab, cols, 128).astype(out_ref.dtype)
+            )
+
+
+def fit(at, w, inverse, width, state):
+    cols, slab, n2 = w.shape
     n = n2 // 2
-    slab = planes_out // 2
     step = 16
     return pl.pallas_call(
         fit_kernel,
@@ -298,21 +311,23 @@
             num_scalar_prefetch=1,
             grid=(cols // step,),
             in_specs=[
-                pl.BlockSpec((step, slab, n2), lambda j, at: (j, at[0], 0)),
+                pl.BlockSpec((step, slab, n2), lambda j, at: (j, 0, 0)),
                 pl.BlockSpec((2 * n, n), lambda j, at: (0, 0)),
-            ],
-            out_specs=pl.BlockSpec((slab, step, n), lambda j, at: (0, j + at[1], 0)),
+            ]
+            + [pl.BlockSpec(memory_space=pl.ANY)] * len(state),
+            out_specs=pl.BlockSpec((slab, step, n), lambda j, at: (0, j + at[0], 0)),
             scratch_shapes=[pltpu.VMEM((n // 128, slab * step, 128), F32)],
         ),
         out_shape=jax.ShapeDtypeStruct((slab, width, n), BF16),
-        compiler_params=pltpu.CompilerParams(vmem_limit_bytes=48 * MIB),
+        input_output_aliases={3: 0} if state else {},
+        compiler_params=pltpu.CompilerParams(vmem_limit_bytes=32 * MIB),
         cost_estimate=pl.CostEstimate(
             flops=6 * cols * slab * n * n,
             bytes_accessed=6 * cols * slab * n + 4 * n * n,
             transcendentals=0,
         ),
         name="fit",
-    )(at, w, inverse)
+    )(at, w, inverse, *state)
 
 
 def zero_after(array):
@@ -331,7 +346,6 @@
     slab = planes // gz_count
     pairs = gz_count // 2
     me = gz % 2
-    pair = gz // 2
     total_bands = bands_local * gz_count * gy_count
     chunks = 2
     chunk = half // chunks
@@ -412,15 +426,17 @@
     lags = jnp.dot(
         kernel, jnp.asarray(table / planes, F32), precision=HIGH, preferred_element_type=F32
     )
-    lags = jnp.roll(lags, pair * (2 * slab), axis=1)
-
-    weights = None
+    lags = jnp.stack([jnp.roll(lags, z * slab, axis=1) for z in (gz, gz ^ 1)])
+
+    weights = ()
     for c in range(chunks):
-        weights = convolve(fields[c], values, lags, 2 * slab, c * chunk, weights, ())
-    there = fit(jnp.stack([1 - me, jnp.zeros((), jnp.int32)]), weights, inverse, half)
-    there = hop(there, 1)
-    result = fit(jnp.stack([me, me * half // 16]), weights, inverse, col_block)
-    return lax.dynamic_update_slice(result, there, (0, (1 - me) * half, 0))
+        after = (inverse,) if c else ()
+        weights = convolve(fields[c], values, lags, slab, c * chunk, weights, after)
+    own_weights, other_weights = weights
+    other_weights = hop(other_weights, 1)
+    blocks_of_16 = half // 16
+    result = fit((me * blocks_of_16)[None], own_weights, inverse, col_block, ())
+    return fit(((1 - me) * blocks_of_16)[None], other_weights, inverse, col_block, (result,))
 
 
 def solution(mesh):

time: 223 us -> 218 us (0.978)
  Pallas kernels: 154 us -> 141 us
  local copies, waits for them, and re-layouts: 20.4 us -> 26.8 us
    unnamed x27 -> x37, local copies, waits for them, and re-layouts: 12.1 us -> 23.7 us
    dynamic_update_slice x1 -> x0, local copies, waits for them, and re-layouts: 4.95 us -> none  [per_device(): return lax.dynamic_update_slice(result, there, (0, (1 - me) * half, 0))]
    pallas_call x2, Pallas kernels: 36.7 us -> 32.5 us  [sweep_gram(): pl.pallas_call(functools.partial(middle_kernel, step=step, **options), ou...]
    pallas_call x2, Pallas kernels: 43 us -> 38.9 us  [fit(): pl.pallas_call(fit_kernel, grid_spec=pltpu.PrefetchScalarGridSpec(num_sca...]
  transfers between devices with their start and end apart: 23 -> 23, of which waited for: 3 -> 3; matrix products, arithmetic and copies ran while one was open for 4% -> 5% of each run, Pallas kernels for 54% -> 50%
where the time goes in v1:
time: 218 us; the launch traced here: 215 us
  Pallas kernels  141 us (65%)
  local copies, waits for them, and re-layouts  26.8 us (12%)
  starting transfers between devices  26.5 us (12%)
  other arithmetic  7.57 us (3%)
  waiting for transfers between devices  7.31 us (3%)
  between operations  5.52 us (3%)
    pallas_call x2, Pallas kernels, fit(): pl.pallas_call(fit_kernel, grid_spec=pltpu.PrefetchScalarGridSpec(num_sca...  38.9 us
    pallas_call x2, Pallas kernels, sweep_gram(): pl.pallas_call(functools.partial(middle_kernel, step=step, **options), ou...  32.5 us
    pallas_call x2, Pallas kernels, convolve(): pl.pallas_call(functools.partial(column_kernel, pieces=len(pieces)), grid...  27.2 us
    unnamed x37, local copies, waits for them, and re-layouts  23.7 us
    pallas_call x1, Pallas kernels, sweep_gram(): pl.pallas_call(functools.partial(first_kernel, **options), out_shape=stat...  17.4 us
    pallas_call x1, Pallas kernels, sweep_gram(): pl.pallas_call(functools.partial(last_kernel, step=step, **options), out_...  16.9 us
    ppermute x14, starting transfers between devices, hop(): return lax.ppermute(array, 'gz', [(z, z ^ bit) for z in range(gz_count)])  14.8 us
    ppermute x9, starting transfers between devices, gy_shift(): lax.ppermute(array, 'gy', [(y, (y + by) % gy_count) for y in range(gy_cou...  11.7 us
  transfers between devices with their start and end apart: 23, of which 3 were waited for; matrix products, arithmetic and copies ran while one was open for 5% of the time, Pallas kernels for 50%

profile of v1, /device:TPU:1, one launch (start us, length us, event | category | flops | bytes accessed | tf_op | source)
XLA Modules:
  0.0 215.4 jit_solution(11404234732243616535)
XLA Ops:
  0.0 3.4 %copy.10 = bf16[8,256,512]{1,0,2:T(8,128)(2,1)S(1)} copy(bf16[8,256,512]{2,1,0:T(8,128)(2,1)} %param.6) | data formatting | bytes 4194304 | tf_op args[0]
  3.4 1.1 dynamic-slice_bitcast_fusion.1
  4.6 0.3 bitcast_convert_fusion.field_ref
  4.9 0.3 copy-done.14
  5.2 7.8 %take_points.1 = f32[8,1024]{1,0:T(8,128)S(1)} custom-call(s32[3,1024]{1,0:T(4,128)S(1)} %pad_add_fusion.where_ref, f32[512,8,256]{2,1,0:T(8,128)S(1)} %bitcast_convert_fusion.field_ref), custom_call_target="tpu_custom_call" | custom-call | tf_op jit(solution)/shard_map/take_points/pallas_call | solution.py:55
  13.3 1.0 collective-permute-done
  14.3 4.5 %collective-permute-start.3 = (bf16[16,1024]{1,0:T(8,128)(2,1)S(1)}, bf16[16,1024]{1,0:T(8,128)(2,1)S(1)}, u32[]{:S(2)}, u32[]{:S(2)}) collective-permute-start(bf16[16,1024]{1,0:T(8,128)(2,1)S(1)} %pad_maximum_fusion.1), channel_id=1, source_target_pairs={{0,3},{1,0},{2,1},{3,2},{4,7},{5,4},{6,5},{7,6},{8,11},{9,8},{10,9... | collective-permute-start | bytes 98312 | tf_op jit(solution)/shard_map/ppermute | solution.py:366
  18.8 0.5 collective-permute-start.1
  19.3 4.1 %collective-permute-done.1 = bf16[16,1024]{1,0:T(8,128)(2,1)S(1)} collective-permute-done((bf16[16,1024]{1,0:T(8,128)(2,1)S(1)}, bf16[16,1024]{1,0:T(8,128)(2,1)S(1)}, u32[]{:S(2)}, u32[]{:S(2)}) %collective-permute-start.1) | collective-permute-done | bytes 32800 | tf_op jit(solution)/shard_map/ppermute | solution.py:366
  23.4 0.5 slice.38
  25.1 2.2 %collective-permute-start.6 = (bf16[64,1024]{1,0:T(8,128)(2,1)S(1)}, bf16[64,1024]{1,0:T(8,128)(2,1)S(1)}, u32[]{:S(2)}, u32[]{:S(2)}) collective-permute-start(bf16[64,1024]{1,0:T(8,128)(2,1)S(1)} %get-tuple-element.27), channel_id=1, source_target_pairs={{0,24},{4,28},{8,16},{12,20},{16,8},{20,12},{24,0},{28,4},{1,25},{... | collective-permute-start | bytes 393224 | tf_op jit(solution)/shard_map/ppermute | solution.py:354
  27.8 1.4 fusion.14
  29.3 0.9 collective-permute-start.9
  30.2 2.1 collective-permute-done.4
  32.4 1.3 collective-permute-start.10
  33.8 17.4 %sweep_first.1.refs_0_ = f32[1024,1024]{1,0:T(8,128)S(1)} custom-call(bf16[256,1024]{1,0:T(8,128)(2,1)S(1)} %constant_dynamic-update-slice_fusion.5.values_ref.refs_5_), custom_call_target="tpu_custom_call" | custom-call | flops 1048576 | bytes 1048576 | tf_op jit(solution)/shard_map/sweep_first/pallas_call | solution.py:187
  51.2 0.5 slice.37
  53.3 1.1 collective-permute-start.17
  54.4 1.9 collective-permute-start.11
  56.4 2.5 %collective-permute-start.13 = (bf16[32,16,256]{2,1,0:T(8,128)(2,1)S(1)}, bf16[32,16,256]{2,1,0:T(8,128)(2,1)S(1)}, u32[]{:S(2)}, u32[]{:S(2)}) collective-permute-start(bf16[32,16,256]{2,1,0:T(8,128)(2,1)S(1)} %get-tuple-element.22), channel_id=1, source_target_pairs={{0,3},{1,0},{2,1},{3,2},{4,7},{5,4},{6,5},{7,6},{8,11},{9,8},{10,9... | collective-permute-start | bytes 786440 | tf_op jit(solution)/shard_map/ppermute | solution.py:366
  58.9 1.3 collective-permute-start.16
  60.1 0.9 fusion.10
  61.1 16.2 %sweep_middle.2.refs_0_ = f32[1024,1024]{1,0:T(8,128)S(1)} custom-call(f32[1024,1024]{1,0:T(8,128)S(1)} %sweep_first.1.refs_0_, bf16[32,64,256]{2,1,0:T(8,128)(2,1)S(1)} %maximum_select_fusion.refs_1_.refs_0_), custom_call_target="tpu_custom_call", output_to_operand_aliasing={{}: (0, {})} | custom-call | flops 1048576 | bytes 1048576 | tf_op jit(solution)/shard_map/sweep_middle/pallas_call | solution.py:199
  77.3 0.5 slice.39
  77.8 2.0 copy-done.2
  81.8 1.1 fusion.16
  82.8 1.1 fusion.21
  83.9 1.1 slice_select_fusion.1
  85.0 1.3 collective-permute-start.20
  86.3 1.1 slice_select_fusion
  87.4 1.3 collective-permute-start.21
  88.8 2.2 %copy-done.3 = f32[1024,1024]{1,0:T(8,128)S(1)} copy-done((f32[1024,1024]{1,0:T(8,128)S(1)}, f32[1024,1024]{1,0:T(8,128)}, u32[]{:S(2)}) %copy-start.3) | copy-done | bytes 4194328
  90.9 16.2 %sweep_middle.3.gram_ref = f32[1024,1024]{1,0:T(8,128)S(1)} custom-call(f32[1024,1024]{1,0:T(8,128)S(1)} %copy-done.3, bf16[32,64,256]{2,1,0:T(8,128)(2,1)S(1)} %maximum_select_fusion.1.refs_1_.refs_0_, bf16[32,64,256]{2,1,0:T(8,128)(2,1)} %collective-permute-done.16.refs_2_.refs_1_, ...), custom_call_target="tpu_custom_call", output_to_operand_aliasing={{}: (0, {})} | custom-call | flops 1048576 | bytes 1048576 | tf_op jit(solution)/shard_map/sweep_middle/pallas_call | solution.py:199
  107.2 0.5 slice.40
  109.0 0.3 collective-permute-start.18
  109.3 1.1 slice_select_fusion.2
  110.4 0.3 collective-permute-start.19
  110.7 16.9 %sweep_last.1.refs_9_.inverse_ref = bf16[2048,1024]{1,0:T(8,128)(2,1)S(1)} custom-call(f32[1024,1024]{1,0:T(8,128)S(1)} %sweep_middle.3.gram_ref, bf16[32,64,256]{2,1,0:T(8,128)(2,1)} %collective-permute-done.14.refs_0_.refs_1_, bf16[32,64,256]{2,1,0:T(8,128)(2,1)S(1)} %collective-permute-done.15.refs_1_.refs_2_), custom_call_target="tpu_custom_call" | custom-call | flops 1048576 | bytes 1048576 | tf_op jit(solution)/shard_map/sweep_last/pallas_call | solution.py:210
  127.6 13.9 %convolve.2 = (bf16[64,32,2048]{2,1,0:T(8,128)(2,1)S(1)}, bf16[64,32,2048]{2,1,0:T(8,128)(2,1)}) custom-call(bf16[32,64,256]{2,1,0:T(8,128)(2,1)S(1)} %maximum_select_fusion.refs_1_.refs_0_, bf16[32,64,256]{2,1,0:T(8,128)(2,1)} %collective-permute-done.16.refs_2_.refs_1_, bf16[32,64,256]{2,1,0:T(8,128)(2,1)} %collective-permute-done.17.refs_3_.refs_2_, ...), custom_call_target="tpu_custom_call" | custom-call | flops 8589934592 | bytes 12582912 | tf_op jit(solution)/shard_map/convolve/pallas_call | solution.py:260
  141.6 3.4 %copy-done.9 = bf16[64,32,2048]{2,1,0:T(8,128)(2,1)} copy-done((bf16[64,32,2048]{2,1,0:T(8,128)(2,1)}, bf16[64,32,2048]{2,1,0:T(8,128)(2,1)S(1)}, u32[]{:S(2)}) %copy-start.9) | copy-done | bytes 8388632
  145.0 3.4 %copy-done.10 = bf16[64,32,2048]{2,1,0:T(8,128)(2,1)S(1)} copy-done((bf16[64,32,2048]{2,1,0:T(8,128)(2,1)S(1)}, bf16[64,32,2048]{2,1,0:T(8,128)(2,1)}, u32[]{:S(2)}) %copy-start.10) | copy-done | bytes 8388632
  148.4 13.2 %convolve.3 = (bf16[64,32,2048]{2,1,0:T(8,128)(2,1)S(1)}, bf16[64,32,2048]{2,1,0:T(8,128)(2,1)}) custom-call(bf16[32,64,256]{2,1,0:T(8,128)(2,1)S(1)} %maximum_select_fusion.1.refs_1_.refs_0_, bf16[32,64,256]{2,1,0:T(8,128)(2,1)} %collective-permute-done.14.refs_0_.refs_1_, ...), custom_call_target="tpu_custom_call", output_to_operand_aliasing={{0}: (7, {}), {1}: (8, {})} | custom-call | flops 8589934592 | bytes 12582912 | tf_op jit(solution)/shard_map/convolve/pallas_call | solution.py:260
  161.6 3.4 %copy-done.11 = bf16[64,32,2048]{2,1,0:T(8,128)(2,1)} copy-done((bf16[64,32,2048]{2,1,0:T(8,128)(2,1)}, bf16[64,32,2048]{2,1,0:T(8,128)(2,1)S(1)}, u32[]{:S(2)}) %copy-start.11) | copy-done | bytes 8388632
  165.0 5.7 %collective-permute-start.22 = (bf16[64,32,2048]{2,1,0:T(8,128)(2,1)}, bf16[64,32,2048]{2,1,0:T(8,128)(2,1)}, u32[]{:S(2)}, u32[]{:S(2)}) collective-permute-start(bf16[64,32,2048]{2,1,0:T(8,128)(2,1)} %get-tuple-element.12), channel_id=1, source_target_pairs={{0,4},{4,0},{8,12},{12,8},{16,20},{20,16},{24,28},{28,24},{1,5},{5... | collective-permute-start | bytes 25165832 | tf_op jit(solution)/shard_map/ppermute | solution.py:354
  170.7 2.2 %copy-done.5 = bf16[2048,1024]{1,0:T(8,128)(2,1)S(1)} copy-done((bf16[2048,1024]{1,0:T(8,128)(2,1)S(1)}, bf16[2048,1024]{1,0:T(8,128)(2,1)}, u32[]{:S(2)}) %copy-start.5) | copy-done | bytes 4194328
  172.9 3.4 %copy-done.12 = bf16[64,32,2048]{2,1,0:T(8,128)(2,1)S(1)} copy-done((bf16[64,32,2048]{2,1,0:T(8,128)(2,1)S(1)}, bf16[64,32,2048]{2,1,0:T(8,128)(2,1)}, u32[]{:S(2)}) %copy-start.12) | copy-done | bytes 8388632
  176.3 18.6 %fit.2.refs_0_ = bf16[32,128,1024]{2,1,0:T(8,128)(2,1)} custom-call(s32[1]{0:T(128)} %bitcast.23.at_ref, bf16[64,32,2048]{2,1,0:T(8,128)(2,1)S(1)} %copy-done.12, bf16[2048,1024]{1,0:T(8,128)(2,1)S(1)} %copy-done.5), custom_call_target="tpu_custom_call" | custom-call | flops 12884901888 | bytes 16777216 | tf_op jit(solution)/shard_map/fit/pallas_call | solution.py:308
  194.9 20.3 %fit.3 = bf16[32,128,1024]{2,1,0:T(8,128)(2,1)} custom-call(s32[1]{0:T(128)} %bitcast.at_ref, bf16[64,32,2048]{2,1,0:T(8,128)(2,1)} %collective-permute-done.22.w_ref, bf16[2048,1024]{1,0:T(8,128)(2,1)S(1)} %copy-done.6, bf16[32,128,1024]{2,1,0:T(8,128)(2,1)} %fit.2.refs_0_), custom_call_target="tpu_custom_call", output_to_operand_aliasing={{}: (3, {})} | custom-call | flops 12884901888 | bytes 16777216 | tf_op jit(solution)/shard_map/fit/pallas_call | solution.py:308
  (67 shorter events, 2.2 us)
Async XLA Ops:
  0.0 81.8 %copy-start = (f32[256,128]{1,0:T(8,128)S(1)}, f32[256,128]{1,0:T(8,128)}, u32[]{:S(2)}) copy-start(f32[256,128]{1,0:T(8,128)} %param.8) | copy-start | bytes 393220
  4.5 0.7 copy-start.14
  4.5 23.3 %collective-permute-start.7 = (bf16[4,64,8,256]{3,2,1,0:T(8,128)(2,1)}, bf16[4,64,8,256]{3,2,1,0:T(8,128)(2,1)}, u32[]{:S(2)}, u32[]{:S(2)}) collective-permute-start(bf16[4,64,8,256]{3,2,1,0:T(8,128)(2,1)} %get-tuple-element.24), channel_id=1, source_target_pairs={{0,4},{4,0},{8,12},{12,8},{16,20},{20,16},{24,28},{28,24},{1,5},{5... | collective-permute-start | bytes 3145736 | tf_op jit(solution)/shard_map/ppermute | solution.py:354
  13.1 1.2 collective-permute-start
  14.3 9.1 %collective-permute-start.3 = (bf16[16,1024]{1,0:T(8,128)(2,1)S(1)}, bf16[16,1024]{1,0:T(8,128)(2,1)S(1)}, u32[]{:S(2)}, u32[]{:S(2)}) collective-permute-start(bf16[16,1024]{1,0:T(8,128)(2,1)S(1)} %pad_maximum_fusion.1), channel_id=1, source_target_pairs={{0,3},{1,0},{2,1},{3,2},{4,7},{5,4},{6,5},{7,6},{8,11},{9,8},{10,9... | collective-permute-start | bytes 98312 | tf_op jit(solution)/shard_map/ppermute | solution.py:366
  18.8 6.2 %collective-permute-start.2 = (bf16[16,1024]{1,0:T(8,128)(2,1)S(1)}, bf16[16,1024]{1,0:T(8,128)(2,1)S(1)}, u32[]{:S(2)}, u32[]{:S(2)}) collective-permute-start(bf16[16,1024]{1,0:T(8,128)(2,1)S(1)} %pad_maximum_fusion.1), channel_id=1, source_target_pairs={{0,2},{1,3},{2,0},{3,1},{4,6},{5,7},{6,4},{7,5},{8,10},{9,11},{10,... | collective-permute-start | bytes 98312 | tf_op jit(solution)/shard_map/ppermute | solution.py:366
  18.8 4.6 %collective-permute-start.1 = (bf16[16,1024]{1,0:T(8,128)(2,1)S(1)}, bf16[16,1024]{1,0:T(8,128)(2,1)S(1)}, u32[]{:S(2)}, u32[]{:S(2)}) collective-permute-start(bf16[16,1024]{1,0:T(8,128)(2,1)S(1)} %pad_maximum_fusion.1), channel_id=1, source_target_pairs={{0,1},{1,2},{2,3},{3,0},{4,5},{5,6},{6,7},{7,4},{8,9},{9,10},{10,1... | collective-permute-start | bytes 98312 | tf_op jit(solution)/shard_map/ppermute | solution.py:366
  25.1 8.6 %collective-permute-start.6 = (bf16[64,1024]{1,0:T(8,128)(2,1)S(1)}, bf16[64,1024]{1,0:T(8,128)(2,1)S(1)}, u32[]{:S(2)}, u32[]{:S(2)}) collective-permute-start(bf16[64,1024]{1,0:T(8,128)(2,1)S(1)} %get-tuple-element.27), channel_id=1, source_target_pairs={{0,24},{4,28},{8,16},{12,20},{16,8},{20,12},{24,0},{28,4},{1,25},{... | collective-permute-start | bytes 393224 | tf_op jit(solution)/shard_map/ppermute | solution.py:354
  27.4 6.3 %collective-permute-start.5 = (bf16[64,1024]{1,0:T(8,128)(2,1)S(1)}, bf16[64,1024]{1,0:T(8,128)(2,1)S(1)}, u32[]{:S(2)}, u32[]{:S(2)}) collective-permute-start(bf16[64,1024]{1,0:T(8,128)(2,1)S(1)} %get-tuple-element.27), channel_id=1, source_target_pairs={{0,16},{4,20},{8,24},{12,28},{16,0},{20,4},{24,8},{28,12},{1,17},{... | collective-permute-start | bytes 393224 | tf_op jit(solution)/shard_map/ppermute | solution.py:354
  27.6 4.8 %collective-permute-start.4 = (bf16[64,1024]{1,0:T(8,128)(2,1)S(1)}, bf16[64,1024]{1,0:T(8,128)(2,1)S(1)}, u32[]{:S(2)}, u32[]{:S(2)}) collective-permute-start(bf16[64,1024]{1,0:T(8,128)(2,1)S(1)} %get-tuple-element.27), channel_id=1, source_target_pairs={{0,8},{4,12},{8,0},{12,4},{16,24},{20,28},{24,16},{28,20},{1,9},{5... | collective-permute-start | bytes 393224 | tf_op jit(solution)/shard_map/ppermute | solution.py:354
  29.2 23.8 %collective-permute-start.8 = (bf16[32,16,256]{2,1,0:T(8,128)(2,1)S(1)}, bf16[32,16,256]{2,1,0:T(8,128)(2,1)S(1)}, u32[]{:S(2)}, u32[]{:S(2)}) collective-permute-start(bf16[32,16,256]{2,1,0:T(8,128)(2,1)S(1)} %get-tuple-element.17), channel_id=1, source_target_pairs={{0,1},{1,2},{2,3},{3,0},{4,5},{5,6},{6,7},{7,4},{8,9},{9,10},{10,1... | collective-permute-start | bytes 786440 | tf_op jit(solution)/shard_map/ppermute | solution.py:366
  29.3 23.7 %collective-permute-start.9 = (bf16[32,16,256]{2,1,0:T(8,128)(2,1)S(1)}, bf16[32,16,256]{2,1,0:T(8,128)(2,1)S(1)}, u32[]{:S(2)}, u32[]{:S(2)}) collective-permute-start(bf16[32,16,256]{2,1,0:T(8,128)(2,1)S(1)} %get-tuple-element.18), channel_id=1, source_target_pairs={{0,2},{1,3},{2,0},{3,1},{4,6},{5,7},{6,4},{7,5},{8,10},{9,11},{10,... | collective-permute-start | bytes 786440 | tf_op jit(solution)/shard_map/ppermute | solution.py:366
  32.4 20.7 %collective-permute-start.10 = (bf16[32,16,256]{2,1,0:T(8,128)(2,1)S(1)}, bf16[32,16,256]{2,1,0:T(8,128)(2,1)S(1)}, u32[]{:S(2)}, u32[]{:S(2)}) collective-permute-start(bf16[32,16,256]{2,1,0:T(8,128)(2,1)S(1)} %get-tuple-element.19), channel_id=1, source_target_pairs={{0,3},{1,0},{2,1},{3,2},{4,7},{5,4},{6,5},{7,6},{8,11},{9,8},{10,9... | collective-permute-start | bytes 786440 | tf_op jit(solution)/shard_map/ppermute | solution.py:366
  33.7 17.5 %copy-start.7 = (bf16[256,1024]{1,0:T(8,128)(2,1)}, bf16[256,1024]{1,0:T(8,128)(2,1)S(1)}, u32[]{:S(2)}) copy-start(bf16[256,1024]{1,0:T(8,128)(2,1)S(1)} %constant_dynamic-update-slice_fusion.5.values_ref.refs_5_) | copy-start | bytes 1572868
  53.3 30.6 %collective-permute-start.17 = (bf16[32,64,256]{2,1,0:T(8,128)(2,1)S(1)}, bf16[32,64,256]{2,1,0:T(8,128)(2,1)}, u32[]{:S(2)}, u32[]{:S(2)}) collective-permute-start(bf16[32,64,256]{2,1,0:T(8,128)(2,1)S(1)} %maximum_select_fusion.refs_1_.refs_0_), channel_id=1, source_target_pairs={{0,16},{4,20},{8,24},{12,28},{16,0},{20,4},{24,8},{28,12},{1,17},{... | collective-permute-start | bytes 3145736 | tf_op jit(solution)/shard_map/ppermute | solution.py:354
  54.4 26.6 %collective-permute-start.11 = (bf16[32,16,256]{2,1,0:T(8,128)(2,1)S(1)}, bf16[32,16,256]{2,1,0:T(8,128)(2,1)S(1)}, u32[]{:S(2)}, u32[]{:S(2)}) collective-permute-start(bf16[32,16,256]{2,1,0:T(8,128)(2,1)S(1)} %get-tuple-element.20), channel_id=1, source_target_pairs={{0,1},{1,2},{2,3},{3,0},{4,5},{5,6},{6,7},{7,4},{8,9},{9,10},{10,1... | collective-permute-start | bytes 786440 | tf_op jit(solution)/shard_map/ppermute | solution.py:366
  56.3 24.7 %collective-permute-start.12 = (bf16[32,16,256]{2,1,0:T(8,128)(2,1)S(1)}, bf16[32,16,256]{2,1,0:T(8,128)(2,1)S(1)}, u32[]{:S(2)}, u32[]{:S(2)}) collective-permute-start(bf16[32,16,256]{2,1,0:T(8,128)(2,1)S(1)} %get-tuple-element.21), channel_id=1, source_target_pairs={{0,2},{1,3},{2,0},{3,1},{4,6},{5,7},{6,4},{7,5},{8,10},{9,11},{10,... | collective-permute-start | bytes 786440 | tf_op jit(solution)/shard_map/ppermute | solution.py:366
  56.4 24.6 %collective-permute-start.13 = (bf16[32,16,256]{2,1,0:T(8,128)(2,1)S(1)}, bf16[32,16,256]{2,1,0:T(8,128)(2,1)S(1)}, u32[]{:S(2)}, u32[]{:S(2)}) collective-permute-start(bf16[32,16,256]{2,1,0:T(8,128)(2,1)S(1)} %get-tuple-element.22), channel_id=1, source_target_pairs={{0,3},{1,0},{2,1},{3,2},{4,7},{5,4},{6,5},{7,6},{8,11},{9,8},{10,9... | collective-permute-start | bytes 786440 | tf_op jit(solution)/shard_map/ppermute | solution.py:366
  58.9 27.4 %collective-permute-start.16 = (bf16[32,64,256]{2,1,0:T(8,128)(2,1)S(1)}, bf16[32,64,256]{2,1,0:T(8,128)(2,1)}, u32[]{:S(2)}, u32[]{:S(2)}) collective-permute-start(bf16[32,64,256]{2,1,0:T(8,128)(2,1)S(1)} %maximum_select_fusion.refs_1_.refs_0_), channel_id=1, source_target_pairs={{0,8},{4,12},{8,0},{12,4},{16,24},{20,28},{24,16},{28,20},{1,9},{5... | collective-permute-start | bytes 3145736 | tf_op jit(solution)/shard_map/ppermute | solution.py:354
  77.3 4.5 %copy-start.13 = (f32[256,256]{1,0:T(8,128)S(1)}, f32[256,256]{1,0:T(8,128)}, u32[]{:S(2)}) copy-start(f32[256,256]{1,0:T(8,128)} %constant.132.clone) | copy-start | bytes 786436
  77.8 2.0 copy-start.2
  81.2 27.7 %collective-permute-start.15 = (bf16[32,64,256]{2,1,0:T(8,128)(2,1)S(1)}, bf16[32,64,256]{2,1,0:T(8,128)(2,1)S(1)}, u32[]{:S(2)}, u32[]{:S(2)}) collective-permute-start(bf16[32,64,256]{2,1,0:T(8,128)(2,1)S(1)} %maximum_select_fusion.1.refs_1_.refs_0_), channel_id=1, source_target_pairs={{0,16},{4,20},{8,24},{12,28},{16,0},{20,4},{24,8},{28,12},{1,17},{... | collective-permute-start | bytes 3145736 | tf_op jit(solution)/shard_map/ppermute | solution.py:354
  81.5 27.8 %collective-permute-start.14 = (bf16[32,64,256]{2,1,0:T(8,128)(2,1)S(1)}, bf16[32,64,256]{2,1,0:T(8,128)(2,1)}, u32[]{:S(2)}, u32[]{:S(2)}) collective-permute-start(bf16[32,64,256]{2,1,0:T(8,128)(2,1)S(1)} %maximum_select_fusion.1.refs_1_.refs_0_), channel_id=1, source_target_pairs={{0,8},{4,12},{8,0},{12,4},{16,24},{20,28},{24,16},{28,20},{1,9},{5... | collective-permute-start | bytes 3145736 | tf_op jit(solution)/shard_map/ppermute | solution.py:354
  85.0 42.6 %collective-permute-start.20 = (bf16[32,32,256]{2,1,0:T(8,128)(2,1)S(1)}, bf16[32,32,256]{2,1,0:T(8,128)(2,1)S(1)}, u32[]{:S(2)}, u32[]{:S(2)}) collective-permute-start(bf16[32,32,256]{2,1,0:T(8,128)(2,1)S(1)} %slice_select_fusion.1), channel_id=1, source_target_pairs={{0,8},{4,12},{8,0},{12,4},{16,24},{20,28},{24,16},{28,20},{1,9},{5... | collective-permute-start | bytes 1572872 | tf_op jit(solution)/shard_map/ppermute | solution.py:354
  87.4 40.2 %collective-permute-start.21 = (bf16[32,32,256]{2,1,0:T(8,128)(2,1)S(1)}, bf16[32,32,256]{2,1,0:T(8,128)(2,1)S(1)}, u32[]{:S(2)}, u32[]{:S(2)}) collective-permute-start(bf16[32,32,256]{2,1,0:T(8,128)(2,1)S(1)} %slice_select_fusion), channel_id=1, source_target_pairs={{0,16},{4,20},{8,24},{12,28},{16,0},{20,4},{24,8},{28,12},{1,17},{... | collective-permute-start | bytes 1572872 | tf_op jit(solution)/shard_map/ppermute | solution.py:354
  88.7 2.2 %copy-start.3 = (f32[1024,1024]{1,0:T(8,128)S(1)}, f32[1024,1024]{1,0:T(8,128)}, u32[]{:S(2)}) copy-start(f32[1024,1024]{1,0:T(8,128)} %copy-done.2) | copy-start | bytes 12582916
  109.0 35.9 %collective-permute-start.18 = (bf16[32,32,256]{2,1,0:T(8,128)(2,1)S(1)}, bf16[32,32,256]{2,1,0:T(8,128)(2,1)S(1)}, u32[]{:S(2)}, u32[]{:S(2)}) collective-permute-start(bf16[32,32,256]{2,1,0:T(8,128)(2,1)S(1)} %slice_select_fusion.3), channel_id=1, source_target_pairs={{0,8},{4,12},{8,0},{12,4},{16,24},{20,28},{24,16},{28,20},{1,9},{5... | collective-permute-start | bytes 1572872 | tf_op jit(solution)/shard_map/ppermute | solution.py:354
  110.4 17.2 %copy-start.8 = (bf16[256,1024]{1,0:T(8,128)(2,1)S(1)}, bf16[256,1024]{1,0:T(8,128)(2,1)}, u32[]{:S(2)}) copy-start(bf16[256,1024]{1,0:T(8,128)(2,1)} %copy-done.7) | copy-start | bytes 1572868
  110.4 34.5 %collective-permute-start.19 = (bf16[32,32,256]{2,1,0:T(8,128)(2,1)S(1)}, bf16[32,32,256]{2,1,0:T(8,128)(2,1)S(1)}, u32[]{:S(2)}, u32[]{:S(2)}) collective-permute-start(bf16[32,32,256]{2,1,0:T(8,128)(2,1)S(1)} %slice_select_fusion.2), channel_id=1, source_target_pairs={{0,16},{4,20},{8,24},{12,28},{16,0},{20,4},{24,8},{28,12},{1,17},{... | collective-permute-start | bytes 1572872 | tf_op jit(solution)/shard_map/ppermute | solution.py:354
  127.6 17.4 %copy-start.4 = (bf16[2048,1024]{1,0:T(8,128)(2,1)}, bf16[2048,1024]{1,0:T(8,128)(2,1)S(1)}, u32[]{:S(2)}) copy-start(bf16[2048,1024]{1,0:T(8,128)(2,1)S(1)} %sweep_last.1.refs_9_.inverse_ref) | copy-start | bytes 12582916
  141.6 3.4 %copy-start.9 = (bf16[64,32,2048]{2,1,0:T(8,128)(2,1)}, bf16[64,32,2048]{2,1,0:T(8,128)(2,1)S(1)}, u32[]{:S(2)}) copy-start(bf16[64,32,2048]{2,1,0:T(8,128)(2,1)S(1)} %get-tuple-element.10.refs_7_) | copy-start | bytes 25165828
  145.0 3.4 %copy-start.10 = (bf16[64,32,2048]{2,1,0:T(8,128)(2,1)S(1)}, bf16[64,32,2048]{2,1,0:T(8,128)(2,1)}, u32[]{:S(2)}) copy-start(bf16[64,32,2048]{2,1,0:T(8,128)(2,1)} %copy-done.9) | copy-start | bytes 25165828
  161.6 3.4 %copy-start.11 = (bf16[64,32,2048]{2,1,0:T(8,128)(2,1)}, bf16[64,32,2048]{2,1,0:T(8,128)(2,1)S(1)}, u32[]{:S(2)}) copy-start(bf16[64,32,2048]{2,1,0:T(8,128)(2,1)S(1)} %get-tuple-element.13.w_ref) | copy-start | bytes 25165828
  165.0 29.9 %collective-permute-start.22 = (bf16[64,32,2048]{2,1,0:T(8,128)(2,1)}, bf16[64,32,2048]{2,1,0:T(8,128)(2,1)}, u32[]{:S(2)}, u32[]{:S(2)}) collective-permute-start(bf16[64,32,2048]{2,1,0:T(8,128)(2,1)} %get-tuple-element.12), channel_id=1, source_target_pairs={{0,4},{4,0},{8,12},{12,8},{16,20},{20,16},{24,28},{28,24},{1,5},{5... | collective-permute-start | bytes 25165832 | tf_op jit(solution)/shard_map/ppermute | solution.py:354
  170.7 2.2 %copy-start.5 = (bf16[2048,1024]{1,0:T(8,128)(2,1)S(1)}, bf16[2048,1024]{1,0:T(8,128)(2,1)}, u32[]{:S(2)}) copy-start(bf16[2048,1024]{1,0:T(8,128)(2,1)} %copy-done.4) | copy-start | bytes 12582916
  172.9 3.4 %copy-start.12 = (bf16[64,32,2048]{2,1,0:T(8,128)(2,1)S(1)}, bf16[64,32,2048]{2,1,0:T(8,128)(2,1)}, u32[]{:S(2)}) copy-start(bf16[64,32,2048]{2,1,0:T(8,128)(2,1)} %copy-done.11) | copy-start | bytes 25165828
  176.3 18.6 %copy-start.6 = (bf16[2048,1024]{1,0:T(8,128)(2,1)S(1)}, bf16[2048,1024]{1,0:T(8,128)(2,1)}, u32[]{:S(2)}) copy-start(bf16[2048,1024]{1,0:T(8,128)(2,1)} %copy-done.4) | copy-start | bytes 12582916
  194.9 20.3 %copy-start.1 = (f32[256,128]{1,0:T(8,128)S(1)}, f32[256,128]{1,0:T(8,128)}, u32[]{:S(2)}) copy-start(f32[256,128]{1,0:T(8,128)} %param.8) | copy-start | bytes 393220

commit v2 on v1

--- a/solution.py
+++ b/solution.py
@@ -65,43 +65,54 @@
     )(where, field)
 
 
+def total(terms):
+    while len(terms) > 1:
+        terms = [x + y for x, y in zip(terms[::2], terms[1::2])]
+    return terms[0]
+
+
 def sweep_small(a):
     n = a.shape[0]
     lane = lax.broadcasted_iota(jnp.int32, (8, n), 1)
     wide = lax.broadcasted_iota(jnp.int32, (n, n), 1)
     sub = lax.broadcasted_iota(jnp.int32, (8, n), 0)
+
+    def spread(x, row):
+        return jnp.broadcast_to(x[row : row + 1, :], (8, n))
+
+    t = [jnp.broadcast_to(a[:8, j : j + 1], (8, n)) for j in range(8)]
     for g in range(n // 8):
         lo = 8 * g
-        rows = a[lo : lo + 8, :]
+        to = lo + 8
+        rows = a[lo:to, :]
         cols = [jnp.broadcast_to(a[:, lo + j : lo + j + 1], (n, n)) for j in range(8)]
-        t = [c[lo : lo + 8, :] for c in cols]
         for k in range(8):
-            pivot = jnp.broadcast_to(t[k][k : k + 1, :], (8, n))
-            scale = 1.0 / pivot
+            scale = 1.0 / spread(t[k], k)
             here = sub == k
             new = []
             for j in range(8):
                 if j == k:
                     new.append(jnp.where(here, -1.0, t[k]) * scale)
                 else:
-                    factor = jnp.broadcast_to(t[j][k : k + 1, :], (8, n))
                     kept = jnp.where(here, 0.0, t[j])
-                    new.append(kept - (jnp.where(here, -1.0, t[k]) * factor) * scale)
+                    new.append(kept - (jnp.where(here, -1.0, t[k]) * spread(t[j], k)) * scale)
             t = new
-        terms = [t[j] * jnp.broadcast_to(rows[j : j + 1, :], (8, n)) for j in range(8)]
-        while len(terms) > 1:
-            terms = [x + y for x, y in zip(terms[::2], terms[1::2])]
-        q = -terms[0]
+        swept = t
+        if to < n:
+            near = [c[to : to + 8, :] for c in cols]
+            t = []
+            for j in range(8):
+                held = jnp.broadcast_to(a[to : to + 8, to + j : to + j + 1], (8, n))
+                part = total([swept[m] * spread(near[m], j) for m in range(8)])
+                t.append(held + total([near[k] * spread(part, k) for k in range(8)]))
+        q = -total([swept[j] * spread(rows, j) for j in range(8)])
         for j in range(8):
-            q = jnp.where(lane == lo + j, t[j], q)
-        inside = (wide >= lo) & (wide < lo + 8)
-        terms = [cols[j] * jnp.broadcast_to(q[j : j + 1, :], (n, n)) for j in range(8)]
-        while len(terms) > 1:
-            terms = [x + y for x, y in zip(terms[::2], terms[1::2])]
-        upd = jnp.where(inside, 0.0, a) - terms[0]
-        a = jnp.concatenate(
-            ([upd[:lo]] if lo else []) + [q] + ([upd[lo + 8 :]] if lo + 8 < n else []), axis=0
+            q = jnp.where(lane == lo + j, swept[j], q)
+        inside = (wide >= lo) & (wide < to)
+        upd = jnp.where(inside, 0.0, a) - total(
+            [cols[j] * jnp.broadcast_to(q[j : j + 1, :], (n, n)) for j in range(8)]
         )
+        a = jnp.concatenate(([upd[:lo]] if lo else []) + [q] + ([upd[to:]] if to < n else []), axis=0)
     return a
 
 
@@ -269,7 +280,7 @@
         + [pl.BlockSpec(memory_space=pl.ANY)] * (len(state) + len(after)),
         out_specs=(out_spec, out_spec),
         input_output_aliases={len(pieces) + 2 + i: i for i in range(len(state))},
-        compiler_params=pltpu.CompilerParams(vmem_limit_bytes=28 * MIB),
+        compiler_params=pltpu.CompilerParams(vmem_limit_bytes=48 * MIB),
         cost_estimate=pl.CostEstimate(
             flops=2 * cols * n * planes * (bands + 8 * slab),
             bytes_accessed=2 * cols * (bands * planes + 4 * slab * n),
@@ -320,7 +331,7 @@
         ),
         out_shape=jax.ShapeDtypeStruct((slab, width, n), BF16),
         input_output_aliases={3: 0} if state else {},
-        compiler_params=pltpu.CompilerParams(vmem_limit_bytes=32 * MIB),
+        compiler_params=pltpu.CompilerParams(vmem_limit_bytes=56 * MIB),
         cost_estimate=pl.CostEstimate(
             flops=6 * cols * slab * n * n,
             bytes_accessed=6 * cols * slab * n + 4 * n * n,

time: 218 us -> 211 us (0.968)
  local copies, waits for them, and re-layouts: 26.8 us -> 13.2 us
  Pallas kernels: 141 us -> 145 us
    unnamed x37 -> x25, local copies, waits for them, and re-layouts: 23.7 us -> 9.95 us
    pallas_call x2, Pallas kernels: 38.9 us -> 43 us  [fit(): pl.pallas_call(fit_kernel, grid_spec=pltpu.PrefetchScalarGridSpec(num_sca...]
  transfers between devices with their start and end apart: 23 -> 23, of which waited for: 3 -> 3; matrix products, arithmetic and copies ran while one was open for 5% -> 6% of each run, Pallas kernels for 50% -> 53%
where the time goes in v2:
time: 211 us; the launch traced here: 208 us
  Pallas kernels  145 us (69%)
  starting transfers between devices  26.3 us (12%)
  local copies, waits for them, and re-layouts  13.2 us (6%)
  other arithmetic  9.16 us (4%)
  waiting for transfers between devices  7.31 us (3%)
  between operations  5.65 us (3%)
    pallas_call x2, Pallas kernels, fit(): pl.pallas_call(fit_kernel, grid_spec=pltpu.PrefetchScalarGridSpec(num_sca...  43 us
    pallas_call x2, Pallas kernels, sweep_gram(): pl.pallas_call(functools.partial(middle_kernel, step=step, **options), ou...  32.8 us
    pallas_call x2, Pallas kernels, convolve(): pl.pallas_call(functools.partial(column_kernel, pieces=len(pieces)), grid...  27 us
    pallas_call x1, Pallas kernels, sweep_gram(): pl.pallas_call(functools.partial(first_kernel, **options), out_shape=stat...  17.6 us
    pallas_call x1, Pallas kernels, sweep_gram(): pl.pallas_call(functools.partial(last_kernel, step=step, **options), out_...  17.1 us
    ppermute x14, starting transfers between devices, hop(): return lax.ppermute(array, 'gz', [(z, z ^ bit) for z in range(gz_count)])  15 us
    ppermute x9, starting transfers between devices, gy_shift(): lax.ppermute(array, 'gy', [(y, (y + by) % gy_count) for y in range(gy_cou...  11.3 us
    unnamed x25, local copies, waits for them, and re-layouts  9.95 us
  transfers between devices with their start and end apart: 23, of which 3 were waited for; matrix products, arithmetic and copies ran while one was open for 6% of the time, Pallas kernels for 53%

profile of v2, /device:TPU:1, one launch (start us, length us, event | category | flops | bytes accessed | tf_op | source)
XLA Modules:
  0.0 208.0 jit_solution(9865264594991538101)
XLA Ops:
  0.0 3.4 %copy.10 = bf16[8,256,512]{1,0,2:T(8,128)(2,1)S(1)} copy(bf16[8,256,512]{2,1,0:T(8,128)(2,1)} %param.6) | data formatting | bytes 4194304 | tf_op args[0]
  3.4 1.1 dynamic-slice_bitcast_fusion.1
  4.6 0.3 bitcast_convert_fusion.field_ref
  4.9 0.3 copy-done.8
  5.2 7.8 %take_points.1 = f32[8,1024]{1,0:T(8,128)S(1)} custom-call(s32[3,1024]{1,0:T(4,128)S(1)} %pad_add_fusion.where_ref, f32[512,8,256]{2,1,0:T(8,128)S(1)} %bitcast_convert_fusion.field_ref), custom_call_target="tpu_custom_call" | custom-call | tf_op jit(solution)/shard_map/take_points/pallas_call | solution.py:55
  13.3 1.0 collective-permute-done
  14.3 4.5 %collective-permute-start.3 = (bf16[16,1024]{1,0:T(8,128)(2,1)S(1)}, bf16[16,1024]{1,0:T(8,128)(2,1)S(1)}, u32[]{:S(2)}, u32[]{:S(2)}) collective-permute-start(bf16[16,1024]{1,0:T(8,128)(2,1)S(1)} %pad_maximum_fusion.1), channel_id=1, source_target_pairs={{0,3},{1,0},{2,1},{3,2},{4,7},{5,4},{6,5},{7,6},{8,11},{9,8},{10,9... | collective-permute-start | bytes 98312 | tf_op jit(solution)/shard_map/ppermute | solution.py:377
  18.8 0.5 collective-permute-start.1
  19.3 4.1 %collective-permute-done.1 = bf16[16,1024]{1,0:T(8,128)(2,1)S(1)} collective-permute-done((bf16[16,1024]{1,0:T(8,128)(2,1)S(1)}, bf16[16,1024]{1,0:T(8,128)(2,1)S(1)}, u32[]{:S(2)}, u32[]{:S(2)}) %collective-permute-start.1) | collective-permute-done | bytes 32800 | tf_op jit(solution)/shard_map/ppermute | solution.py:377
  23.4 0.5 slice.38
  25.1 2.2 %collective-permute-start.6 = (bf16[64,1024]{1,0:T(8,128)(2,1)S(1)}, bf16[64,1024]{1,0:T(8,128)(2,1)S(1)}, u32[]{:S(2)}, u32[]{:S(2)}) collective-permute-start(bf16[64,1024]{1,0:T(8,128)(2,1)S(1)} %get-tuple-element.27), channel_id=1, source_target_pairs={{0,24},{4,28},{8,16},{12,20},{16,8},{20,12},{24,0},{28,4},{1,25},{... | collective-permute-start | bytes 393224 | tf_op jit(solution)/shard_map/ppermute | solution.py:365
  27.6 0.3 collective-permute-start.4
  27.8 1.4 fusion.14
  29.3 0.9 collective-permute-start.9
  30.2 2.1 %collective-permute-done.4 = bf16[64,1024]{1,0:T(8,128)(2,1)S(1)} collective-permute-done((bf16[64,1024]{1,0:T(8,128)(2,1)S(1)}, bf16[64,1024]{1,0:T(8,128)(2,1)S(1)}, u32[]{:S(2)}, u32[]{:S(2)}) %collective-permute-start.4) | collective-permute-done | bytes 131104 | tf_op jit(solution)/shard_map/ppermute | solution.py:365
  32.4 1.5 collective-permute-start.10
  34.0 17.6 %sweep_first.1.refs_0_ = f32[1024,1024]{1,0:T(8,128)S(1)} custom-call(bf16[256,1024]{1,0:T(8,128)(2,1)S(1)} %constant_dynamic-update-slice_fusion.5.values_ref.refs_5_), custom_call_target="tpu_custom_call" | custom-call | flops 1048576 | bytes 1048576 | tf_op jit(solution)/shard_map/sweep_first/pallas_call | solution.py:198
  51.6 0.5 slice.37
  53.4 0.2 maximum_select_fusion.refs_1_.refs_0_
  53.7 1.1 collective-permute-start.17
  54.7 1.6 collective-permute-start.11
  56.3 0.4 collective-permute-start.12
  56.7 1.8 collective-permute-start.13
  58.5 1.3 collective-permute-start.16
  59.8 0.9 fusion.10
  60.7 16.3 %sweep_middle.2.refs_0_ = f32[1024,1024]{1,0:T(8,128)S(1)} custom-call(f32[1024,1024]{1,0:T(8,128)S(1)} %sweep_first.1.refs_0_, bf16[32,64,256]{2,1,0:T(8,128)(2,1)S(1)} %maximum_select_fusion.refs_1_.refs_0_), custom_call_target="tpu_custom_call", output_to_operand_aliasing={{}: (0, {})} | custom-call | flops 1048576 | bytes 1048576 | tf_op jit(solution)/shard_map/sweep_middle/pallas_call | solution.py:210
  77.1 0.6 slice.39
  77.7 2.0 copy-done.2
  81.4 0.3 collective-permute-start.15
  81.6 0.3 collective-permute-start.14
  81.9 1.1 fusion.16
  82.9 1.1 fusion.21
  84.1 1.1 slice_select_fusion.1
  85.1 1.3 collective-permute-start.20
  86.5 1.1 slice_select_fusion
  87.6 1.3 collective-permute-start.21
  88.9 2.2 %copy-done.3 = f32[1024,1024]{1,0:T(8,128)S(1)} copy-done((f32[1024,1024]{1,0:T(8,128)S(1)}, f32[1024,1024]{1,0:T(8,128)}, u32[]{:S(2)}) %copy-start.3) | copy-done | bytes 4194328
  91.1 16.5 %sweep_middle.3.gram_ref = f32[1024,1024]{1,0:T(8,128)S(1)} custom-call(f32[1024,1024]{1,0:T(8,128)S(1)} %copy-done.3, bf16[32,64,256]{2,1,0:T(8,128)(2,1)S(1)} %maximum_select_fusion.1.refs_1_.refs_0_, bf16[32,64,256]{2,1,0:T(8,128)(2,1)} %collective-permute-done.16.refs_2_.refs_1_, ...), custom_call_target="tpu_custom_call", output_to_operand_aliasing={{}: (0, {})} | custom-call | flops 1048576 | bytes 1048576 | tf_op jit(solution)/shard_map/sweep_middle/pallas_call | solution.py:210
  107.6 0.5 slice.40
  109.4 0.8 slice_select_fusion.3
  110.4 1.9 slice_select_fusion.2
  112.6 17.1 %sweep_last.1.refs_9_.inverse_ref = bf16[2048,1024]{1,0:T(8,128)(2,1)S(1)} custom-call(f32[1024,1024]{1,0:T(8,128)S(1)} %sweep_middle.3.gram_ref, bf16[32,64,256]{2,1,0:T(8,128)(2,1)} %collective-permute-done.14.refs_0_.refs_1_, bf16[32,64,256]{2,1,0:T(8,128)(2,1)S(1)} %collective-permute-done.15.refs_1_.refs_2_), custom_call_target="tpu_custom_call" | custom-call | flops 1048576 | bytes 1048576 | tf_op jit(solution)/shard_map/sweep_last/pallas_call | solution.py:221
  129.7 2.0 copy-done.4
  131.7 13.5 %convolve.2 = (bf16[64,32,2048]{2,1,0:T(8,128)(2,1)}, bf16[64,32,2048]{2,1,0:T(8,128)(2,1)}) custom-call(bf16[32,64,256]{2,1,0:T(8,128)(2,1)S(1)} %maximum_select_fusion.refs_1_.refs_0_, bf16[32,64,256]{2,1,0:T(8,128)(2,1)} %collective-permute-done.16.refs_2_.refs_1_, bf16[32,64,256]{2,1,0:T(8,128)(2,1)} %collective-permute-done.17.refs_3_.refs_2_, ...), custom_call_target="tpu_custom_call" | custom-call | flops 8589934592 | bytes 12582912 | tf_op jit(solution)/shard_map/convolve/pallas_call | solution.py:271
  145.3 13.5 %convolve.3 = (bf16[64,32,2048]{2,1,0:T(8,128)(2,1)}, bf16[64,32,2048]{2,1,0:T(8,128)(2,1)}) custom-call(bf16[32,64,256]{2,1,0:T(8,128)(2,1)S(1)} %maximum_select_fusion.1.refs_1_.refs_0_, bf16[32,64,256]{2,1,0:T(8,128)(2,1)} %collective-permute-done.14.refs_0_.refs_1_, ...), custom_call_target="tpu_custom_call", output_to_operand_aliasing={{0}: (7, {}), {1}: (8, {})} | custom-call | flops 8589934592 | bytes 12582912 | tf_op jit(solution)/shard_map/convolve/pallas_call | solution.py:271
  158.7 6.1 %collective-permute-start.22 = (bf16[64,32,2048]{2,1,0:T(8,128)(2,1)}, bf16[64,32,2048]{2,1,0:T(8,128)(2,1)}, u32[]{:S(2)}, u32[]{:S(2)}) collective-permute-start(bf16[64,32,2048]{2,1,0:T(8,128)(2,1)} %get-tuple-element.12), channel_id=1, source_target_pairs={{0,4},{4,0},{8,12},{12,8},{16,20},{20,16},{24,28},{28,24},{1,5},{5... | collective-permute-start | bytes 25165832 | tf_op jit(solution)/shard_map/ppermute | solution.py:365
  164.8 21.5 %fit.2.refs_0_ = bf16[32,128,1024]{2,1,0:T(8,128)(2,1)} custom-call(s32[1]{0:T(128)} %bitcast.23.at_ref, bf16[64,32,2048]{2,1,0:T(8,128)(2,1)} %get-tuple-element.13.w_ref, bf16[2048,1024]{1,0:T(8,128)(2,1)} %copy-done.4), custom_call_target="tpu_custom_call" | custom-call | flops 12884901888 | bytes 16777216 | tf_op jit(solution)/shard_map/fit/pallas_call | solution.py:319
  186.3 21.5 %fit.3 = bf16[32,128,1024]{2,1,0:T(8,128)(2,1)} custom-call(s32[1]{0:T(128)} %bitcast.at_ref, bf16[64,32,2048]{2,1,0:T(8,128)(2,1)} %collective-permute-done.22.w_ref, bf16[2048,1024]{1,0:T(8,128)(2,1)} %copy-done.4, bf16[32,128,1024]{2,1,0:T(8,128)(2,1)} %fit.2.refs_0_), custom_call_target="tpu_custom_call", output_to_operand_aliasing={{}: (3, {})} | custom-call | flops 12884901888 | bytes 16777216 | tf_op jit(solution)/shard_map/fit/pallas_call | solution.py:319
  (55 shorter events, 1.5 us)
Async XLA Ops:
  0.0 81.9 %copy-start = (f32[256,128]{1,0:T(8,128)S(1)}, f32[256,128]{1,0:T(8,128)}, u32[]{:S(2)}) copy-start(f32[256,128]{1,0:T(8,128)} %param.8) | copy-start | bytes 393220
  4.5 0.7 copy-start.8
  4.5 23.3 %collective-permute-start.7 = (bf16[4,64,8,256]{3,2,1,0:T(8,128)(2,1)}, bf16[4,64,8,256]{3,2,1,0:T(8,128)(2,1)}, u32[]{:S(2)}, u32[]{:S(2)}) collective-permute-start(bf16[4,64,8,256]{3,2,1,0:T(8,128)(2,1)} %get-tuple-element.24), channel_id=1, source_target_pairs={{0,4},{4,0},{8,12},{12,8},{16,20},{20,16},{24,28},{28,24},{1,5},{5... | collective-permute-start | bytes 3145736 | tf_op jit(solution)/shard_map/ppermute | solution.py:365
  13.1 1.2 collective-permute-start
  14.3 9.1 %collective-permute-start.3 = (bf16[16,1024]{1,0:T(8,128)(2,1)S(1)}, bf16[16,1024]{1,0:T(8,128)(2,1)S(1)}, u32[]{:S(2)}, u32[]{:S(2)}) collective-permute-start(bf16[16,1024]{1,0:T(8,128)(2,1)S(1)} %pad_maximum_fusion.1), channel_id=1, source_target_pairs={{0,3},{1,0},{2,1},{3,2},{4,7},{5,4},{6,5},{7,6},{8,11},{9,8},{10,9... | collective-permute-start | bytes 98312 | tf_op jit(solution)/shard_map/ppermute | solution.py:377
  18.8 6.2 %collective-permute-start.2 = (bf16[16,1024]{1,0:T(8,128)(2,1)S(1)}, bf16[16,1024]{1,0:T(8,128)(2,1)S(1)}, u32[]{:S(2)}, u32[]{:S(2)}) collective-permute-start(bf16[16,1024]{1,0:T(8,128)(2,1)S(1)} %pad_maximum_fusion.1), channel_id=1, source_target_pairs={{0,2},{1,3},{2,0},{3,1},{4,6},{5,7},{6,4},{7,5},{8,10},{9,11},{10,... | collective-permute-start | bytes 98312 | tf_op jit(solution)/shard_map/ppermute | solution.py:377
  18.8 4.6 %collective-permute-start.1 = (bf16[16,1024]{1,0:T(8,128)(2,1)S(1)}, bf16[16,1024]{1,0:T(8,128)(2,1)S(1)}, u32[]{:S(2)}, u32[]{:S(2)}) collective-permute-start(bf16[16,1024]{1,0:T(8,128)(2,1)S(1)} %pad_maximum_fusion.1), channel_id=1, source_target_pairs={{0,1},{1,2},{2,3},{3,0},{4,5},{5,6},{6,7},{7,4},{8,9},{9,10},{10,1... | collective-permute-start | bytes 98312 | tf_op jit(solution)/shard_map/ppermute | solution.py:377
  25.1 8.8 %collective-permute-start.6 = (bf16[64,1024]{1,0:T(8,128)(2,1)S(1)}, bf16[64,1024]{1,0:T(8,128)(2,1)S(1)}, u32[]{:S(2)}, u32[]{:S(2)}) collective-permute-start(bf16[64,1024]{1,0:T(8,128)(2,1)S(1)} %get-tuple-element.27), channel_id=1, source_target_pairs={{0,24},{4,28},{8,16},{12,20},{16,8},{20,12},{24,0},{28,4},{1,25},{... | collective-permute-start | bytes 393224 | tf_op jit(solution)/shard_map/ppermute | solution.py:365
  27.4 6.6 %collective-permute-start.5 = (bf16[64,1024]{1,0:T(8,128)(2,1)S(1)}, bf16[64,1024]{1,0:T(8,128)(2,1)S(1)}, u32[]{:S(2)}, u32[]{:S(2)}) collective-permute-start(bf16[64,1024]{1,0:T(8,128)(2,1)S(1)} %get-tuple-element.27), channel_id=1, source_target_pairs={{0,16},{4,20},{8,24},{12,28},{16,0},{20,4},{24,8},{28,12},{1,17},{... | collective-permute-start | bytes 393224 | tf_op jit(solution)/shard_map/ppermute | solution.py:365
  27.6 4.8 %collective-permute-start.4 = (bf16[64,1024]{1,0:T(8,128)(2,1)S(1)}, bf16[64,1024]{1,0:T(8,128)(2,1)S(1)}, u32[]{:S(2)}, u32[]{:S(2)}) collective-permute-start(bf16[64,1024]{1,0:T(8,128)(2,1)S(1)} %get-tuple-element.27), channel_id=1, source_target_pairs={{0,8},{4,12},{8,0},{12,4},{16,24},{20,28},{24,16},{28,20},{1,9},{5... | collective-permute-start | bytes 393224 | tf_op jit(solution)/shard_map/ppermute | solution.py:365
  29.2 24.1 %collective-permute-start.8 = (bf16[32,16,256]{2,1,0:T(8,128)(2,1)S(1)}, bf16[32,16,256]{2,1,0:T(8,128)(2,1)S(1)}, u32[]{:S(2)}, u32[]{:S(2)}) collective-permute-start(bf16[32,16,256]{2,1,0:T(8,128)(2,1)S(1)} %get-tuple-element.17), channel_id=1, source_target_pairs={{0,1},{1,2},{2,3},{3,0},{4,5},{5,6},{6,7},{7,4},{8,9},{9,10},{10,1... | collective-permute-start | bytes 786440 | tf_op jit(solution)/shard_map/ppermute | solution.py:377
  29.3 24.1 %collective-permute-start.9 = (bf16[32,16,256]{2,1,0:T(8,128)(2,1)S(1)}, bf16[32,16,256]{2,1,0:T(8,128)(2,1)S(1)}, u32[]{:S(2)}, u32[]{:S(2)}) collective-permute-start(bf16[32,16,256]{2,1,0:T(8,128)(2,1)S(1)} %get-tuple-element.18), channel_id=1, source_target_pairs={{0,2},{1,3},{2,0},{3,1},{4,6},{5,7},{6,4},{7,5},{8,10},{9,11},{10,... | collective-permute-start | bytes 786440 | tf_op jit(solution)/shard_map/ppermute | solution.py:377
  32.4 21.0 %collective-permute-start.10 = (bf16[32,16,256]{2,1,0:T(8,128)(2,1)S(1)}, bf16[32,16,256]{2,1,0:T(8,128)(2,1)S(1)}, u32[]{:S(2)}, u32[]{:S(2)}) collective-permute-start(bf16[32,16,256]{2,1,0:T(8,128)(2,1)S(1)} %get-tuple-element.19), channel_id=1, source_target_pairs={{0,3},{1,0},{2,1},{3,2},{4,7},{5,4},{6,5},{7,6},{8,11},{9,8},{10,9... | collective-permute-start | bytes 786440 | tf_op jit(solution)/shard_map/ppermute | solution.py:377
  34.0 17.6 %copy-start.5 = (bf16[256,1024]{1,0:T(8,128)(2,1)}, bf16[256,1024]{1,0:T(8,128)(2,1)S(1)}, u32[]{:S(2)}) copy-start(bf16[256,1024]{1,0:T(8,128)(2,1)S(1)} %constant_dynamic-update-slice_fusion.5.values_ref.refs_5_) | copy-start | bytes 1572868
  53.7 30.4 %collective-permute-start.17 = (bf16[32,64,256]{2,1,0:T(8,128)(2,1)S(1)}, bf16[32,64,256]{2,1,0:T(8,128)(2,1)}, u32[]{:S(2)}, u32[]{:S(2)}) collective-permute-start(bf16[32,64,256]{2,1,0:T(8,128)(2,1)S(1)} %maximum_select_fusion.refs_1_.refs_0_), channel_id=1, source_target_pairs={{0,16},{4,20},{8,24},{12,28},{16,0},{20,4},{24,8},{28,12},{1,17},{... | collective-permute-start | bytes 3145736 | tf_op jit(solution)/shard_map/ppermute | solution.py:365
  54.7 26.3 %collective-permute-start.11 = (bf16[32,16,256]{2,1,0:T(8,128)(2,1)S(1)}, bf16[32,16,256]{2,1,0:T(8,128)(2,1)S(1)}, u32[]{:S(2)}, u32[]{:S(2)}) collective-permute-start(bf16[32,16,256]{2,1,0:T(8,128)(2,1)S(1)} %get-tuple-element.20), channel_id=1, source_target_pairs={{0,1},{1,2},{2,3},{3,0},{4,5},{5,6},{6,7},{7,4},{8,9},{9,10},{10,1... | collective-permute-start | bytes 786440 | tf_op jit(solution)/shard_map/ppermute | solution.py:377
  56.3 24.8 %collective-permute-start.12 = (bf16[32,16,256]{2,1,0:T(8,128)(2,1)S(1)}, bf16[32,16,256]{2,1,0:T(8,128)(2,1)S(1)}, u32[]{:S(2)}, u32[]{:S(2)}) collective-permute-start(bf16[32,16,256]{2,1,0:T(8,128)(2,1)S(1)} %get-tuple-element.21), channel_id=1, source_target_pairs={{0,2},{1,3},{2,0},{3,1},{4,6},{5,7},{6,4},{7,5},{8,10},{9,11},{10,... | collective-permute-start | bytes 786440 | tf_op jit(solution)/shard_map/ppermute | solution.py:377
  56.7 24.4 %collective-permute-start.13 = (bf16[32,16,256]{2,1,0:T(8,128)(2,1)S(1)}, bf16[32,16,256]{2,1,0:T(8,128)(2,1)S(1)}, u32[]{:S(2)}, u32[]{:S(2)}) collective-permute-start(bf16[32,16,256]{2,1,0:T(8,128)(2,1)S(1)} %get-tuple-element.22), channel_id=1, source_target_pairs={{0,3},{1,0},{2,1},{3,2},{4,7},{5,4},{6,5},{7,6},{8,11},{9,8},{10,9... | collective-permute-start | bytes 786440 | tf_op jit(solution)/shard_map/ppermute | solution.py:377
  58.5 27.9 %collective-permute-start.16 = (bf16[32,64,256]{2,1,0:T(8,128)(2,1)S(1)}, bf16[32,64,256]{2,1,0:T(8,128)(2,1)}, u32[]{:S(2)}, u32[]{:S(2)}) collective-permute-start(bf16[32,64,256]{2,1,0:T(8,128)(2,1)S(1)} %maximum_select_fusion.refs_1_.refs_0_), channel_id=1, source_target_pairs={{0,8},{4,12},{8,0},{12,4},{16,24},{20,28},{24,16},{28,20},{1,9},{5... | collective-permute-start | bytes 3145736 | tf_op jit(solution)/shard_map/ppermute | solution.py:365
  77.1 4.8 %copy-start.7 = (f32[256,256]{1,0:T(8,128)S(1)}, f32[256,256]{1,0:T(8,128)}, u32[]{:S(2)}) copy-start(f32[256,256]{1,0:T(8,128)} %constant.132.clone) | copy-start | bytes 786436
  77.7 2.0 copy-start.2
  81.4 28.0 %collective-permute-start.15 = (bf16[32,64,256]{2,1,0:T(8,128)(2,1)S(1)}, bf16[32,64,256]{2,1,0:T(8,128)(2,1)S(1)}, u32[]{:S(2)}, u32[]{:S(2)}) collective-permute-start(bf16[32,64,256]{2,1,0:T(8,128)(2,1)S(1)} %maximum_select_fusion.1.refs_1_.refs_0_), channel_id=1, source_target_pairs={{0,16},{4,20},{8,24},{12,28},{16,0},{20,4},{24,8},{28,12},{1,17},{... | collective-permute-start | bytes 3145736 | tf_op jit(solution)/shard_map/ppermute | solution.py:365
  81.6 28.8 %collective-permute-start.14 = (bf16[32,64,256]{2,1,0:T(8,128)(2,1)S(1)}, bf16[32,64,256]{2,1,0:T(8,128)(2,1)}, u32[]{:S(2)}, u32[]{:S(2)}) collective-permute-start(bf16[32,64,256]{2,1,0:T(8,128)(2,1)S(1)} %maximum_select_fusion.1.refs_1_.refs_0_), channel_id=1, source_target_pairs={{0,8},{4,12},{8,0},{12,4},{16,24},{20,28},{24,16},{28,20},{1,9},{5... | collective-permute-start | bytes 3145736 | tf_op jit(solution)/shard_map/ppermute | solution.py:365
  85.1 46.6 %collective-permute-start.20 = (bf16[32,32,256]{2,1,0:T(8,128)(2,1)S(1)}, bf16[32,32,256]{2,1,0:T(8,128)(2,1)S(1)}, u32[]{:S(2)}, u32[]{:S(2)}) collective-permute-start(bf16[32,32,256]{2,1,0:T(8,128)(2,1)S(1)} %slice_select_fusion.1), channel_id=1, source_target_pairs={{0,8},{4,12},{8,0},{12,4},{16,24},{20,28},{24,16},{28,20},{1,9},{5... | collective-permute-start | bytes 1572872 | tf_op jit(solution)/shard_map/ppermute | solution.py:365
  87.6 44.2 %collective-permute-start.21 = (bf16[32,32,256]{2,1,0:T(8,128)(2,1)S(1)}, bf16[32,32,256]{2,1,0:T(8,128)(2,1)S(1)}, u32[]{:S(2)}, u32[]{:S(2)}) collective-permute-start(bf16[32,32,256]{2,1,0:T(8,128)(2,1)S(1)} %slice_select_fusion), channel_id=1, source_target_pairs={{0,16},{4,20},{8,24},{12,28},{16,0},{20,4},{24,8},{28,12},{1,17},{... | collective-permute-start | bytes 1572872 | tf_op jit(solution)/shard_map/ppermute | solution.py:365
  88.9 2.2 %copy-start.3 = (f32[1024,1024]{1,0:T(8,128)S(1)}, f32[1024,1024]{1,0:T(8,128)}, u32[]{:S(2)}) copy-start(f32[1024,1024]{1,0:T(8,128)} %copy-done.2) | copy-start | bytes 12582916
  110.2 35.0 %collective-permute-start.18 = (bf16[32,32,256]{2,1,0:T(8,128)(2,1)}, bf16[32,32,256]{2,1,0:T(8,128)(2,1)S(1)}, u32[]{:S(2)}, u32[]{:S(2)}) collective-permute-start(bf16[32,32,256]{2,1,0:T(8,128)(2,1)} %slice_select_fusion.3), channel_id=1, source_target_pairs={{0,8},{4,12},{8,0},{12,4},{16,24},{20,28},{24,16},{28,20},{1,9},{5... | collective-permute-start | bytes 1572872 | tf_op jit(solution)/shard_map/ppermute | solution.py:365
  112.3 19.4 %copy-start.6 = (bf16[256,1024]{1,0:T(8,128)(2,1)S(1)}, bf16[256,1024]{1,0:T(8,128)(2,1)}, u32[]{:S(2)}) copy-start(bf16[256,1024]{1,0:T(8,128)(2,1)} %copy-done.5) | copy-start | bytes 1572868
  112.3 32.9 %collective-permute-start.19 = (bf16[32,32,256]{2,1,0:T(8,128)(2,1)}, bf16[32,32,256]{2,1,0:T(8,128)(2,1)S(1)}, u32[]{:S(2)}, u32[]{:S(2)}) collective-permute-start(bf16[32,32,256]{2,1,0:T(8,128)(2,1)} %slice_select_fusion.2), channel_id=1, source_target_pairs={{0,16},{4,20},{8,24},{12,28},{16,0},{20,4},{24,8},{28,12},{1,17},{... | collective-permute-start | bytes 1572872 | tf_op jit(solution)/shard_map/ppermute | solution.py:365
  129.7 2.0 copy-start.4
  158.7 27.5 %collective-permute-start.22 = (bf16[64,32,2048]{2,1,0:T(8,128)(2,1)}, bf16[64,32,2048]{2,1,0:T(8,128)(2,1)}, u32[]{:S(2)}, u32[]{:S(2)}) collective-permute-start(bf16[64,32,2048]{2,1,0:T(8,128)(2,1)} %get-tuple-element.12), channel_id=1, source_target_pairs={{0,4},{4,0},{8,12},{12,8},{16,20},{20,16},{24,28},{28,24},{1,5},{5... | collective-permute-start | bytes 25165832 | tf_op jit(solution)/shard_map/ppermute | solution.py:365
  186.3 21.5 %copy-start.1 = (f32[256,128]{1,0:T(8,128)S(1)}, f32[256,128]{1,0:T(8,128)}, u32[]{:S(2)}) copy-start(f32[256,128]{1,0:T(8,128)} %param.8) | copy-start | bytes 393220

commit v3 on v2

--- a/solution.py
+++ b/solution.py
@@ -80,31 +80,32 @@
     def spread(x, row):
         return jnp.broadcast_to(x[row : row + 1, :], (8, n))
 
-    t = [jnp.broadcast_to(a[:8, j : j + 1], (8, n)) for j in range(8)]
     for g in range(n // 8):
         lo = 8 * g
         to = lo + 8
         rows = a[lo:to, :]
         cols = [jnp.broadcast_to(a[:, lo + j : lo + j + 1], (n, n)) for j in range(8)]
+        t = {(i, j): spread(cols[j][lo:to, :], i) for i in range(8) for j in range(i + 1)}
+
+        def at(i, j):
+            return t[max(i, j), min(i, j)]
+
         for k in range(8):
-            scale = 1.0 / spread(t[k], k)
-            here = sub == k
-            new = []
-            for j in range(8):
-                if j == k:
-                    new.append(jnp.where(here, -1.0, t[k]) * scale)
-                else:
-                    kept = jnp.where(here, 0.0, t[j])
-                    new.append(kept - (jnp.where(here, -1.0, t[k]) * spread(t[j], k)) * scale)
-            t = new
-        swept = t
-        if to < n:
-            near = [c[to : to + 8, :] for c in cols]
-            t = []
-            for j in range(8):
-                held = jnp.broadcast_to(a[to : to + 8, to + j : to + j + 1], (8, n))
-                part = total([swept[m] * spread(near[m], j) for m in range(8)])
-                t.append(held + total([near[k] * spread(part, k) for k in range(8)]))
+            scale = 1.0 / t[k, k]
+            old = {i: at(i, k) for i in range(8) if i != k}
+            scaled = {i: old[i] * scale for i in old}
+            for i in old:
+                for j in old:
+                    if j <= i:
+                        t[i, j] = t[i, j] - scaled[i] * old[j]
+                t[max(i, k), min(i, k)] = scaled[i]
+            t[k, k] = -scale
+        swept = []
+        for j in range(8):
+            column = at(0, j)
+            for i in range(1, 8):
+                column = jnp.where(sub == i, at(i, j), column)
+            swept.append(column)
         q = -total([swept[j] * spread(rows, j) for j in range(8)])
         for j in range(8):
             q = jnp.where(lane == lo + j, swept[j], q)
@@ -230,13 +231,14 @@
     )(gram, *after)
 
 
-def column_kernel(*refs, pieces):
+def column_kernel(*refs, pieces, step):
     fields = refs[:pieces]
     values_ref, lags_ref, own_ref, other_ref = refs[pieces], refs[pieces + 1], refs[-2], refs[-1]
-    step, slab, _ = own_ref.shape
-    n = values_ref.shape[1]
+    tiles = own_ref.shape[0]
+    slab = own_ref.shape[2] // 16
     planes = lags_ref.shape[2]
-    first = pl.program_id(0) * step
+    inner = pl.program_id(1) * step
+    first = pl.program_id(0) * 16 + inner
     turned = [jnp.concatenate([f[i] for f in fields], axis=0).T for i in range(step)]
     sums = jnp.dot(
         jnp.concatenate(turned, axis=0), values_ref[...], preferred_element_type=F32
@@ -254,11 +256,12 @@
             jnp.concatenate([high, low], axis=0),
             preferred_element_type=F32,
         )
-        w_high, w_low = split(both[: 2 * slab] + both[2 * slab :])
-        own_ref[i, :, :n] = w_high[:slab]
-        own_ref[i, :, n:] = w_low[:slab]
-        other_ref[i, :, :n] = w_high[slab:]
-        other_ref[i, :, n:] = w_low[slab:]
+        w = both[: 2 * slab] + both[2 * slab :]
+        rows = pl.ds(inner + i, slab, stride=16)
+        for t in range(tiles):
+            lanes = slice(t * 128, (t + 1) * 128)
+            own_ref[t, 0, rows, :] = w[:slab, lanes]
+            other_ref[t, 0, rows, :] = w[slab:, lanes]
 
 
 def convolve(pieces, values, lags, slab, start, state, after):
@@ -266,16 +269,21 @@
     all_cols = lags.shape[1]
     bands, n = values.shape
     step = 4
-    shape = jax.ShapeDtypeStruct((all_cols, slab, 2 * n), BF16)
-    out_spec = pl.BlockSpec((step, slab, 2 * n), lambda j: (j + start // step, 0, 0))
+    inner = 16 // step
+    tiles = n // 128
+    shape = jax.ShapeDtypeStruct((tiles, all_cols // 16, slab * 16, 128), F32)
+    out_spec = pl.BlockSpec((tiles, 1, slab * 16, 128), lambda j, i: (0, j + start // 16, 0, 0))
     return pl.pallas_call(
-        functools.partial(column_kernel, pieces=len(pieces)),
-        grid=(cols // step,),
+        functools.partial(column_kernel, pieces=len(pieces), step=step),
+        grid=(cols // 16, inner),
         out_shape=(shape, shape),
-        in_specs=[pl.BlockSpec((step, p.shape[1], planes), lambda j: (j, 0, 0)) for p in pieces]
+        in_specs=[
+            pl.BlockSpec((step, p.shape[1], planes), lambda j, i: (j * inner + i, 0, 0))
+            for p in pieces
+        ]
         + [
-            pl.BlockSpec((bands, n), lambda j: (0, 0)),
-            pl.BlockSpec((2, cols, planes), lambda j: (0, start // cols, 0)),
+            pl.BlockSpec((bands, n), lambda j, i: (0, 0)),
+            pl.BlockSpec((2, cols, planes), lambda j, i: (0, start // cols, 0)),
         ]
         + [pl.BlockSpec(memory_space=pl.ANY)] * (len(state) + len(after)),
         out_specs=(out_spec, out_spec),
@@ -291,10 +299,9 @@
 
 
 def fit_kernel(at_ref, w_ref, inverse_ref, *refs):
-    out_ref, turn = refs[-2:]
+    out_ref = refs[-1]
     slab, cols, n = out_ref.shape
-    w = w_ref[...].reshape(cols * slab, 2 * n)
-    w_high, w_low = w[:, :n], w[:, n:]
+    w_high, w_low = split(jnp.concatenate([w_ref[t, 0] for t in range(n // 128)], axis=1))
     tile = 256
     for first in range(0, n, tile):
         lanes = slice(first, first + tile)
@@ -302,39 +309,32 @@
         out = jnp.dot(w_high, high, preferred_element_type=F32)
         out = out + jnp.dot(w_high, inverse_ref[n:, lanes], preferred_element_type=F32)
         out = out + jnp.dot(w_low, high, preferred_element_type=F32)
-        for t in range(tile // 128):
-            at = first // 128 + t
-            part = slice(t * 128, (t + 1) * 128)
-            for c in range(cols):
-                turn[at, pl.ds(c, slab, stride=cols), :] = out[c * slab : (c + 1) * slab, part]
-            out_ref[:, :, at * 128 : (at + 1) * 128] = (
-                turn[at].reshape(slab, cols, 128).astype(out_ref.dtype)
-            )
+        out_ref[:, :, lanes] = out.reshape(slab, cols, tile).astype(out_ref.dtype)
 
 
 def fit(at, w, inverse, width, state):
-    cols, slab, n2 = w.shape
-    n = n2 // 2
+    tiles, blocks, rows, _ = w.shape
+    n = tiles * 128
     step = 16
+    slab = rows // step
     return pl.pallas_call(
         fit_kernel,
         grid_spec=pltpu.PrefetchScalarGridSpec(
             num_scalar_prefetch=1,
-            grid=(cols // step,),
+            grid=(blocks,),
             in_specs=[
-                pl.BlockSpec((step, slab, n2), lambda j, at: (j, 0, 0)),
+                pl.BlockSpec((tiles, 1, rows, 128), lambda j, at: (0, j, 0, 0)),
                 pl.BlockSpec((2 * n, n), lambda j, at: (0, 0)),
             ]
             + [pl.BlockSpec(memory_space=pl.ANY)] * len(state),
             out_specs=pl.BlockSpec((slab, step, n), lambda j, at: (0, j + at[0], 0)),
-            scratch_shapes=[pltpu.VMEM((n // 128, slab * step, 128), F32)],
         ),
         out_shape=jax.ShapeDtypeStruct((slab, width, n), BF16),
         input_output_aliases={3: 0} if state else {},
         compiler_params=pltpu.CompilerParams(vmem_limit_bytes=56 * MIB),
         cost_estimate=pl.CostEstimate(
-            flops=6 * cols * slab * n * n,
-            bytes_accessed=6 * cols * slab * n + 4 * n * n,
+            flops=6 * blocks * rows * n * n,
+            bytes_accessed=6 * blocks * rows * n + 4 * n * n,
             transcendentals=0,
         ),
         name="fit",

time: 211 us -> 221 us (1.047)
  Pallas kernels: 145 us -> 155 us
    pallas_call x2, Pallas kernels: 43 us -> 35.1 us  [fit(): pl.pallas_call(fit_kernel, grid_spec=pltpu.PrefetchScalarGridSpec(num_sca...]
    pallas_call x2, Pallas kernels: 27 us -> 34.6 us  [convolve(): pl.pallas_call(functools.partial(column_kernel, pieces=len(pieces), step=...]
    pallas_call x2, Pallas kernels: 32.8 us -> 37.6 us  [sweep_gram(): pl.pallas_call(functools.partial(middle_kernel, step=step, **options), ou...]
    pallas_call x1, Pallas kernels: 17.6 us -> 20 us  [sweep_gram(): pl.pallas_call(functools.partial(first_kernel, **options), out_shape=stat...]
    pallas_call x1, Pallas kernels: 17.1 us -> 19.6 us  [sweep_gram(): pl.pallas_call(functools.partial(last_kernel, step=step, **options), out_...]
  transfers between devices with their start and end apart: 23 -> 23, of which waited for: 3 -> 3; matrix products, arithmetic and copies ran while one was open for 6% -> 6% of each run, Pallas kernels for 53% -> 55%
where the time goes in v3:
time: 221 us; the launch traced here: 218 us
  Pallas kernels  155 us (70%)
  starting transfers between devices  26.2 us (12%)
  local copies, waits for them, and re-layouts  13.2 us (6%)
  other arithmetic  9.16 us (4%)
  waiting for transfers between devices  7.31 us (3%)
  between operations  5.91 us (3%)
    pallas_call x2, Pallas kernels, sweep_gram(): pl.pallas_call(functools.partial(middle_kernel, step=step, **options), ou...  37.6 us
    pallas_call x2, Pallas kernels, fit(): pl.pallas_call(fit_kernel, grid_spec=pltpu.PrefetchScalarGridSpec(num_sca...  35.1 us
    pallas_call x2, Pallas kernels, convolve(): pl.pallas_call(functools.partial(column_kernel, pieces=len(pieces), step=...  34.6 us
    pallas_call x1, Pallas kernels, sweep_gram(): pl.pallas_call(functools.partial(first_kernel, **options), out_shape=stat...  20 us
    pallas_call x1, Pallas kernels, sweep_gram(): pl.pallas_call(functools.partial(last_kernel, step=step, **options), out_...  19.6 us
    ppermute x14, starting transfers between devices, hop(): return lax.ppermute(array, 'gz', [(z, z ^ bit) for z in range(gz_count)])  15.4 us
    ppermute x9, starting transfers between devices, gy_shift(): lax.ppermute(array, 'gy', [(y, (y + by) % gy_count) for y in range(gy_cou...  10.9 us
    unnamed x25, local copies, waits for them, and re-layouts  9.95 us
  transfers between devices with their start and end apart: 23, of which 3 were waited for; matrix products, arithmetic and copies ran while one was open for 6% of the time, Pallas kernels for 55%

profile of v3, /device:TPU:1, one launch (start us, length us, event | category | flops | bytes accessed | tf_op | source)
XLA Modules:
  0.0 217.6 jit_solution(11705316618797601994)
XLA Ops:
  0.0 3.4 %copy.10 = bf16[8,256,512]{1,0,2:T(8,128)(2,1)S(1)} copy(bf16[8,256,512]{2,1,0:T(8,128)(2,1)} %param.6) | data formatting | bytes 4194304 | tf_op args[0]
  3.4 1.1 dynamic-slice_bitcast_fusion.1
  4.6 0.3 bitcast_convert_fusion.field_ref
  4.9 0.3 copy-done.8
  5.2 7.8 %take_points.1 = f32[8,1024]{1,0:T(8,128)S(1)} custom-call(s32[3,1024]{1,0:T(4,128)S(1)} %pad_add_fusion.where_ref, f32[512,8,256]{2,1,0:T(8,128)S(1)} %bitcast_convert_fusion.field_ref), custom_call_target="tpu_custom_call" | custom-call | tf_op jit(solution)/shard_map/take_points/pallas_call | solution.py:55
  13.3 1.0 collective-permute-done
  14.3 4.5 %collective-permute-start.3 = (bf16[16,1024]{1,0:T(8,128)(2,1)S(1)}, bf16[16,1024]{1,0:T(8,128)(2,1)S(1)}, u32[]{:S(2)}, u32[]{:S(2)}) collective-permute-start(bf16[16,1024]{1,0:T(8,128)(2,1)S(1)} %pad_maximum_fusion.1), channel_id=1, source_target_pairs={{0,3},{1,0},{2,1},{3,2},{4,7},{5,4},{6,5},{7,6},{8,11},{9,8},{10,9... | collective-permute-start | bytes 98312 | tf_op jit(solution)/shard_map/ppermute | solution.py:377
  18.8 0.5 collective-permute-start.1
  19.3 4.1 %collective-permute-done.1 = bf16[16,1024]{1,0:T(8,128)(2,1)S(1)} collective-permute-done((bf16[16,1024]{1,0:T(8,128)(2,1)S(1)}, bf16[16,1024]{1,0:T(8,128)(2,1)S(1)}, u32[]{:S(2)}, u32[]{:S(2)}) %collective-permute-start.1) | collective-permute-done | bytes 32800 | tf_op jit(solution)/shard_map/ppermute | solution.py:377
  23.4 0.5 slice.38
  25.1 2.2 %collective-permute-start.6 = (bf16[64,1024]{1,0:T(8,128)(2,1)S(1)}, bf16[64,1024]{1,0:T(8,128)(2,1)S(1)}, u32[]{:S(2)}, u32[]{:S(2)}) collective-permute-start(bf16[64,1024]{1,0:T(8,128)(2,1)S(1)} %get-tuple-element.27), channel_id=1, source_target_pairs={{0,24},{4,28},{8,16},{12,20},{16,8},{20,12},{24,0},{28,4},{1,25},{... | collective-permute-start | bytes 393224 | tf_op jit(solution)/shard_map/ppermute | solution.py:365
  27.8 1.4 fusion.14
  29.3 0.9 collective-permute-start.9
  30.2 2.1 collective-permute-done.4
  32.4 1.2 collective-permute-start.10
  33.7 20.0 %sweep_first.1.refs_0_ = f32[1024,1024]{1,0:T(8,128)S(1)} custom-call(bf16[256,1024]{1,0:T(8,128)(2,1)S(1)} %constant_dynamic-update-slice_fusion.5.values_ref.refs_5_), custom_call_target="tpu_custom_call" | custom-call | flops 1048576 | bytes 1048576 | tf_op jit(solution)/shard_map/sweep_first/pallas_call | solution.py:199
  53.7 0.5 slice.37
  55.8 1.1 collective-permute-start.17
  56.9 1.1 collective-permute-start.11
  58.1 0.8 collective-permute-start.12
  58.9 1.7 collective-permute-start.13
  60.6 1.2 collective-permute-start.16
  61.8 0.9 fusion.10
  62.7 18.8 %sweep_middle.2.refs_0_ = f32[1024,1024]{1,0:T(8,128)S(1)} custom-call(f32[1024,1024]{1,0:T(8,128)S(1)} %sweep_first.1.refs_0_, bf16[32,64,256]{2,1,0:T(8,128)(2,1)S(1)} %maximum_select_fusion.refs_1_.refs_0_), custom_call_target="tpu_custom_call", output_to_operand_aliasing={{}: (0, {})} | custom-call | flops 1048576 | bytes 1048576 | tf_op jit(solution)/shard_map/sweep_middle/pallas_call | solution.py:211
  81.6 0.6 slice.39
  82.2 2.0 copy-done.2
  85.8 0.4 collective-permute-start.15
  86.3 0.4 collective-permute-start.14
  86.7 1.1 fusion.16
  87.7 1.1 fusion.21
  88.8 1.1 slice_select_fusion.1
  89.9 1.2 collective-permute-start.20
  91.1 1.1 slice_select_fusion
  92.2 1.1 collective-permute-start.21
  93.3 2.2 %copy-done.3 = f32[1024,1024]{1,0:T(8,128)S(1)} copy-done((f32[1024,1024]{1,0:T(8,128)S(1)}, f32[1024,1024]{1,0:T(8,128)}, u32[]{:S(2)}) %copy-start.3) | copy-done | bytes 4194328
  95.5 18.7 %sweep_middle.3.gram_ref = f32[1024,1024]{1,0:T(8,128)S(1)} custom-call(f32[1024,1024]{1,0:T(8,128)S(1)} %copy-done.3, bf16[32,64,256]{2,1,0:T(8,128)(2,1)S(1)} %maximum_select_fusion.1.refs_1_.refs_0_, bf16[32,64,256]{2,1,0:T(8,128)(2,1)} %collective-permute-done.16.refs_2_.refs_1_, ...), custom_call_target="tpu_custom_call", output_to_operand_aliasing={{}: (0, {})} | custom-call | flops 1048576 | bytes 1048576 | tf_op jit(solution)/shard_map/sweep_middle/pallas_call | solution.py:211
  114.3 0.5 slice.40
  116.1 0.8 slice_select_fusion.3
  116.9 0.3 collective-permute-start.18
  117.3 1.9 slice_select_fusion.2
  119.1 0.4 collective-permute-start.19
  119.6 19.6 %sweep_last.1.refs_9_.inverse_ref = bf16[2048,1024]{1,0:T(8,128)(2,1)S(1)} custom-call(f32[1024,1024]{1,0:T(8,128)S(1)} %sweep_middle.3.gram_ref, bf16[32,64,256]{2,1,0:T(8,128)(2,1)} %collective-permute-done.14.refs_0_.refs_1_, bf16[32,64,256]{2,1,0:T(8,128)(2,1)S(1)} %collective-permute-done.15.refs_1_.refs_2_), custom_call_target="tpu_custom_call" | custom-call | flops 1048576 | bytes 1048576 | tf_op jit(solution)/shard_map/sweep_last/pallas_call | solution.py:222
  139.2 2.0 copy-done.4
  141.2 17.4 %convolve.2 = (f32[8,4,512,128]{3,2,1,0:T(8,128)}, f32[8,4,512,128]{3,2,1,0:T(8,128)}) custom-call(bf16[32,64,256]{2,1,0:T(8,128)(2,1)S(1)} %maximum_select_fusion.refs_1_.refs_0_, bf16[32,64,256]{2,1,0:T(8,128)(2,1)} %collective-permute-done.16.refs_2_.refs_1_, bf16[32,64,256]{2,1,0:T(8,128)(2,1)} %collective-permute-done.17.refs_3_.refs_2_, ...), custom_call_target="tpu_custom_call" | custom-call | flops 8589934592 | bytes 12582912 | tf_op jit(solution)/shard_map/convolve/pallas_call | solution.py:276
  158.6 17.2 %convolve.3 = (f32[8,4,512,128]{3,2,1,0:T(8,128)}, f32[8,4,512,128]{3,2,1,0:T(8,128)}) custom-call(bf16[32,64,256]{2,1,0:T(8,128)(2,1)S(1)} %maximum_select_fusion.1.refs_1_.refs_0_, bf16[32,64,256]{2,1,0:T(8,128)(2,1)} %collective-permute-done.14.refs_0_.refs_1_, ...), custom_call_target="tpu_custom_call", output_to_operand_aliasing={{0}: (7, {}), {1}: (8, {})} | custom-call | flops 8589934592 | bytes 12582912 | tf_op jit(solution)/shard_map/convolve/pallas_call | solution.py:276
  175.9 6.2 %collective-permute-start.22 = (f32[8,4,512,128]{3,2,1,0:T(8,128)}, f32[8,4,512,128]{3,2,1,0:T(8,128)}, u32[]{:S(2)}, u32[]{:S(2)}) collective-permute-start(f32[8,4,512,128]{3,2,1,0:T(8,128)} %get-tuple-element.12), channel_id=1, source_target_pairs={{0,4},{4,0},{8,12},{12,8},{16,20},{20,16},{24,28},{28,24},{1,5},{5... | collective-permute-start | bytes 25165832 | tf_op jit(solution)/shard_map/ppermute | solution.py:365
  182.1 17.5 %fit.2.refs_0_ = bf16[32,128,1024]{2,1,0:T(8,128)(2,1)} custom-call(s32[1]{0:T(128)} %bitcast.23.at_ref, f32[8,4,512,128]{3,2,1,0:T(8,128)} %get-tuple-element.13.w_ref, bf16[2048,1024]{1,0:T(8,128)(2,1)} %copy-done.4), custom_call_target="tpu_custom_call" | custom-call | flops 12884901888 | bytes 16777216 | tf_op jit(solution)/shard_map/fit/pallas_call | solution.py:320
  199.6 17.6 %fit.3 = bf16[32,128,1024]{2,1,0:T(8,128)(2,1)} custom-call(s32[1]{0:T(128)} %bitcast.at_ref, f32[8,4,512,128]{3,2,1,0:T(8,128)} %collective-permute-done.22.w_ref, bf16[2048,1024]{1,0:T(8,128)(2,1)} %copy-done.4, bf16[32,128,1024]{2,1,0:T(8,128)(2,1)} %fit.2.refs_0_), custom_call_target="tpu_custom_call", output_to_operand_aliasing={{}: (3, {})} | custom-call | flops 12884901888 | bytes 16777216 | tf_op jit(solution)/shard_map/fit/pallas_call | solution.py:320
  (55 shorter events, 1.5 us)
Async XLA Ops:
  0.0 86.7 %copy-start = (f32[256,128]{1,0:T(8,128)S(1)}, f32[256,128]{1,0:T(8,128)}, u32[]{:S(2)}) copy-start(f32[256,128]{1,0:T(8,128)} %param.8) | copy-start | bytes 393220
  4.5 0.7 copy-start.8
  4.5 23.3 %collective-permute-start.7 = (bf16[4,64,8,256]{3,2,1,0:T(8,128)(2,1)}, bf16[4,64,8,256]{3,2,1,0:T(8,128)(2,1)}, u32[]{:S(2)}, u32[]{:S(2)}) collective-permute-start(bf16[4,64,8,256]{3,2,1,0:T(8,128)(2,1)} %get-tuple-element.24), channel_id=1, source_target_pairs={{0,4},{4,0},{8,12},{12,8},{16,20},{20,16},{24,28},{28,24},{1,5},{5... | collective-permute-start | bytes 3145736 | tf_op jit(solution)/shard_map/ppermute | solution.py:365
  13.1 1.2 collective-permute-start
  14.3 9.1 %collective-permute-start.3 = (bf16[16,1024]{1,0:T(8,128)(2,1)S(1)}, bf16[16,1024]{1,0:T(8,128)(2,1)S(1)}, u32[]{:S(2)}, u32[]{:S(2)}) collective-permute-start(bf16[16,1024]{1,0:T(8,128)(2,1)S(1)} %pad_maximum_fusion.1), channel_id=1, source_target_pairs={{0,3},{1,0},{2,1},{3,2},{4,7},{5,4},{6,5},{7,6},{8,11},{9,8},{10,9... | collective-permute-start | bytes 98312 | tf_op jit(solution)/shard_map/ppermute | solution.py:377
  18.8 6.2 %collective-permute-start.2 = (bf16[16,1024]{1,0:T(8,128)(2,1)S(1)}, bf16[16,1024]{1,0:T(8,128)(2,1)S(1)}, u32[]{:S(2)}, u32[]{:S(2)}) collective-permute-start(bf16[16,1024]{1,0:T(8,128)(2,1)S(1)} %pad_maximum_fusion.1), channel_id=1, source_target_pairs={{0,2},{1,3},{2,0},{3,1},{4,6},{5,7},{6,4},{7,5},{8,10},{9,11},{10,... | collective-permute-start | bytes 98312 | tf_op jit(solution)/shard_map/ppermute | solution.py:377
  18.8 4.6 %collective-permute-start.1 = (bf16[16,1024]{1,0:T(8,128)(2,1)S(1)}, bf16[16,1024]{1,0:T(8,128)(2,1)S(1)}, u32[]{:S(2)}, u32[]{:S(2)}) collective-permute-start(bf16[16,1024]{1,0:T(8,128)(2,1)S(1)} %pad_maximum_fusion.1), channel_id=1, source_target_pairs={{0,1},{1,2},{2,3},{3,0},{4,5},{5,6},{6,7},{7,4},{8,9},{9,10},{10,1... | collective-permute-start | bytes 98312 | tf_op jit(solution)/shard_map/ppermute | solution.py:377
  25.1 8.5 %collective-permute-start.6 = (bf16[64,1024]{1,0:T(8,128)(2,1)S(1)}, bf16[64,1024]{1,0:T(8,128)(2,1)S(1)}, u32[]{:S(2)}, u32[]{:S(2)}) collective-permute-start(bf16[64,1024]{1,0:T(8,128)(2,1)S(1)} %get-tuple-element.27), channel_id=1, source_target_pairs={{0,24},{4,28},{8,16},{12,20},{16,8},{20,12},{24,0},{28,4},{1,25},{... | collective-permute-start | bytes 393224 | tf_op jit(solution)/shard_map/ppermute | solution.py:365
  27.4 6.3 %collective-permute-start.5 = (bf16[64,1024]{1,0:T(8,128)(2,1)S(1)}, bf16[64,1024]{1,0:T(8,128)(2,1)S(1)}, u32[]{:S(2)}, u32[]{:S(2)}) collective-permute-start(bf16[64,1024]{1,0:T(8,128)(2,1)S(1)} %get-tuple-element.27), channel_id=1, source_target_pairs={{0,16},{4,20},{8,24},{12,28},{16,0},{20,4},{24,8},{28,12},{1,17},{... | collective-permute-start | bytes 393224 | tf_op jit(solution)/shard_map/ppermute | solution.py:365
  27.6 4.8 %collective-permute-start.4 = (bf16[64,1024]{1,0:T(8,128)(2,1)S(1)}, bf16[64,1024]{1,0:T(8,128)(2,1)S(1)}, u32[]{:S(2)}, u32[]{:S(2)}) collective-permute-start(bf16[64,1024]{1,0:T(8,128)(2,1)S(1)} %get-tuple-element.27), channel_id=1, source_target_pairs={{0,8},{4,12},{8,0},{12,4},{16,24},{20,28},{24,16},{28,20},{1,9},{5... | collective-permute-start | bytes 393224 | tf_op jit(solution)/shard_map/ppermute | solution.py:365
  29.2 26.3 %collective-permute-start.8 = (bf16[32,16,256]{2,1,0:T(8,128)(2,1)S(1)}, bf16[32,16,256]{2,1,0:T(8,128)(2,1)S(1)}, u32[]{:S(2)}, u32[]{:S(2)}) collective-permute-start(bf16[32,16,256]{2,1,0:T(8,128)(2,1)S(1)} %get-tuple-element.17), channel_id=1, source_target_pairs={{0,1},{1,2},{2,3},{3,0},{4,5},{5,6},{6,7},{7,4},{8,9},{9,10},{10,1... | collective-permute-start | bytes 786440 | tf_op jit(solution)/shard_map/ppermute | solution.py:377
  29.3 26.3 %collective-permute-start.9 = (bf16[32,16,256]{2,1,0:T(8,128)(2,1)S(1)}, bf16[32,16,256]{2,1,0:T(8,128)(2,1)S(1)}, u32[]{:S(2)}, u32[]{:S(2)}) collective-permute-start(bf16[32,16,256]{2,1,0:T(8,128)(2,1)S(1)} %get-tuple-element.18), channel_id=1, source_target_pairs={{0,2},{1,3},{2,0},{3,1},{4,6},{5,7},{6,4},{7,5},{8,10},{9,11},{10,... | collective-permute-start | bytes 786440 | tf_op jit(solution)/shard_map/ppermute | solution.py:377
  32.4 23.2 %collective-permute-start.10 = (bf16[32,16,256]{2,1,0:T(8,128)(2,1)S(1)}, bf16[32,16,256]{2,1,0:T(8,128)(2,1)S(1)}, u32[]{:S(2)}, u32[]{:S(2)}) collective-permute-start(bf16[32,16,256]{2,1,0:T(8,128)(2,1)S(1)} %get-tuple-element.19), channel_id=1, source_target_pairs={{0,3},{1,0},{2,1},{3,2},{4,7},{5,4},{6,5},{7,6},{8,11},{9,8},{10,9... | collective-permute-start | bytes 786440 | tf_op jit(solution)/shard_map/ppermute | solution.py:377
  33.7 20.1 %copy-start.5 = (bf16[256,1024]{1,0:T(8,128)(2,1)}, bf16[256,1024]{1,0:T(8,128)(2,1)S(1)}, u32[]{:S(2)}) copy-start(bf16[256,1024]{1,0:T(8,128)(2,1)S(1)} %constant_dynamic-update-slice_fusion.5.values_ref.refs_5_) | copy-start | bytes 1572868
  55.8 33.0 %collective-permute-start.17 = (bf16[32,64,256]{2,1,0:T(8,128)(2,1)S(1)}, bf16[32,64,256]{2,1,0:T(8,128)(2,1)}, u32[]{:S(2)}, u32[]{:S(2)}) collective-permute-start(bf16[32,64,256]{2,1,0:T(8,128)(2,1)S(1)} %maximum_select_fusion.refs_1_.refs_0_), channel_id=1, source_target_pairs={{0,16},{4,20},{8,24},{12,28},{16,0},{20,4},{24,8},{28,12},{1,17},{... | collective-permute-start | bytes 3145736 | tf_op jit(solution)/shard_map/ppermute | solution.py:365
  56.9 28.6 %collective-permute-start.11 = (bf16[32,16,256]{2,1,0:T(8,128)(2,1)S(1)}, bf16[32,16,256]{2,1,0:T(8,128)(2,1)S(1)}, u32[]{:S(2)}, u32[]{:S(2)}) collective-permute-start(bf16[32,16,256]{2,1,0:T(8,128)(2,1)S(1)} %get-tuple-element.20), channel_id=1, source_target_pairs={{0,1},{1,2},{2,3},{3,0},{4,5},{5,6},{6,7},{7,4},{8,9},{9,10},{10,1... | collective-permute-start | bytes 786440 | tf_op jit(solution)/shard_map/ppermute | solution.py:377
  58.1 27.5 %collective-permute-start.12 = (bf16[32,16,256]{2,1,0:T(8,128)(2,1)S(1)}, bf16[32,16,256]{2,1,0:T(8,128)(2,1)S(1)}, u32[]{:S(2)}, u32[]{:S(2)}) collective-permute-start(bf16[32,16,256]{2,1,0:T(8,128)(2,1)S(1)} %get-tuple-element.21), channel_id=1, source_target_pairs={{0,2},{1,3},{2,0},{3,1},{4,6},{5,7},{6,4},{7,5},{8,10},{9,11},{10,... | collective-permute-start | bytes 786440 | tf_op jit(solution)/shard_map/ppermute | solution.py:377
  58.9 26.7 %collective-permute-start.13 = (bf16[32,16,256]{2,1,0:T(8,128)(2,1)S(1)}, bf16[32,16,256]{2,1,0:T(8,128)(2,1)S(1)}, u32[]{:S(2)}, u32[]{:S(2)}) collective-permute-start(bf16[32,16,256]{2,1,0:T(8,128)(2,1)S(1)} %get-tuple-element.22), channel_id=1, source_target_pairs={{0,3},{1,0},{2,1},{3,2},{4,7},{5,4},{6,5},{7,6},{8,11},{9,8},{10,9... | collective-permute-start | bytes 786440 | tf_op jit(solution)/shard_map/ppermute | solution.py:377
  60.6 30.5 %collective-permute-start.16 = (bf16[32,64,256]{2,1,0:T(8,128)(2,1)S(1)}, bf16[32,64,256]{2,1,0:T(8,128)(2,1)}, u32[]{:S(2)}, u32[]{:S(2)}) collective-permute-start(bf16[32,64,256]{2,1,0:T(8,128)(2,1)S(1)} %maximum_select_fusion.refs_1_.refs_0_), channel_id=1, source_target_pairs={{0,8},{4,12},{8,0},{12,4},{16,24},{20,28},{24,16},{28,20},{1,9},{5... | collective-permute-start | bytes 3145736 | tf_op jit(solution)/shard_map/ppermute | solution.py:365
  81.5 5.1 %copy-start.7 = (f32[256,256]{1,0:T(8,128)S(1)}, f32[256,256]{1,0:T(8,128)}, u32[]{:S(2)}) copy-start(f32[256,256]{1,0:T(8,128)} %constant.132.clone) | copy-start | bytes 786436
  82.2 2.0 copy-start.2
  85.8 30.3 %collective-permute-start.15 = (bf16[32,64,256]{2,1,0:T(8,128)(2,1)S(1)}, bf16[32,64,256]{2,1,0:T(8,128)(2,1)S(1)}, u32[]{:S(2)}, u32[]{:S(2)}) collective-permute-start(bf16[32,64,256]{2,1,0:T(8,128)(2,1)S(1)} %maximum_select_fusion.1.refs_1_.refs_0_), channel_id=1, source_target_pairs={{0,16},{4,20},{8,24},{12,28},{16,0},{20,4},{24,8},{28,12},{1,17},{... | collective-permute-start | bytes 3145736 | tf_op jit(solution)/shard_map/ppermute | solution.py:365
  86.3 31.0 %collective-permute-start.14 = (bf16[32,64,256]{2,1,0:T(8,128)(2,1)S(1)}, bf16[32,64,256]{2,1,0:T(8,128)(2,1)}, u32[]{:S(2)}, u32[]{:S(2)}) collective-permute-start(bf16[32,64,256]{2,1,0:T(8,128)(2,1)S(1)} %maximum_select_fusion.1.refs_1_.refs_0_), channel_id=1, source_target_pairs={{0,8},{4,12},{8,0},{12,4},{16,24},{20,28},{24,16},{28,20},{1,9},{5... | collective-permute-start | bytes 3145736 | tf_op jit(solution)/shard_map/ppermute | solution.py:365
  89.9 51.3 %collective-permute-start.20 = (bf16[32,32,256]{2,1,0:T(8,128)(2,1)S(1)}, bf16[32,32,256]{2,1,0:T(8,128)(2,1)S(1)}, u32[]{:S(2)}, u32[]{:S(2)}) collective-permute-start(bf16[32,32,256]{2,1,0:T(8,128)(2,1)S(1)} %slice_select_fusion.1), channel_id=1, source_target_pairs={{0,8},{4,12},{8,0},{12,4},{16,24},{20,28},{24,16},{28,20},{1,9},{5... | collective-permute-start | bytes 1572872 | tf_op jit(solution)/shard_map/ppermute | solution.py:365
  92.2 49.0 %collective-permute-start.21 = (bf16[32,32,256]{2,1,0:T(8,128)(2,1)S(1)}, bf16[32,32,256]{2,1,0:T(8,128)(2,1)S(1)}, u32[]{:S(2)}, u32[]{:S(2)}) collective-permute-start(bf16[32,32,256]{2,1,0:T(8,128)(2,1)S(1)} %slice_select_fusion), channel_id=1, source_target_pairs={{0,16},{4,20},{8,24},{12,28},{16,0},{20,4},{24,8},{28,12},{1,17},{... | collective-permute-start | bytes 1572872 | tf_op jit(solution)/shard_map/ppermute | solution.py:365
  93.3 2.2 %copy-start.3 = (f32[1024,1024]{1,0:T(8,128)S(1)}, f32[1024,1024]{1,0:T(8,128)}, u32[]{:S(2)}) copy-start(f32[1024,1024]{1,0:T(8,128)} %copy-done.2) | copy-start | bytes 12582916
  116.9 41.7 %collective-permute-start.18 = (bf16[32,32,256]{2,1,0:T(8,128)(2,1)}, bf16[32,32,256]{2,1,0:T(8,128)(2,1)S(1)}, u32[]{:S(2)}, u32[]{:S(2)}) collective-permute-start(bf16[32,32,256]{2,1,0:T(8,128)(2,1)} %slice_select_fusion.3), channel_id=1, source_target_pairs={{0,8},{4,12},{8,0},{12,4},{16,24},{20,28},{24,16},{28,20},{1,9},{5... | collective-permute-start | bytes 1572872 | tf_op jit(solution)/shard_map/ppermute | solution.py:365
  119.1 22.1 %copy-start.6 = (bf16[256,1024]{1,0:T(8,128)(2,1)S(1)}, bf16[256,1024]{1,0:T(8,128)(2,1)}, u32[]{:S(2)}) copy-start(bf16[256,1024]{1,0:T(8,128)(2,1)} %copy-done.5) | copy-start | bytes 1572868
  119.1 39.5 %collective-permute-start.19 = (bf16[32,32,256]{2,1,0:T(8,128)(2,1)}, bf16[32,32,256]{2,1,0:T(8,128)(2,1)S(1)}, u32[]{:S(2)}, u32[]{:S(2)}) collective-permute-start(bf16[32,32,256]{2,1,0:T(8,128)(2,1)} %slice_select_fusion.2), channel_id=1, source_target_pairs={{0,16},{4,20},{8,24},{12,28},{16,0},{20,4},{24,8},{28,12},{1,17},{... | collective-permute-start | bytes 1572872 | tf_op jit(solution)/shard_map/ppermute | solution.py:365
  139.2 2.0 copy-start.4
  175.9 23.7 %collective-permute-start.22 = (f32[8,4,512,128]{3,2,1,0:T(8,128)}, f32[8,4,512,128]{3,2,1,0:T(8,128)}, u32[]{:S(2)}, u32[]{:S(2)}) collective-permute-start(f32[8,4,512,128]{3,2,1,0:T(8,128)} %get-tuple-element.12), channel_id=1, source_target_pairs={{0,4},{4,0},{8,12},{12,8},{16,20},{20,16},{24,28},{28,24},{1,5},{5... | collective-permute-start | bytes 25165832 | tf_op jit(solution)/shard_map/ppermute | solution.py:365
  199.6 17.6 %copy-start.1 = (f32[256,128]{1,0:T(8,128)S(1)}, f32[256,128]{1,0:T(8,128)}, u32[]{:S(2)}) copy-start(f32[256,128]{1,0:T(8,128)} %param.8) | copy-start | bytes 393220

commit v4 on v1

--- a/solution.py
+++ b/solution.py
@@ -141,7 +141,9 @@
     gram[kr, :] = panel[...]
 
 
-def first_kernel(values_ref, gram, block, panel, *, big, small):
+def first_kernel(values_ref, *refs, big, small):
+    gram, block, panel = refs[-3:]
+
     @pl.loop(0, gram.shape[0] // big)
     def _(t):
         r = pl.ds(pl.multiple_of(t * big, big), big)
@@ -187,13 +189,13 @@
         return pl.pallas_call(
             functools.partial(first_kernel, **options),
             out_shape=state,
-            in_specs=[vmem],
+            in_specs=[vmem] + [anywhere] * len(after),
             out_specs=vmem,
             scratch_shapes=scratch,
             compiler_params=params,
             cost_estimate=cost,
             name="sweep_first",
-        )(values)
+        )(values, *after)
     specs = [vmem] + [anywhere] * len(after)
     if not last:
         return pl.pallas_call(
@@ -269,7 +271,7 @@
         + [pl.BlockSpec(memory_space=pl.ANY)] * (len(state) + len(after)),
         out_specs=(out_spec, out_spec),
         input_output_aliases={len(pieces) + 2 + i: i for i in range(len(state))},
-        compiler_params=pltpu.CompilerParams(vmem_limit_bytes=28 * MIB),
+        compiler_params=pltpu.CompilerParams(vmem_limit_bytes=48 * MIB),
         cost_estimate=pl.CostEstimate(
             flops=2 * cols * n * planes * (bands + 8 * slab),
             bytes_accessed=2 * cols * (bands * planes + 4 * slab * n),
@@ -320,7 +322,7 @@
         ),
         out_shape=jax.ShapeDtypeStruct((slab, width, n), BF16),
         input_output_aliases={3: 0} if state else {},
-        compiler_params=pltpu.CompilerParams(vmem_limit_bytes=32 * MIB),
+        compiler_params=pltpu.CompilerParams(vmem_limit_bytes=56 * MIB),
         cost_estimate=pl.CostEstimate(
             flops=6 * cols * slab * n * n,
             bytes_accessed=6 * cols * slab * n + 4 * n * n,
@@ -393,8 +395,16 @@
             )[0]
             arriving[c].append(gy_shift(part, dg) if dg else part)
 
+    grid = np.arange(planes, dtype=np.int64)
+    table = np.cos((2.0 * np.pi / planes) * ((grid[:, None] * grid[None, :]) % planes))
+    kernel = lax.dynamic_slice_in_dim(coulomb, me * half, half, 1).T
+    lags = jnp.dot(
+        kernel, jnp.asarray(table / planes, F32), precision=HIGH, preferred_element_type=F32
+    )
+    lags = jnp.stack([jnp.roll(lags, z * slab, axis=1) for z in (gz, gz ^ 1)])
+
     steps = n // 256
-    gram = sweep_gram(values, None, 0, ())
+    gram = sweep_gram(values, None, 0, (lags,))
 
     fields = [None] * chunks
     rows = total_bands // pairs
@@ -420,14 +430,6 @@
         gram = sweep_gram(values, gram, step, after)
     inverse = gram
 
-    grid = np.arange(planes, dtype=np.int64)
-    table = np.cos((2.0 * np.pi / planes) * ((grid[:, None] * grid[None, :]) % planes))
-    kernel = lax.dynamic_slice_in_dim(coulomb, me * half, half, 1).T
-    lags = jnp.dot(
-        kernel, jnp.asarray(table / planes, F32), precision=HIGH, preferred_element_type=F32
-    )
-    lags = jnp.stack([jnp.roll(lags, z * slab, axis=1) for z in (gz, gz ^ 1)])
-
     weights = ()
     for c in range(chunks):
         after = (inverse,) if c else ()

time: 218 us -> 205 us (0.940)
  local copies, waits for them, and re-layouts: 26.8 us -> 12.2 us
  other arithmetic: 7.57 us -> 4.06 us
  starting transfers between devices: 26.5 us -> 28.8 us
    unnamed x37 -> x17, local copies, waits for them, and re-layouts: 23.7 us -> 8.43 us
    pallas_call x2, Pallas kernels: 38.9 us -> 43 us  [fit(): pl.pallas_call(fit_kernel, grid_spec=pltpu.PrefetchScalarGridSpec(num_sca...]
    select_n x6, other arithmetic: 3.79 us -> 0.62 us  [wait_for(): return jnp.where(zero_after(other) == 0, array, jnp.zeros_like(array))]
    ppermute x14, starting transfers between devices: 14.8 us -> 17.8 us  [hop(): return lax.ppermute(array, 'gz', [(z, z ^ bit) for z in range(gz_count)])]
  transfers between devices with their start and end apart: 23 -> 23, of which waited for: 3 -> 4; matrix products, arithmetic and copies ran while one was open for 5% -> 5% of each run, Pallas kernels for 50% -> 54%
where the time goes in v4:
time: 205 us; the launch traced here: 202 us
  Pallas kernels  143 us (70%)
  starting transfers between devices  28.8 us (14%)
  local copies, waits for them, and re-layouts  12.2 us (6%)
  waiting for transfers between devices  8.27 us (4%)
  between operations  5.68 us (3%)
  other arithmetic  4.06 us (2%)
    pallas_call x2, Pallas kernels, fit(): pl.pallas_call(fit_kernel, grid_spec=pltpu.PrefetchScalarGridSpec(num_sca...  43 us
    pallas_call x2, Pallas kernels, sweep_gram(): pl.pallas_call(functools.partial(middle_kernel, step=step, **options), ou...  32.4 us
    pallas_call x2, Pallas kernels, convolve(): pl.pallas_call(functools.partial(column_kernel, pieces=len(pieces)), grid...  25.1 us
    ppermute x14, starting transfers between devices, hop(): return lax.ppermute(array, 'gz', [(z, z ^ bit) for z in range(gz_count)])  17.8 us
    pallas_call x1, Pallas kernels, sweep_gram(): pl.pallas_call(functools.partial(first_kernel, **options), out_shape=stat...  17.4 us
    pallas_call x1, Pallas kernels, sweep_gram(): pl.pallas_call(functools.partial(last_kernel, step=step, **options), out_...  16.9 us
    ppermute x9, starting transfers between devices, gy_shift(): lax.ppermute(array, 'gy', [(y, (y + by) % gy_count) for y in range(gy_cou...  11 us
    unnamed x17, local copies, waits for them, and re-layouts  8.43 us
  transfers between devices with their start and end apart: 23, of which 4 were waited for; matrix products, arithmetic and copies ran while one was open for 5% of the time, Pallas kernels for 54%

profile of v4, /device:TPU:1, one launch (start us, length us, event | category | flops | bytes accessed | tf_op | source)
XLA Modules:
  0.0 202.1 jit_solution(14415987001057976317)
XLA Ops:
  0.0 3.4 %copy.10 = bf16[8,256,512]{1,0,2:T(8,128)(2,1)S(1)} copy(bf16[8,256,512]{2,1,0:T(8,128)(2,1)} %param.6) | data formatting | bytes 4194304 | tf_op args[0]
  3.4 1.1 dynamic-slice_bitcast_fusion.1
  4.6 0.3 bitcast_convert_fusion.field_ref
  4.9 0.3 copy-done.4
  5.3 7.8 %take_points.1 = f32[8,1024]{1,0:T(8,128)S(1)} custom-call(s32[3,1024]{1,0:T(4,128)S(1)} %pad_add_fusion.where_ref, f32[512,8,256]{2,1,0:T(8,128)S(1)} %bitcast_convert_fusion.field_ref), custom_call_target="tpu_custom_call" | custom-call | tf_op jit(solution)/shard_map/take_points/pallas_call | solution.py:55
  13.1 0.6 constant_dynamic-update-slice_fusion.4
  13.9 0.4 fusion.16
  14.5 0.4 collective-permute-done
  14.9 4.5 %collective-permute-start.3 = (bf16[16,1024]{1,0:T(8,128)(2,1)S(1)}, bf16[16,1024]{1,0:T(8,128)(2,1)S(1)}, u32[]{:S(2)}, u32[]{:S(2)}) collective-permute-start(bf16[16,1024]{1,0:T(8,128)(2,1)S(1)} %pad_maximum_fusion.1), channel_id=1, source_target_pairs={{0,3},{1,0},{2,1},{3,2},{4,7},{5,4},{6,5},{7,6},{8,11},{9,8},{10,9... | collective-permute-start | bytes 98312 | tf_op jit(solution)/shard_map/ppermute | solution.py:368
  19.4 0.5 collective-permute-start.1
  19.8 0.6 constant_dynamic-update-slice_fusion.3
  20.4 3.5 %collective-permute-done.1 = bf16[16,1024]{1,0:T(8,128)(2,1)S(1)} collective-permute-done((bf16[16,1024]{1,0:T(8,128)(2,1)S(1)}, bf16[16,1024]{1,0:T(8,128)(2,1)S(1)}, u32[]{:S(2)}, u32[]{:S(2)}) %collective-permute-start.1) | collective-permute-done | bytes 32800 | tf_op jit(solution)/shard_map/ppermute | solution.py:368
  24.0 0.6 constant_dynamic-update-slice_fusion.2
  24.6 0.5 slice.38
  26.3 0.6 constant_dynamic-update-slice_fusion.1
  26.9 0.6 constant_dynamic-update-slice_fusion
  27.6 2.2 %collective-permute-start.6 = (bf16[64,1024]{1,0:T(8,128)(2,1)}, bf16[64,1024]{1,0:T(8,128)(2,1)S(1)}, u32[]{:S(2)}, u32[]{:S(2)}) collective-permute-start(bf16[64,1024]{1,0:T(8,128)(2,1)} %get-tuple-element.27), channel_id=1, source_target_pairs={{0,24},{4,28},{8,16},{12,20},{16,8},{20,12},{24,0},{28,4},{1,25},{... | collective-permute-start | bytes 393224 | tf_op jit(solution)/shard_map/ppermute | solution.py:356
  30.0 0.3 collective-permute-start.4
  30.2 1.4 fusion.14
  31.7 0.9 collective-permute-start.9
  32.6 2.3 %collective-permute-done.4 = bf16[64,1024]{1,0:T(8,128)(2,1)} collective-permute-done((bf16[64,1024]{1,0:T(8,128)(2,1)}, bf16[64,1024]{1,0:T(8,128)(2,1)}, u32[]{:S(2)}, u32[]{:S(2)}) %collective-permute-start.4) | collective-permute-done | bytes 131104 | tf_op jit(solution)/shard_map/ppermute | solution.py:356
  34.9 1.3 collective-permute-start.10
  36.3 0.9 constant_dynamic-update-slice_fusion.7
  37.2 17.4 %sweep_first.1.refs_0_ = f32[1024,1024]{1,0:T(8,128)S(1)} custom-call(bf16[256,1024]{1,0:T(8,128)(2,1)S(1)} %constant_dynamic-update-slice_fusion.5.values_ref.refs_5_, f32[2,64,256]{2,1,0:T(8,128)S(1)} %pad_maximum_fusion.refs_0_.refs_6_), custom_call_target="tpu_custom_call" | custom-call | flops 1048576 | bytes 1048576 | tf_op jit(solution)/shard_map/sweep_first/pallas_call | solution.py:189
  54.6 0.5 slice.37
  56.7 1.1 collective-permute-start.17
  57.8 1.1 collective-permute-start.11
  58.9 0.8 collective-permute-start.12
  59.8 1.8 collective-permute-start.13
  61.5 1.0 collective-permute-start.16
  62.5 0.9 fusion.10
  63.4 16.2 %sweep_middle.2.refs_0_ = f32[1024,1024]{1,0:T(8,128)S(1)} custom-call(f32[1024,1024]{1,0:T(8,128)S(1)} %sweep_first.1.refs_0_, bf16[32,64,256]{2,1,0:T(8,128)(2,1)S(1)} %maximum_select_fusion.refs_1_.refs_0_), custom_call_target="tpu_custom_call", output_to_operand_aliasing={{}: (0, {})} | custom-call | flops 1048576 | bytes 1048576 | tf_op jit(solution)/shard_map/sweep_middle/pallas_call | solution.py:201
  79.6 0.5 slice.39
  81.7 0.6 collective-permute-start.15
  82.3 0.4 collective-permute-start.14
  82.8 1.1 collective-permute-start.20
  84.0 0.9 collective-permute-start.21
  84.9 16.2 %sweep_middle.3.gram_ref = f32[1024,1024]{1,0:T(8,128)S(1)} custom-call(f32[1024,1024]{1,0:T(8,128)S(1)} %sweep_middle.2.refs_0_, bf16[32,64,256]{2,1,0:T(8,128)(2,1)S(1)} %maximum_select_fusion.1.refs_1_.refs_0_, bf16[32,64,256]{2,1,0:T(8,128)(2,1)S(1)} %collective-permute-done.16.refs_2_.refs_1_, ...), custom_call_target="tpu_custom_call", output_to_operand_aliasing={{}: (0, {})} | custom-call | flops 1048576 | bytes 1048576 | tf_op jit(solution)/shard_map/sweep_middle/pallas_call | solution.py:201
  101.2 0.5 slice.40
  103.0 0.6 collective-permute-start.18
  103.6 2.0 collective-permute-done.14.refs_0_.refs_1_
  105.7 16.9 %sweep_last.1.refs_9_.inverse_ref = bf16[2048,1024]{1,0:T(8,128)(2,1)S(1)} custom-call(f32[1024,1024]{1,0:T(8,128)S(1)} %sweep_middle.3.gram_ref, bf16[32,64,256]{2,1,0:T(8,128)(2,1)S(1)} %collective-permute-done.14.refs_0_.refs_1_, bf16[32,64,256]{2,1,0:T(8,128)(2,1)S(1)} %collective-permute-done.15.refs_1_.refs_2_), custom_call_target="tpu_custom_call" | custom-call | flops 1048576 | bytes 1048576 | tf_op jit(solution)/shard_map/sweep_last/pallas_call | solution.py:212
  122.6 2.0 copy-done.2
  124.6 12.7 %convolve.2 = (bf16[64,32,2048]{2,1,0:T(8,128)(2,1)}, bf16[64,32,2048]{2,1,0:T(8,128)(2,1)}) custom-call(bf16[32,64,256]{2,1,0:T(8,128)(2,1)S(1)} %maximum_select_fusion.refs_1_.refs_0_, bf16[32,64,256]{2,1,0:T(8,128)(2,1)S(1)} %collective-permute-done.16.refs_2_.refs_1_, bf16[32,64,256]{2,1,0:T(8,128)(2,1)S(1)} %collective-permute-done.17.refs_3_.refs_2_, ...), custom_call_target="tpu_custom_call" | custom-call | flops 8589934592 | bytes 12582912 | tf_op jit(solution)/shard_map/convolve/pallas_call | solution.py:262
  137.3 12.4 %convolve.3 = (bf16[64,32,2048]{2,1,0:T(8,128)(2,1)}, bf16[64,32,2048]{2,1,0:T(8,128)(2,1)}) custom-call(bf16[32,64,256]{2,1,0:T(8,128)(2,1)S(1)} %maximum_select_fusion.1.refs_1_.refs_0_, bf16[32,64,256]{2,1,0:T(8,128)(2,1)S(1)} %collective-permute-done.14.refs_0_.refs_1_, ...), custom_call_target="tpu_custom_call", output_to_operand_aliasing={{0}: (7, {}), {1}: (8, {})} | custom-call | flops 8589934592 | bytes 12582912 | tf_op jit(solution)/shard_map/convolve/pallas_call | solution.py:262
  149.7 9.1 %collective-permute-start.22 = (bf16[64,32,2048]{2,1,0:T(8,128)(2,1)}, bf16[64,32,2048]{2,1,0:T(8,128)(2,1)}, u32[]{:S(2)}, u32[]{:S(2)}) collective-permute-start(bf16[64,32,2048]{2,1,0:T(8,128)(2,1)} %get-tuple-element.12), channel_id=1, source_target_pairs={{0,4},{4,0},{8,12},{12,8},{16,20},{20,16},{24,28},{28,24},{1,5},{5... | collective-permute-start | bytes 25165832 | tf_op jit(solution)/shard_map/ppermute | solution.py:356
  158.8 21.5 %fit.2.refs_0_ = bf16[32,128,1024]{2,1,0:T(8,128)(2,1)} custom-call(s32[1]{0:T(128)} %bitcast.23.at_ref, bf16[64,32,2048]{2,1,0:T(8,128)(2,1)} %get-tuple-element.13.w_ref, bf16[2048,1024]{1,0:T(8,128)(2,1)} %copy-done.2), custom_call_target="tpu_custom_call" | custom-call | flops 12884901888 | bytes 16777216 | tf_op jit(solution)/shard_map/fit/pallas_call | solution.py:310
  180.3 21.5 %fit.3 = bf16[32,128,1024]{2,1,0:T(8,128)(2,1)} custom-call(s32[1]{0:T(128)} %bitcast.at_ref, bf16[64,32,2048]{2,1,0:T(8,128)(2,1)} %collective-permute-done.22.w_ref, bf16[2048,1024]{1,0:T(8,128)(2,1)} %copy-done.2, bf16[32,128,1024]{2,1,0:T(8,128)(2,1)} %fit.2.refs_0_), custom_call_target="tpu_custom_call", output_to_operand_aliasing={{}: (3, {})} | custom-call | flops 12884901888 | bytes 16777216 | tf_op jit(solution)/shard_map/fit/pallas_call | solution.py:310
  (47 shorter events, 1.5 us)
Async XLA Ops:
  0.0 13.9 %copy-start = (f32[256,128]{1,0:T(8,128)S(1)}, f32[256,128]{1,0:T(8,128)}, u32[]{:S(2)}) copy-start(f32[256,128]{1,0:T(8,128)} %param.8) | copy-start | bytes 393220
  4.5 0.7 copy-start.4
  4.5 25.7 %collective-permute-start.7 = (bf16[4,64,8,256]{3,2,1,0:T(8,128)(2,1)}, bf16[4,64,8,256]{3,2,1,0:T(8,128)(2,1)}, u32[]{:S(2)}, u32[]{:S(2)}) collective-permute-start(bf16[4,64,8,256]{3,2,1,0:T(8,128)(2,1)} %get-tuple-element.24), channel_id=1, source_target_pairs={{0,4},{4,0},{8,12},{12,8},{16,20},{20,16},{24,28},{28,24},{1,5},{5... | collective-permute-start | bytes 3145736 | tf_op jit(solution)/shard_map/ppermute | solution.py:356
  5.2 8.6 %copy-start.3 = (f32[256,256]{1,0:T(8,128)S(1)}, f32[256,256]{1,0:T(8,128)}, u32[]{:S(2)}) copy-start(f32[256,256]{1,0:T(8,128)} %constant.132.clone) | copy-start | bytes 786436
  13.7 1.2 collective-permute-start
  14.9 9.7 %collective-permute-start.3 = (bf16[16,1024]{1,0:T(8,128)(2,1)S(1)}, bf16[16,1024]{1,0:T(8,128)(2,1)S(1)}, u32[]{:S(2)}, u32[]{:S(2)}) collective-permute-start(bf16[16,1024]{1,0:T(8,128)(2,1)S(1)} %pad_maximum_fusion.1), channel_id=1, source_target_pairs={{0,3},{1,0},{2,1},{3,2},{4,7},{5,4},{6,5},{7,6},{8,11},{9,8},{10,9... | collective-permute-start | bytes 98312 | tf_op jit(solution)/shard_map/ppermute | solution.py:368
  19.4 6.9 %collective-permute-start.2 = (bf16[16,1024]{1,0:T(8,128)(2,1)S(1)}, bf16[16,1024]{1,0:T(8,128)(2,1)S(1)}, u32[]{:S(2)}, u32[]{:S(2)}) collective-permute-start(bf16[16,1024]{1,0:T(8,128)(2,1)S(1)} %pad_maximum_fusion.1), channel_id=1, source_target_pairs={{0,2},{1,3},{2,0},{3,1},{4,6},{5,7},{6,4},{7,5},{8,10},{9,11},{10,... | collective-permute-start | bytes 98312 | tf_op jit(solution)/shard_map/ppermute | solution.py:368
  19.4 4.6 %collective-permute-start.1 = (bf16[16,1024]{1,0:T(8,128)(2,1)S(1)}, bf16[16,1024]{1,0:T(8,128)(2,1)S(1)}, u32[]{:S(2)}, u32[]{:S(2)}) collective-permute-start(bf16[16,1024]{1,0:T(8,128)(2,1)S(1)} %pad_maximum_fusion.1), channel_id=1, source_target_pairs={{0,1},{1,2},{2,3},{3,0},{4,5},{5,6},{6,7},{7,4},{8,9},{9,10},{10,1... | collective-permute-start | bytes 98312 | tf_op jit(solution)/shard_map/ppermute | solution.py:368
  27.6 9.6 %collective-permute-start.6 = (bf16[64,1024]{1,0:T(8,128)(2,1)}, bf16[64,1024]{1,0:T(8,128)(2,1)S(1)}, u32[]{:S(2)}, u32[]{:S(2)}) collective-permute-start(bf16[64,1024]{1,0:T(8,128)(2,1)} %get-tuple-element.27), channel_id=1, source_target_pairs={{0,24},{4,28},{8,16},{12,20},{16,8},{20,12},{24,0},{28,4},{1,25},{... | collective-permute-start | bytes 393224 | tf_op jit(solution)/shard_map/ppermute | solution.py:356
  29.7 7.4 %collective-permute-start.5 = (bf16[64,1024]{1,0:T(8,128)(2,1)}, bf16[64,1024]{1,0:T(8,128)(2,1)S(1)}, u32[]{:S(2)}, u32[]{:S(2)}) collective-permute-start(bf16[64,1024]{1,0:T(8,128)(2,1)} %get-tuple-element.27), channel_id=1, source_target_pairs={{0,16},{4,20},{8,24},{12,28},{16,0},{20,4},{24,8},{28,12},{1,17},{... | collective-permute-start | bytes 393224 | tf_op jit(solution)/shard_map/ppermute | solution.py:356
  30.0 5.0 %collective-permute-start.4 = (bf16[64,1024]{1,0:T(8,128)(2,1)}, bf16[64,1024]{1,0:T(8,128)(2,1)}, u32[]{:S(2)}, u32[]{:S(2)}) collective-permute-start(bf16[64,1024]{1,0:T(8,128)(2,1)} %get-tuple-element.27), channel_id=1, source_target_pairs={{0,8},{4,12},{8,0},{12,4},{16,24},{20,28},{24,16},{28,20},{1,9},{5... | collective-permute-start | bytes 393224 | tf_op jit(solution)/shard_map/ppermute | solution.py:356
  31.6 24.8 %collective-permute-start.8 = (bf16[32,16,256]{2,1,0:T(8,128)(2,1)S(1)}, bf16[32,16,256]{2,1,0:T(8,128)(2,1)S(1)}, u32[]{:S(2)}, u32[]{:S(2)}) collective-permute-start(bf16[32,16,256]{2,1,0:T(8,128)(2,1)S(1)} %get-tuple-element.17), channel_id=1, source_target_pairs={{0,1},{1,2},{2,3},{3,0},{4,5},{5,6},{6,7},{7,4},{8,9},{9,10},{10,1... | collective-permute-start | bytes 786440 | tf_op jit(solution)/shard_map/ppermute | solution.py:368
  31.7 24.8 %collective-permute-start.9 = (bf16[32,16,256]{2,1,0:T(8,128)(2,1)S(1)}, bf16[32,16,256]{2,1,0:T(8,128)(2,1)S(1)}, u32[]{:S(2)}, u32[]{:S(2)}) collective-permute-start(bf16[32,16,256]{2,1,0:T(8,128)(2,1)S(1)} %get-tuple-element.18), channel_id=1, source_target_pairs={{0,2},{1,3},{2,0},{3,1},{4,6},{5,7},{6,4},{7,5},{8,10},{9,11},{10,... | collective-permute-start | bytes 786440 | tf_op jit(solution)/shard_map/ppermute | solution.py:368
  34.9 21.5 %collective-permute-start.10 = (bf16[32,16,256]{2,1,0:T(8,128)(2,1)S(1)}, bf16[32,16,256]{2,1,0:T(8,128)(2,1)S(1)}, u32[]{:S(2)}, u32[]{:S(2)}) collective-permute-start(bf16[32,16,256]{2,1,0:T(8,128)(2,1)S(1)} %get-tuple-element.19), channel_id=1, source_target_pairs={{0,3},{1,0},{2,1},{3,2},{4,7},{5,4},{6,5},{7,6},{8,11},{9,8},{10,9... | collective-permute-start | bytes 786440 | tf_op jit(solution)/shard_map/ppermute | solution.py:368
  56.7 26.0 %collective-permute-start.17 = (bf16[32,64,256]{2,1,0:T(8,128)(2,1)S(1)}, bf16[32,64,256]{2,1,0:T(8,128)(2,1)S(1)}, u32[]{:S(2)}, u32[]{:S(2)}) collective-permute-start(bf16[32,64,256]{2,1,0:T(8,128)(2,1)S(1)} %maximum_select_fusion.refs_1_.refs_0_), channel_id=1, source_target_pairs={{0,16},{4,20},{8,24},{12,28},{16,0},{20,4},{24,8},{28,12},{1,17},{... | collective-permute-start | bytes 3145736 | tf_op jit(solution)/shard_map/ppermute | solution.py:356
  57.8 23.7 %collective-permute-start.11 = (bf16[32,16,256]{2,1,0:T(8,128)(2,1)S(1)}, bf16[32,16,256]{2,1,0:T(8,128)(2,1)S(1)}, u32[]{:S(2)}, u32[]{:S(2)}) collective-permute-start(bf16[32,16,256]{2,1,0:T(8,128)(2,1)S(1)} %get-tuple-element.20), channel_id=1, source_target_pairs={{0,1},{1,2},{2,3},{3,0},{4,5},{5,6},{6,7},{7,4},{8,9},{9,10},{10,1... | collective-permute-start | bytes 786440 | tf_op jit(solution)/shard_map/ppermute | solution.py:368
  58.9 22.5 %collective-permute-start.12 = (bf16[32,16,256]{2,1,0:T(8,128)(2,1)S(1)}, bf16[32,16,256]{2,1,0:T(8,128)(2,1)S(1)}, u32[]{:S(2)}, u32[]{:S(2)}) collective-permute-start(bf16[32,16,256]{2,1,0:T(8,128)(2,1)S(1)} %get-tuple-element.21), channel_id=1, source_target_pairs={{0,2},{1,3},{2,0},{3,1},{4,6},{5,7},{6,4},{7,5},{8,10},{9,11},{10,... | collective-permute-start | bytes 786440 | tf_op jit(solution)/shard_map/ppermute | solution.py:368
  59.8 21.7 %collective-permute-start.13 = (bf16[32,16,256]{2,1,0:T(8,128)(2,1)S(1)}, bf16[32,16,256]{2,1,0:T(8,128)(2,1)S(1)}, u32[]{:S(2)}, u32[]{:S(2)}) collective-permute-start(bf16[32,16,256]{2,1,0:T(8,128)(2,1)S(1)} %get-tuple-element.22), channel_id=1, source_target_pairs={{0,3},{1,0},{2,1},{3,2},{4,7},{5,4},{6,5},{7,6},{8,11},{9,8},{10,9... | collective-permute-start | bytes 786440 | tf_op jit(solution)/shard_map/ppermute | solution.py:368
  61.5 22.4 %collective-permute-start.16 = (bf16[32,64,256]{2,1,0:T(8,128)(2,1)S(1)}, bf16[32,64,256]{2,1,0:T(8,128)(2,1)S(1)}, u32[]{:S(2)}, u32[]{:S(2)}) collective-permute-start(bf16[32,64,256]{2,1,0:T(8,128)(2,1)S(1)} %maximum_select_fusion.refs_1_.refs_0_), channel_id=1, source_target_pairs={{0,8},{4,12},{8,0},{12,4},{16,24},{20,28},{24,16},{28,20},{1,9},{5... | collective-permute-start | bytes 3145736 | tf_op jit(solution)/shard_map/ppermute | solution.py:356
  81.7 21.3 %collective-permute-start.15 = (bf16[32,64,256]{2,1,0:T(8,128)(2,1)S(1)}, bf16[32,64,256]{2,1,0:T(8,128)(2,1)S(1)}, u32[]{:S(2)}, u32[]{:S(2)}) collective-permute-start(bf16[32,64,256]{2,1,0:T(8,128)(2,1)S(1)} %maximum_select_fusion.1.refs_1_.refs_0_), channel_id=1, source_target_pairs={{0,16},{4,20},{8,24},{12,28},{16,0},{20,4},{24,8},{28,12},{1,17},{... | collective-permute-start | bytes 3145736 | tf_op jit(solution)/shard_map/ppermute | solution.py:356
  82.3 23.3 %collective-permute-start.14 = (bf16[32,64,256]{2,1,0:T(8,128)(2,1)S(1)}, bf16[32,64,256]{2,1,0:T(8,128)(2,1)S(1)}, u32[]{:S(2)}, u32[]{:S(2)}) collective-permute-start(bf16[32,64,256]{2,1,0:T(8,128)(2,1)S(1)} %maximum_select_fusion.1.refs_1_.refs_0_), channel_id=1, source_target_pairs={{0,8},{4,12},{8,0},{12,4},{16,24},{20,28},{24,16},{28,20},{1,9},{5... | collective-permute-start | bytes 3145736 | tf_op jit(solution)/shard_map/ppermute | solution.py:356
  82.8 41.8 %collective-permute-start.20 = (bf16[32,32,256]{2,1,0:T(8,128)(2,1)S(1)}, bf16[32,32,256]{2,1,0:T(8,128)(2,1)S(1)}, u32[]{:S(2)}, u32[]{:S(2)}) collective-permute-start(bf16[32,32,256]{2,1,0:T(8,128)(2,1)S(1)} %slice_select_fusion.1), channel_id=1, source_target_pairs={{0,8},{4,12},{8,0},{12,4},{16,24},{20,28},{24,16},{28,20},{1,9},{5... | collective-permute-start | bytes 1572872 | tf_op jit(solution)/shard_map/ppermute | solution.py:356
  84.0 40.6 %collective-permute-start.21 = (bf16[32,32,256]{2,1,0:T(8,128)(2,1)S(1)}, bf16[32,32,256]{2,1,0:T(8,128)(2,1)S(1)}, u32[]{:S(2)}, u32[]{:S(2)}) collective-permute-start(bf16[32,32,256]{2,1,0:T(8,128)(2,1)S(1)} %slice_select_fusion), channel_id=1, source_target_pairs={{0,16},{4,20},{8,24},{12,28},{16,0},{20,4},{24,8},{28,12},{1,17},{... | collective-permute-start | bytes 1572872 | tf_op jit(solution)/shard_map/ppermute | solution.py:356
  103.0 34.3 %collective-permute-start.18 = (bf16[32,32,256]{2,1,0:T(8,128)(2,1)S(1)}, bf16[32,32,256]{2,1,0:T(8,128)(2,1)S(1)}, u32[]{:S(2)}, u32[]{:S(2)}) collective-permute-start(bf16[32,32,256]{2,1,0:T(8,128)(2,1)S(1)} %slice_select_fusion.3), channel_id=1, source_target_pairs={{0,8},{4,12},{8,0},{12,4},{16,24},{20,28},{24,16},{28,20},{1,9},{5... | collective-permute-start | bytes 1572872 | tf_op jit(solution)/shard_map/ppermute | solution.py:356
  105.6 31.7 %collective-permute-start.19 = (bf16[32,32,256]{2,1,0:T(8,128)(2,1)S(1)}, bf16[32,32,256]{2,1,0:T(8,128)(2,1)S(1)}, u32[]{:S(2)}, u32[]{:S(2)}) collective-permute-start(bf16[32,32,256]{2,1,0:T(8,128)(2,1)S(1)} %slice_select_fusion.2), channel_id=1, source_target_pairs={{0,16},{4,20},{8,24},{12,28},{16,0},{20,4},{24,8},{28,12},{1,17},{... | collective-permute-start | bytes 1572872 | tf_op jit(solution)/shard_map/ppermute | solution.py:356
  122.6 2.0 copy-start.2
  149.7 30.6 %collective-permute-start.22 = (bf16[64,32,2048]{2,1,0:T(8,128)(2,1)}, bf16[64,32,2048]{2,1,0:T(8,128)(2,1)}, u32[]{:S(2)}, u32[]{:S(2)}) collective-permute-start(bf16[64,32,2048]{2,1,0:T(8,128)(2,1)} %get-tuple-element.12), channel_id=1, source_target_pairs={{0,4},{4,0},{8,12},{12,8},{16,20},{20,16},{24,28},{28,24},{1,5},{5... | collective-permute-start | bytes 25165832 | tf_op jit(solution)/shard_map/ppermute | solution.py:356
  180.3 21.5 %copy-start.1 = (f32[256,128]{1,0:T(8,128)S(1)}, f32[256,128]{1,0:T(8,128)}, u32[]{:S(2)}) copy-start(f32[256,128]{1,0:T(8,128)} %param.8) | copy-start | bytes 393220

commit v5 on v4

--- a/solution.py
+++ b/solution.py
@@ -65,44 +65,48 @@
     )(where, field)
 
 
+def total(terms):
+    while len(terms) > 1:
+        terms = [x + y for x, y in zip(terms[::2], terms[1::2])]
+    return terms[0]
+
+
 def sweep_small(a):
     n = a.shape[0]
     lane = lax.broadcasted_iota(jnp.int32, (8, n), 1)
-    wide = lax.broadcasted_iota(jnp.int32, (n, n), 1)
     sub = lax.broadcasted_iota(jnp.int32, (8, n), 0)
+    tiles = [a[i : i + 8, :] for i in range(0, n, 8)]
+
+    def spread_row(x, row):
+        return jnp.broadcast_to(x[row : row + 1, :], (8, n))
+
+    def spread_column(x, column):
+        return jnp.broadcast_to(x[:, column : column + 1], (8, n))
+
     for g in range(n // 8):
         lo = 8 * g
-        rows = a[lo : lo + 8, :]
-        cols = [jnp.broadcast_to(a[:, lo + j : lo + j + 1], (n, n)) for j in range(8)]
-        t = [c[lo : lo + 8, :] for c in cols]
+        rows = tiles[g]
+        t = [spread_column(rows, lo + j) for j in range(8)]
         for k in range(8):
-            pivot = jnp.broadcast_to(t[k][k : k + 1, :], (8, n))
-            scale = 1.0 / pivot
             here = sub == k
-            new = []
-            for j in range(8):
-                if j == k:
-                    new.append(jnp.where(here, -1.0, t[k]) * scale)
-                else:
-                    factor = jnp.broadcast_to(t[j][k : k + 1, :], (8, n))
-                    kept = jnp.where(here, 0.0, t[j])
-                    new.append(kept - (jnp.where(here, -1.0, t[k]) * factor) * scale)
-            t = new
-        terms = [t[j] * jnp.broadcast_to(rows[j : j + 1, :], (8, n)) for j in range(8)]
-        while len(terms) > 1:
-            terms = [x + y for x, y in zip(terms[::2], terms[1::2])]
-        q = -terms[0]
+            pivot = jnp.where(here, -1.0, t[k]) * (1.0 / spread_row(t[k], k))
+            t = [
+                pivot if j == k else jnp.where(here, 0.0, t[j]) - pivot * spread_row(t[j], k)
+                for j in range(8)
+            ]
+        q = -total([t[j] * spread_row(rows, j) for j in range(8)])
         for j in range(8):
             q = jnp.where(lane == lo + j, t[j], q)
-        inside = (wide >= lo) & (wide < lo + 8)
-        terms = [cols[j] * jnp.broadcast_to(q[j : j + 1, :], (n, n)) for j in range(8)]
-        while len(terms) > 1:
-            terms = [x + y for x, y in zip(terms[::2], terms[1::2])]
-        upd = jnp.where(inside, 0.0, a) - terms[0]
-        a = jnp.concatenate(
-            ([upd[:lo]] if lo else []) + [q] + ([upd[lo + 8 :]] if lo + 8 < n else []), axis=0
-        )
-    return a
+        inside = (lane >= lo) & (lane < lo + 8)
+        q_rows = [spread_row(q, j) for j in range(8)]
+        tiles = [
+            q
+            if i == g
+            else jnp.where(inside, 0.0, tile)
+            - total([spread_column(tile, lo + j) * q_rows[j] for j in range(8)])
+            for i, tile in enumerate(tiles)
+        ]
+    return jnp.concatenate(tiles, axis=0)
 
 
 def mm(a, b):

time: 205 us -> 202 us (0.985)
  Pallas kernels: 143 us -> 137 us
  waiting for transfers between devices: 8.27 us -> 12.2 us
    ppermute x14, waiting for transfers between devices: 4.72 us -> 8.62 us  [hop(): return lax.ppermute(array, 'gz', [(z, z ^ bit) for z in range(gz_count)])]
    ppermute x14, starting transfers between devices: 17.8 us -> 14.7 us  [hop(): return lax.ppermute(array, 'gz', [(z, z ^ bit) for z in range(gz_count)])]
    pallas_call x2, Pallas kernels: 32.4 us -> 29.6 us  [sweep_gram(): pl.pallas_call(functools.partial(middle_kernel, step=step, **options), ou...]
  transfers between devices with their start and end apart: 23 -> 23, of which waited for: 4 -> 6; matrix products, arithmetic and copies ran while one was open for 5% -> 5% of each run, Pallas kernels for 54% -> 52%
where the time goes in v5:
time: 202 us; the launch traced here: 198 us
  Pallas kernels  137 us (68%)
  starting transfers between devices  26.8 us (13%)
  local copies, waits for them, and re-layouts  12.2 us (6%)
  waiting for transfers between devices  12.2 us (6%)
  between operations  5.66 us (3%)
  other arithmetic  4.05 us (2%)
    pallas_call x2, Pallas kernels, fit(): pl.pallas_call(fit_kernel, grid_spec=pltpu.PrefetchScalarGridSpec(num_sca...  43 us
    pallas_call x2, Pallas kernels, sweep_gram(): pl.pallas_call(functools.partial(middle_kernel, step=step, **options), ou...  29.6 us
    pallas_call x2, Pallas kernels, convolve(): pl.pallas_call(functools.partial(column_kernel, pieces=len(pieces)), grid...  25.1 us
    pallas_call x1, Pallas kernels, sweep_gram(): pl.pallas_call(functools.partial(first_kernel, **options), out_shape=stat...  16 us
    pallas_call x1, Pallas kernels, sweep_gram(): pl.pallas_call(functools.partial(last_kernel, step=step, **options), out_...  15.5 us
    ppermute x14, starting transfers between devices, hop(): return lax.ppermute(array, 'gz', [(z, z ^ bit) for z in range(gz_count)])  14.7 us
    ppermute x9, starting transfers between devices, gy_shift(): lax.ppermute(array, 'gy', [(y, (y + by) % gy_count) for y in range(gy_cou...  12.1 us
    ppermute x14, waiting for transfers between devices, hop(): return lax.ppermute(array, 'gz', [(z, z ^ bit) for z in range(gz_count)])  8.62 us
  transfers between devices with their start and end apart: 23, of which 6 were waited for; matrix products, arithmetic and copies ran while one was open for 5% of the time, Pallas kernels for 52%

profile of v5, /device:TPU:1, one launch (start us, length us, event | category | flops | bytes accessed | tf_op | source)
XLA Modules:
  0.0 198.4 jit_solution(18225288003836555426)
XLA Ops:
  0.0 3.4 %copy.10 = bf16[8,256,512]{1,0,2:T(8,128)(2,1)S(1)} copy(bf16[8,256,512]{2,1,0:T(8,128)(2,1)} %param.6) | data formatting | bytes 4194304 | tf_op args[0]
  3.4 1.1 dynamic-slice_bitcast_fusion.1
  4.6 0.3 bitcast_convert_fusion.field_ref
  4.9 0.3 copy-done.4
  5.3 7.8 %take_points.1 = f32[8,1024]{1,0:T(8,128)S(1)} custom-call(s32[3,1024]{1,0:T(4,128)S(1)} %pad_add_fusion.where_ref, f32[512,8,256]{2,1,0:T(8,128)S(1)} %bitcast_convert_fusion.field_ref), custom_call_target="tpu_custom_call" | custom-call | tf_op jit(solution)/shard_map/take_points/pallas_call | solution.py:55
  13.1 0.6 constant_dynamic-update-slice_fusion.4
  13.9 0.4 fusion.16
  14.5 0.4 collective-permute-done
  14.9 4.5 %collective-permute-start.3 = (bf16[16,1024]{1,0:T(8,128)(2,1)S(1)}, bf16[16,1024]{1,0:T(8,128)(2,1)S(1)}, u32[]{:S(2)}, u32[]{:S(2)}) collective-permute-start(bf16[16,1024]{1,0:T(8,128)(2,1)S(1)} %pad_maximum_fusion.1), channel_id=1, source_target_pairs={{0,3},{1,0},{2,1},{3,2},{4,7},{5,4},{6,5},{7,6},{8,11},{9,8},{10,9... | collective-permute-start | bytes 98312 | tf_op jit(solution)/shard_map/ppermute | solution.py:372
  19.4 0.5 collective-permute-start.1
  19.8 0.6 constant_dynamic-update-slice_fusion.3
  20.4 3.5 %collective-permute-done.1 = bf16[16,1024]{1,0:T(8,128)(2,1)S(1)} collective-permute-done((bf16[16,1024]{1,0:T(8,128)(2,1)S(1)}, bf16[16,1024]{1,0:T(8,128)(2,1)S(1)}, u32[]{:S(2)}, u32[]{:S(2)}) %collective-permute-start.1) | collective-permute-done | bytes 32800 | tf_op jit(solution)/shard_map/ppermute | solution.py:372
  24.0 0.6 constant_dynamic-update-slice_fusion.2
  24.6 0.5 slice.38
  26.3 0.6 constant_dynamic-update-slice_fusion.1
  26.9 0.6 constant_dynamic-update-slice_fusion
  27.6 2.2 %collective-permute-start.6 = (bf16[64,1024]{1,0:T(8,128)(2,1)}, bf16[64,1024]{1,0:T(8,128)(2,1)S(1)}, u32[]{:S(2)}, u32[]{:S(2)}) collective-permute-start(bf16[64,1024]{1,0:T(8,128)(2,1)} %get-tuple-element.27), channel_id=1, source_target_pairs={{0,24},{4,28},{8,16},{12,20},{16,8},{20,12},{24,0},{28,4},{1,25},{... | collective-permute-start | bytes 393224 | tf_op jit(solution)/shard_map/ppermute | solution.py:360
  30.2 1.4 fusion.14
  31.7 0.9 collective-permute-start.9
  32.6 2.3 %collective-permute-done.4 = bf16[64,1024]{1,0:T(8,128)(2,1)} collective-permute-done((bf16[64,1024]{1,0:T(8,128)(2,1)}, bf16[64,1024]{1,0:T(8,128)(2,1)}, u32[]{:S(2)}, u32[]{:S(2)}) %collective-permute-start.4) | collective-permute-done | bytes 131104 | tf_op jit(solution)/shard_map/ppermute | solution.py:360
  34.9 1.3 collective-permute-start.10
  36.3 0.9 constant_dynamic-update-slice_fusion.7
  37.2 16.0 %sweep_first.1.refs_0_ = f32[1024,1024]{1,0:T(8,128)S(1)} custom-call(bf16[256,1024]{1,0:T(8,128)(2,1)S(1)} %constant_dynamic-update-slice_fusion.5.values_ref.refs_5_, f32[2,64,256]{2,1,0:T(8,128)S(1)} %pad_maximum_fusion.refs_0_.refs_6_), custom_call_target="tpu_custom_call" | custom-call | flops 1048576 | bytes 1048576 | tf_op jit(solution)/shard_map/sweep_first/pallas_call | solution.py:193
  53.2 0.5 slice.37
  55.3 1.1 collective-permute-start.17
  56.4 2.3 %collective-permute-start.11 = (bf16[32,16,256]{2,1,0:T(8,128)(2,1)S(1)}, bf16[32,16,256]{2,1,0:T(8,128)(2,1)S(1)}, u32[]{:S(2)}, u32[]{:S(2)}) collective-permute-start(bf16[32,16,256]{2,1,0:T(8,128)(2,1)S(1)} %get-tuple-element.20), channel_id=1, source_target_pairs={{0,1},{1,2},{2,3},{3,0},{4,5},{5,6},{6,7},{7,4},{8,9},{9,10},{10,1... | collective-permute-start | bytes 786440 | tf_op jit(solution)/shard_map/ppermute | solution.py:372
  58.7 2.6 %collective-permute-start.13 = (bf16[32,16,256]{2,1,0:T(8,128)(2,1)S(1)}, bf16[32,16,256]{2,1,0:T(8,128)(2,1)S(1)}, u32[]{:S(2)}, u32[]{:S(2)}) collective-permute-start(bf16[32,16,256]{2,1,0:T(8,128)(2,1)S(1)} %get-tuple-element.22), channel_id=1, source_target_pairs={{0,3},{1,0},{2,1},{3,2},{4,7},{5,4},{6,5},{7,6},{8,11},{9,8},{10,9... | collective-permute-start | bytes 786440 | tf_op jit(solution)/shard_map/ppermute | solution.py:372
  61.2 1.3 collective-permute-start.16
  62.5 0.9 fusion.10
  63.4 14.8 %sweep_middle.2.refs_0_ = f32[1024,1024]{1,0:T(8,128)S(1)} custom-call(f32[1024,1024]{1,0:T(8,128)S(1)} %sweep_first.1.refs_0_, bf16[32,64,256]{2,1,0:T(8,128)(2,1)S(1)} %maximum_select_fusion.refs_1_.refs_0_), custom_call_target="tpu_custom_call", output_to_operand_aliasing={{}: (0, {})} | custom-call | flops 1048576 | bytes 1048576 | tf_op jit(solution)/shard_map/sweep_middle/pallas_call | solution.py:205
  78.2 0.5 slice.39
  80.3 0.3 collective-permute-start.15
  80.9 1.3 collective-permute-start.20
  82.2 0.5 collective-permute-done.16.refs_2_.refs_1_
  82.7 0.8 collective-permute-start.21
  83.5 14.8 %sweep_middle.3.gram_ref = f32[1024,1024]{1,0:T(8,128)S(1)} custom-call(f32[1024,1024]{1,0:T(8,128)S(1)} %sweep_middle.2.refs_0_, bf16[32,64,256]{2,1,0:T(8,128)(2,1)S(1)} %maximum_select_fusion.1.refs_1_.refs_0_, bf16[32,64,256]{2,1,0:T(8,128)(2,1)S(1)} %collective-permute-done.16.refs_2_.refs_1_, ...), custom_call_target="tpu_custom_call", output_to_operand_aliasing={{}: (0, {})} | custom-call | flops 1048576 | bytes 1048576 | tf_op jit(solution)/shard_map/sweep_middle/pallas_call | solution.py:205
  98.3 0.5 slice.40
  100.2 1.4 collective-permute-done.15.refs_1_.refs_2_
  101.6 0.3 collective-permute-start.18
  101.9 3.9 %collective-permute-done.14.refs_0_.refs_1_ = bf16[32,64,256]{2,1,0:T(8,128)(2,1)S(1)} collective-permute-done((bf16[32,64,256]{2,1,0:T(8,128)(2,1)S(1)}, bf16[32,64,256]{2,1,0:T(8,128)(2,1)S(1)}, u32[]{:S(2)}, u32[]{:S(2)}) %collective-permute-start.14) | collective-permute-done | bytes 1048608 | tf_op jit(solution)/shard_map/ppermute | solution.py:360
  105.9 1.2 collective-permute-start.19
  107.1 15.5 %sweep_last.1.refs_9_.inverse_ref = bf16[2048,1024]{1,0:T(8,128)(2,1)S(1)} custom-call(f32[1024,1024]{1,0:T(8,128)S(1)} %sweep_middle.3.gram_ref, bf16[32,64,256]{2,1,0:T(8,128)(2,1)S(1)} %collective-permute-done.14.refs_0_.refs_1_, bf16[32,64,256]{2,1,0:T(8,128)(2,1)S(1)} %collective-permute-done.15.refs_1_.refs_2_), custom_call_target="tpu_custom_call" | custom-call | flops 1048576 | bytes 1048576 | tf_op jit(solution)/shard_map/sweep_last/pallas_call | solution.py:216
  122.6 2.0 %copy-done.2 = bf16[2048,1024]{1,0:T(8,128)(2,1)} copy-done((bf16[2048,1024]{1,0:T(8,128)(2,1)}, bf16[2048,1024]{1,0:T(8,128)(2,1)S(1)}, u32[]{:S(2)}) %copy-start.2) | copy-done | bytes 4194328
  124.6 12.4 %convolve.2 = (bf16[64,32,2048]{2,1,0:T(8,128)(2,1)}, bf16[64,32,2048]{2,1,0:T(8,128)(2,1)}) custom-call(bf16[32,64,256]{2,1,0:T(8,128)(2,1)S(1)} %maximum_select_fusion.refs_1_.refs_0_, bf16[32,64,256]{2,1,0:T(8,128)(2,1)S(1)} %collective-permute-done.16.refs_2_.refs_1_, bf16[32,64,256]{2,1,0:T(8,128)(2,1)S(1)} %collective-permute-done.17.refs_3_.refs_2_, ...), custom_call_target="tpu_custom_call" | custom-call | flops 8589934592 | bytes 12582912 | tf_op jit(solution)/shard_map/convolve/pallas_call | solution.py:266
  137.0 12.7 %convolve.3 = (bf16[64,32,2048]{2,1,0:T(8,128)(2,1)}, bf16[64,32,2048]{2,1,0:T(8,128)(2,1)}) custom-call(bf16[32,64,256]{2,1,0:T(8,128)(2,1)S(1)} %maximum_select_fusion.1.refs_1_.refs_0_, bf16[32,64,256]{2,1,0:T(8,128)(2,1)S(1)} %collective-permute-done.14.refs_0_.refs_1_, ...), custom_call_target="tpu_custom_call", output_to_operand_aliasing={{0}: (7, {}), {1}: (8, {})} | custom-call | flops 8589934592 | bytes 12582912 | tf_op jit(solution)/shard_map/convolve/pallas_call | solution.py:266
  149.7 5.4 %collective-permute-start.22 = (bf16[64,32,2048]{2,1,0:T(8,128)(2,1)}, bf16[64,32,2048]{2,1,0:T(8,128)(2,1)}, u32[]{:S(2)}, u32[]{:S(2)}) collective-permute-start(bf16[64,32,2048]{2,1,0:T(8,128)(2,1)} %get-tuple-element.12), channel_id=1, source_target_pairs={{0,4},{4,0},{8,12},{12,8},{16,20},{20,16},{24,28},{28,24},{1,5},{5... | collective-permute-start | bytes 25165832 | tf_op jit(solution)/shard_map/ppermute | solution.py:360
  155.1 21.5 %fit.2.refs_0_ = bf16[32,128,1024]{2,1,0:T(8,128)(2,1)} custom-call(s32[1]{0:T(128)} %bitcast.23.at_ref, bf16[64,32,2048]{2,1,0:T(8,128)(2,1)} %get-tuple-element.13.w_ref, bf16[2048,1024]{1,0:T(8,128)(2,1)} %copy-done.2), custom_call_target="tpu_custom_call" | custom-call | flops 12884901888 | bytes 16777216 | tf_op jit(solution)/shard_map/fit/pallas_call | solution.py:314
  176.6 21.5 %fit.3 = bf16[32,128,1024]{2,1,0:T(8,128)(2,1)} custom-call(s32[1]{0:T(128)} %bitcast.at_ref, bf16[64,32,2048]{2,1,0:T(8,128)(2,1)} %collective-permute-done.22.w_ref, bf16[2048,1024]{1,0:T(8,128)(2,1)} %copy-done.2, bf16[32,128,1024]{2,1,0:T(8,128)(2,1)} %fit.2.refs_0_), custom_call_target="tpu_custom_call", output_to_operand_aliasing={{}: (3, {})} | custom-call | flops 12884901888 | bytes 16777216 | tf_op jit(solution)/shard_map/fit/pallas_call | solution.py:314
  (47 shorter events, 1.9 us)
Async XLA Ops:
  0.0 13.9 %copy-start = (f32[256,128]{1,0:T(8,128)S(1)}, f32[256,128]{1,0:T(8,128)}, u32[]{:S(2)}) copy-start(f32[256,128]{1,0:T(8,128)} %param.8) | copy-start | bytes 393220
  4.5 0.7 copy-start.4
  4.5 25.7 %collective-permute-start.7 = (bf16[4,64,8,256]{3,2,1,0:T(8,128)(2,1)}, bf16[4,64,8,256]{3,2,1,0:T(8,128)(2,1)}, u32[]{:S(2)}, u32[]{:S(2)}) collective-permute-start(bf16[4,64,8,256]{3,2,1,0:T(8,128)(2,1)} %get-tuple-element.24), channel_id=1, source_target_pairs={{0,4},{4,0},{8,12},{12,8},{16,20},{20,16},{24,28},{28,24},{1,5},{5... | collective-permute-start | bytes 3145736 | tf_op jit(solution)/shard_map/ppermute | solution.py:360
  5.2 8.6 %copy-start.3 = (f32[256,256]{1,0:T(8,128)S(1)}, f32[256,256]{1,0:T(8,128)}, u32[]{:S(2)}) copy-start(f32[256,256]{1,0:T(8,128)} %constant.132.clone) | copy-start | bytes 786436
  13.7 1.2 collective-permute-start
  14.9 9.7 %collective-permute-start.3 = (bf16[16,1024]{1,0:T(8,128)(2,1)S(1)}, bf16[16,1024]{1,0:T(8,128)(2,1)S(1)}, u32[]{:S(2)}, u32[]{:S(2)}) collective-permute-start(bf16[16,1024]{1,0:T(8,128)(2,1)S(1)} %pad_maximum_fusion.1), channel_id=1, source_target_pairs={{0,3},{1,0},{2,1},{3,2},{4,7},{5,4},{6,5},{7,6},{8,11},{9,8},{10,9... | collective-permute-start | bytes 98312 | tf_op jit(solution)/shard_map/ppermute | solution.py:372
  19.4 6.9 %collective-permute-start.2 = (bf16[16,1024]{1,0:T(8,128)(2,1)S(1)}, bf16[16,1024]{1,0:T(8,128)(2,1)S(1)}, u32[]{:S(2)}, u32[]{:S(2)}) collective-permute-start(bf16[16,1024]{1,0:T(8,128)(2,1)S(1)} %pad_maximum_fusion.1), channel_id=1, source_target_pairs={{0,2},{1,3},{2,0},{3,1},{4,6},{5,7},{6,4},{7,5},{8,10},{9,11},{10,... | collective-permute-start | bytes 98312 | tf_op jit(solution)/shard_map/ppermute | solution.py:372
  19.4 4.6 %collective-permute-start.1 = (bf16[16,1024]{1,0:T(8,128)(2,1)S(1)}, bf16[16,1024]{1,0:T(8,128)(2,1)S(1)}, u32[]{:S(2)}, u32[]{:S(2)}) collective-permute-start(bf16[16,1024]{1,0:T(8,128)(2,1)S(1)} %pad_maximum_fusion.1), channel_id=1, source_target_pairs={{0,1},{1,2},{2,3},{3,0},{4,5},{5,6},{6,7},{7,4},{8,9},{9,10},{10,1... | collective-permute-start | bytes 98312 | tf_op jit(solution)/shard_map/ppermute | solution.py:372
  27.6 9.6 %collective-permute-start.6 = (bf16[64,1024]{1,0:T(8,128)(2,1)}, bf16[64,1024]{1,0:T(8,128)(2,1)S(1)}, u32[]{:S(2)}, u32[]{:S(2)}) collective-permute-start(bf16[64,1024]{1,0:T(8,128)(2,1)} %get-tuple-element.27), channel_id=1, source_target_pairs={{0,24},{4,28},{8,16},{12,20},{16,8},{20,12},{24,0},{28,4},{1,25},{... | collective-permute-start | bytes 393224 | tf_op jit(solution)/shard_map/ppermute | solution.py:360
  29.7 7.4 %collective-permute-start.5 = (bf16[64,1024]{1,0:T(8,128)(2,1)}, bf16[64,1024]{1,0:T(8,128)(2,1)S(1)}, u32[]{:S(2)}, u32[]{:S(2)}) collective-permute-start(bf16[64,1024]{1,0:T(8,128)(2,1)} %get-tuple-element.27), channel_id=1, source_target_pairs={{0,16},{4,20},{8,24},{12,28},{16,0},{20,4},{24,8},{28,12},{1,17},{... | collective-permute-start | bytes 393224 | tf_op jit(solution)/shard_map/ppermute | solution.py:360
  30.0 5.0 %collective-permute-start.4 = (bf16[64,1024]{1,0:T(8,128)(2,1)}, bf16[64,1024]{1,0:T(8,128)(2,1)}, u32[]{:S(2)}, u32[]{:S(2)}) collective-permute-start(bf16[64,1024]{1,0:T(8,128)(2,1)} %get-tuple-element.27), channel_id=1, source_target_pairs={{0,8},{4,12},{8,0},{12,4},{16,24},{20,28},{24,16},{28,20},{1,9},{5... | collective-permute-start | bytes 393224 | tf_op jit(solution)/shard_map/ppermute | solution.py:360
  31.6 23.4 %collective-permute-start.8 = (bf16[32,16,256]{2,1,0:T(8,128)(2,1)S(1)}, bf16[32,16,256]{2,1,0:T(8,128)(2,1)S(1)}, u32[]{:S(2)}, u32[]{:S(2)}) collective-permute-start(bf16[32,16,256]{2,1,0:T(8,128)(2,1)S(1)} %get-tuple-element.17), channel_id=1, source_target_pairs={{0,1},{1,2},{2,3},{3,0},{4,5},{5,6},{6,7},{7,4},{8,9},{9,10},{10,1... | collective-permute-start | bytes 786440 | tf_op jit(solution)/shard_map/ppermute | solution.py:372
  31.7 23.4 %collective-permute-start.9 = (bf16[32,16,256]{2,1,0:T(8,128)(2,1)S(1)}, bf16[32,16,256]{2,1,0:T(8,128)(2,1)S(1)}, u32[]{:S(2)}, u32[]{:S(2)}) collective-permute-start(bf16[32,16,256]{2,1,0:T(8,128)(2,1)S(1)} %get-tuple-element.18), channel_id=1, source_target_pairs={{0,2},{1,3},{2,0},{3,1},{4,6},{5,7},{6,4},{7,5},{8,10},{9,11},{10,... | collective-permute-start | bytes 786440 | tf_op jit(solution)/shard_map/ppermute | solution.py:372
  34.9 20.1 %collective-permute-start.10 = (bf16[32,16,256]{2,1,0:T(8,128)(2,1)S(1)}, bf16[32,16,256]{2,1,0:T(8,128)(2,1)S(1)}, u32[]{:S(2)}, u32[]{:S(2)}) collective-permute-start(bf16[32,16,256]{2,1,0:T(8,128)(2,1)S(1)} %get-tuple-element.19), channel_id=1, source_target_pairs={{0,3},{1,0},{2,1},{3,2},{4,7},{5,4},{6,5},{7,6},{8,11},{9,8},{10,9... | collective-permute-start | bytes 786440 | tf_op jit(solution)/shard_map/ppermute | solution.py:372
  55.3 25.5 %collective-permute-start.17 = (bf16[32,64,256]{2,1,0:T(8,128)(2,1)S(1)}, bf16[32,64,256]{2,1,0:T(8,128)(2,1)S(1)}, u32[]{:S(2)}, u32[]{:S(2)}) collective-permute-start(bf16[32,64,256]{2,1,0:T(8,128)(2,1)S(1)} %maximum_select_fusion.refs_1_.refs_0_), channel_id=1, source_target_pairs={{0,16},{4,20},{8,24},{12,28},{16,0},{20,4},{24,8},{28,12},{1,17},{... | collective-permute-start | bytes 3145736 | tf_op jit(solution)/shard_map/ppermute | solution.py:360
  56.4 23.7 %collective-permute-start.11 = (bf16[32,16,256]{2,1,0:T(8,128)(2,1)S(1)}, bf16[32,16,256]{2,1,0:T(8,128)(2,1)S(1)}, u32[]{:S(2)}, u32[]{:S(2)}) collective-permute-start(bf16[32,16,256]{2,1,0:T(8,128)(2,1)S(1)} %get-tuple-element.20), channel_id=1, source_target_pairs={{0,1},{1,2},{2,3},{3,0},{4,5},{5,6},{6,7},{7,4},{8,9},{9,10},{10,1... | collective-permute-start | bytes 786440 | tf_op jit(solution)/shard_map/ppermute | solution.py:372
  58.7 21.4 %collective-permute-start.12 = (bf16[32,16,256]{2,1,0:T(8,128)(2,1)S(1)}, bf16[32,16,256]{2,1,0:T(8,128)(2,1)S(1)}, u32[]{:S(2)}, u32[]{:S(2)}) collective-permute-start(bf16[32,16,256]{2,1,0:T(8,128)(2,1)S(1)} %get-tuple-element.21), channel_id=1, source_target_pairs={{0,2},{1,3},{2,0},{3,1},{4,6},{5,7},{6,4},{7,5},{8,10},{9,11},{10,... | collective-permute-start | bytes 786440 | tf_op jit(solution)/shard_map/ppermute | solution.py:372
  58.7 21.4 %collective-permute-start.13 = (bf16[32,16,256]{2,1,0:T(8,128)(2,1)S(1)}, bf16[32,16,256]{2,1,0:T(8,128)(2,1)S(1)}, u32[]{:S(2)}, u32[]{:S(2)}) collective-permute-start(bf16[32,16,256]{2,1,0:T(8,128)(2,1)S(1)} %get-tuple-element.22), channel_id=1, source_target_pairs={{0,3},{1,0},{2,1},{3,2},{4,7},{5,4},{6,5},{7,6},{8,11},{9,8},{10,9... | collective-permute-start | bytes 786440 | tf_op jit(solution)/shard_map/ppermute | solution.py:372
  61.2 21.4 %collective-permute-start.16 = (bf16[32,64,256]{2,1,0:T(8,128)(2,1)S(1)}, bf16[32,64,256]{2,1,0:T(8,128)(2,1)S(1)}, u32[]{:S(2)}, u32[]{:S(2)}) collective-permute-start(bf16[32,64,256]{2,1,0:T(8,128)(2,1)S(1)} %maximum_select_fusion.refs_1_.refs_0_), channel_id=1, source_target_pairs={{0,8},{4,12},{8,0},{12,4},{16,24},{20,28},{24,16},{28,20},{1,9},{5... | collective-permute-start | bytes 3145736 | tf_op jit(solution)/shard_map/ppermute | solution.py:360
  80.3 21.3 %collective-permute-start.15 = (bf16[32,64,256]{2,1,0:T(8,128)(2,1)S(1)}, bf16[32,64,256]{2,1,0:T(8,128)(2,1)S(1)}, u32[]{:S(2)}, u32[]{:S(2)}) collective-permute-start(bf16[32,64,256]{2,1,0:T(8,128)(2,1)S(1)} %maximum_select_fusion.1.refs_1_.refs_0_), channel_id=1, source_target_pairs={{0,16},{4,20},{8,24},{12,28},{16,0},{20,4},{24,8},{28,12},{1,17},{... | collective-permute-start | bytes 3145736 | tf_op jit(solution)/shard_map/ppermute | solution.py:360
  80.6 25.2 %collective-permute-start.14 = (bf16[32,64,256]{2,1,0:T(8,128)(2,1)S(1)}, bf16[32,64,256]{2,1,0:T(8,128)(2,1)S(1)}, u32[]{:S(2)}, u32[]{:S(2)}) collective-permute-start(bf16[32,64,256]{2,1,0:T(8,128)(2,1)S(1)} %maximum_select_fusion.1.refs_1_.refs_0_), channel_id=1, source_target_pairs={{0,8},{4,12},{8,0},{12,4},{16,24},{20,28},{24,16},{28,20},{1,9},{5... | collective-permute-start | bytes 3145736 | tf_op jit(solution)/shard_map/ppermute | solution.py:360
  80.9 43.7 %collective-permute-start.20 = (bf16[32,32,256]{2,1,0:T(8,128)(2,1)S(1)}, bf16[32,32,256]{2,1,0:T(8,128)(2,1)S(1)}, u32[]{:S(2)}, u32[]{:S(2)}) collective-permute-start(bf16[32,32,256]{2,1,0:T(8,128)(2,1)S(1)} %slice_select_fusion.1), channel_id=1, source_target_pairs={{0,8},{4,12},{8,0},{12,4},{16,24},{20,28},{24,16},{28,20},{1,9},{5... | collective-permute-start | bytes 1572872 | tf_op jit(solution)/shard_map/ppermute | solution.py:360
  82.7 41.8 %collective-permute-start.21 = (bf16[32,32,256]{2,1,0:T(8,128)(2,1)S(1)}, bf16[32,32,256]{2,1,0:T(8,128)(2,1)S(1)}, u32[]{:S(2)}, u32[]{:S(2)}) collective-permute-start(bf16[32,32,256]{2,1,0:T(8,128)(2,1)S(1)} %slice_select_fusion), channel_id=1, source_target_pairs={{0,16},{4,20},{8,24},{12,28},{16,0},{20,4},{24,8},{28,12},{1,17},{... | collective-permute-start | bytes 1572872 | tf_op jit(solution)/shard_map/ppermute | solution.py:360
  101.6 35.4 %collective-permute-start.18 = (bf16[32,32,256]{2,1,0:T(8,128)(2,1)S(1)}, bf16[32,32,256]{2,1,0:T(8,128)(2,1)S(1)}, u32[]{:S(2)}, u32[]{:S(2)}) collective-permute-start(bf16[32,32,256]{2,1,0:T(8,128)(2,1)S(1)} %slice_select_fusion.3), channel_id=1, source_target_pairs={{0,8},{4,12},{8,0},{12,4},{16,24},{20,28},{24,16},{28,20},{1,9},{5... | collective-permute-start | bytes 1572872 | tf_op jit(solution)/shard_map/ppermute | solution.py:360
  105.9 31.1 %collective-permute-start.19 = (bf16[32,32,256]{2,1,0:T(8,128)(2,1)S(1)}, bf16[32,32,256]{2,1,0:T(8,128)(2,1)S(1)}, u32[]{:S(2)}, u32[]{:S(2)}) collective-permute-start(bf16[32,32,256]{2,1,0:T(8,128)(2,1)S(1)} %slice_select_fusion.2), channel_id=1, source_target_pairs={{0,16},{4,20},{8,24},{12,28},{16,0},{20,4},{24,8},{28,12},{1,17},{... | collective-permute-start | bytes 1572872 | tf_op jit(solution)/shard_map/ppermute | solution.py:360
  122.6 2.0 %copy-start.2 = (bf16[2048,1024]{1,0:T(8,128)(2,1)}, bf16[2048,1024]{1,0:T(8,128)(2,1)S(1)}, u32[]{:S(2)}) copy-start(bf16[2048,1024]{1,0:T(8,128)(2,1)S(1)} %sweep_last.1.refs_9_.inverse_ref) | copy-start | bytes 12582916
  149.7 26.9 %collective-permute-start.22 = (bf16[64,32,2048]{2,1,0:T(8,128)(2,1)}, bf16[64,32,2048]{2,1,0:T(8,128)(2,1)}, u32[]{:S(2)}, u32[]{:S(2)}) collective-permute-start(bf16[64,32,2048]{2,1,0:T(8,128)(2,1)} %get-tuple-element.12), channel_id=1, source_target_pairs={{0,4},{4,0},{8,12},{12,8},{16,20},{20,16},{24,28},{28,24},{1,5},{5... | collective-permute-start | bytes 25165832 | tf_op jit(solution)/shard_map/ppermute | solution.py:360
  176.6 21.5 %copy-start.1 = (f32[256,128]{1,0:T(8,128)S(1)}, f32[256,128]{1,0:T(8,128)}, u32[]{:S(2)}) copy-start(f32[256,128]{1,0:T(8,128)} %param.8) | copy-start | bytes 393220
